TPU v7x, 32 devices: a whole 2x2x4 slice. The times are simulated.
32 devices in a mesh: ctx: 8 (over z, x), tp: 4 (over y, core).
Axes of the slice: x: 2, y: 2, z: 4, core: 2. Of those that a mesh axis runs over, the one named last changes fastest.
Arguments:
- queries: bfloat16 [2048, 2048], P('ctx', 'tp'), may hold values from -6 to 6
- keys: bfloat16 [2048, 512], P('ctx', 'tp'), may hold values from -6 to 6
- values: bfloat16 [2048, 512], P('ctx', 'tp'), may hold values from -6 to 6
- outputs: bfloat16 [2048, 2048], P('ctx', 'tp'), may hold values from -6 to 6
- out_grad: bfloat16 [2048, 2048], P('ctx', 'tp'), may hold values from -6 to 6
- log_norm: float32 [2048, 16], P('ctx', 'tp'), as said below
- block_mask: int32 [8, 4], P('ctx'), may hold values from 0 to 1, as said below
- counter_base: int32 [2], replicated, may hold values from 0 to 1048575
- q_weight: bfloat16 [4096, 2048], P(None, 'tp'), may hold values from -0.125 to 0.125
- k_weight: bfloat16 [4096, 512], P(None, 'tp'), may hold values from -0.09375 to 0.09375
- v_weight: bfloat16 [4096, 512], P(None, 'tp'), may hold values from -0.09375 to 0.09375
Outputs:
- input_grad: bfloat16 [2048, 4096], P('ctx', 'tp')
Inputs may be any that keep to these rules, and one draw needn't show every extreme that they name: block_mask[i, r] is 1 where query block i attends to key block i - r; column 0 and the row of the last block are all 1. log_norm lies between log(512) - 0.5 and log(512) + 2.5.
All inputs are finite; a program needn't handle non-finite values.
Results may differ from a plain program's by a relative error of at most 0.015.
Values may be sent and summed in bfloat16 or wider, within the bound.
No kernel may reach another device: no remote copies, remote signals or barrier semaphores. Data moves between devices by JAX's collectives and lax.ppermute only.
A program may use at most 64 MiB of HBM per device.

v0:
```python
import jax
import jax.numpy as jnp
from jax import lax
from jax.sharding import PartitionSpec as P

keep_level = 103
keep_scale = 1024.0 / 921.0


def shifted(array, axis, by):
    devices = lax.axis_size(axis)
    pairs = [(i, i + by) for i in range(devices) if 0 <= i + by < devices]
    return lax.ppermute(array, axis, pairs)


def passed_along(value, axis, steps):
    count = lax.axis_size(axis)
    pairs = [(source, (source + steps) % count) for source in range(count)]
    return lax.ppermute(value, axis, pairs)


def keep_mask(head_ids, query_pos, key_pos, seed_value):
    mixed = (
        head_ids[:, None, None] * 83492791
        + query_pos[None, :, None] * 73856093
        + key_pos[None, None, :] * 19349663
        + seed_value
    )
    mixed = mixed ^ lax.shift_right_logical(mixed, jnp.int32(15))
    mixed = mixed * 739982445
    mixed = mixed ^ lax.shift_right_logical(mixed, jnp.int32(12))
    mixed = mixed * 695872825
    mixed = mixed ^ lax.shift_right_logical(mixed, jnp.int32(15))
    return mixed & 1023 >= keep_level


def pair_grads(
    query_blk,
    grad_out,
    norm_blk,
    row_delta,
    key_blk,
    value_blk,
    query_start,
    key_start,
    active,
    head_ids,
    counter_base,
    window,
):
    rows_count = query_blk.shape[0]
    scaling = query_blk.shape[2] ** (-0.5)
    scores = (
        jnp.einsum("qhd,kd->hqk", query_blk, key_blk, preferred_element_type=jnp.float32) * scaling
    )
    query_pos = query_start + jnp.arange(rows_count, dtype=jnp.int32)
    key_pos = key_start + jnp.arange(rows_count, dtype=jnp.int32)
    spacing = query_pos[:, None] - key_pos[None, :]
    allowed = (spacing >= 0) & (spacing < window) & active
    probs = jnp.where(
        allowed[None], jnp.exp(scores - jnp.transpose(norm_blk)[:, :, None]), jnp.float32(0.0)
    )
    kept = keep_mask(
        head_ids, query_pos + counter_base[1], key_pos + counter_base[1], counter_base[0]
    )
    dropped = jnp.where(kept, probs * keep_scale, jnp.float32(0.0)).astype(jnp.bfloat16)
    grad_value = jnp.einsum("hqk,qhd->kd", dropped, grad_out, preferred_element_type=jnp.float32)
    grad_probs = jnp.einsum("qhd,kd->hqk", grad_out, value_blk, preferred_element_type=jnp.float32)
    grad_scores = (
        probs
        * (
            jnp.where(kept, grad_probs * keep_scale, jnp.float32(0.0))
            - jnp.transpose(row_delta)[:, :, None]
        )
    ).astype(jnp.bfloat16)
    grad_query = (
        jnp.einsum("hqk,kd->qhd", grad_scores, key_blk, preferred_element_type=jnp.float32)
        * scaling
    )
    grad_key = (
        jnp.einsum("hqk,qhd->kd", grad_scores, query_blk, preferred_element_type=jnp.float32)
        * scaling
    )
    return (grad_query, grad_key, grad_value)


def on_device(
    queries,
    keys,
    values,
    outputs,
    out_grad,
    log_norm,
    block_mask,
    counter_base,
    q_weight,
    k_weight,
    v_weight,
):
    rows_count = queries.shape[0]
    head_count = log_norm.shape[1]
    head_dim = keys.shape[1]
    window = 3 * rows_count + rows_count // 2
    block_id = lax.axis_index("ctx")
    group_id = lax.axis_index("tp")
    head_ids = group_id * head_count + jnp.arange(head_count, dtype=jnp.int32)
    query_blk = queries.reshape(rows_count, head_count, head_dim)
    grad_out = out_grad.reshape(rows_count, head_count, head_dim)
    row_delta = jnp.sum(
        grad_out.astype(jnp.float32)
        * outputs.reshape(rows_count, head_count, head_dim).astype(jnp.float32),
        axis=2,
    )
    mask_row = block_mask[0]
    key_blk = keys
    value_blk = values
    grad_query = jnp.zeros((rows_count, head_count, head_dim), jnp.float32)
    empty_grad = jnp.zeros((rows_count, head_dim), jnp.float32)
    carried = (empty_grad, empty_grad)
    for offset in range(block_mask.shape[1]):
        if offset > 0:
            key_blk, value_blk = shifted((key_blk, value_blk), "ctx", 1)
        source = block_id - offset
        active = (source >= 0) & (mask_row[offset] == 1)
        add_query, add_key, add_value = pair_grads(
            query_blk,
            grad_out,
            log_norm,
            row_delta,
            key_blk,
            value_blk,
            block_id * rows_count,
            source * rows_count,
            active,
            head_ids,
            counter_base,
            window,
        )
        grad_query = grad_query + add_query
        if offset > 0:
            carried = (
                passed_along(carried[0].astype(jnp.bfloat16), "ctx", 1).astype(jnp.float32),
                passed_along(carried[1].astype(jnp.bfloat16), "ctx", 1).astype(jnp.float32),
            )
        carried = (carried[0] + add_key, carried[1] + add_value)
    steps_back = 1 - block_mask.shape[1]
    grad_key, grad_value = (
        passed_along(carried[0].astype(jnp.bfloat16), "ctx", steps_back).astype(jnp.float32),
        passed_along(carried[1].astype(jnp.bfloat16), "ctx", steps_back).astype(jnp.float32),
    )
    contract = (((1,), (1,)), ((), ()))
    query_round = grad_query.reshape(rows_count, head_count * head_dim).astype(jnp.bfloat16)
    partial_term = lax.dot_general(
        query_round, q_weight, contract, preferred_element_type=jnp.float32
    )
    partial_term = partial_term + lax.dot_general(
        grad_key.astype(jnp.bfloat16), k_weight, contract, preferred_element_type=jnp.float32
    )
    partial_term = partial_term + lax.dot_general(
        grad_value.astype(jnp.bfloat16), v_weight, contract, preferred_element_type=jnp.float32
    )
    return lax.psum_scatter(
        partial_term.astype(jnp.bfloat16), "tp", scatter_dimension=1, tiled=True
    )


def solution(mesh):
    return jax.shard_map(
        on_device,
        mesh=mesh,
        in_specs=(
            P("ctx", "tp"),
            P("ctx", "tp"),
            P("ctx", "tp"),
            P("ctx", "tp"),
            P("ctx", "tp"),
            P("ctx", "tp"),
            P("ctx", None),
            P(),
            P(None, "tp"),
            P(None, "tp"),
            P(None, "tp"),
        ),
        out_specs=P("ctx", "tp"),
        check_vma=False,
    )
```

profile of v0, /device:TPU:0, one launch (start us, length us, event | category | flops | bytes accessed | tf_op | source)
XLA Modules:
  0.0 119.0 jit_solution(18008330085167050707)
XLA Ops:
  6.5 5.0 %collective-permute-start.1 = (bf16[256,128]{1,0:T(8,128)(2,1)}, bf16[256,128]{1,0:T(8,128)(2,1)S(1)}, u32[]{:S(2)}, u32[]{:S(2)}) collective-permute-start(bf16[256,128]{1,0:T(8,128)(2,1)} %param.13), channel_id=1, source_target_pairs={{0,4},{4,8},{8,12},{12,16},{16,20},{20,24},{24,28},{1,5},{5,9},{9,... | collective-permute-start | bytes 196616 | tf_op jit(solution)/shard_map/ppermute | solution.py:13
  11.5 3.5 %collective-permute-start = (bf16[256,128]{1,0:T(8,128)(2,1)}, bf16[256,128]{1,0:T(8,128)(2,1)S(1)}, u32[]{:S(2)}, u32[]{:S(2)}) collective-permute-start(bf16[256,128]{1,0:T(8,128)(2,1)} %param.12), channel_id=1, source_target_pairs={{0,4},{4,8},{8,12},{12,16},{16,20},{20,24},{24,28},{1,5},{5,9},{9,... | collective-permute-start | bytes 196616 | tf_op jit(solution)/shard_map/ppermute | solution.py:13
  15.0 1.3 %fusion.163 = (s32[1]{0:T(128)}, s32[1]{0:T(128)}) fusion(s32[2]{0:T(128)} %param.18), kind=kLoop, calls=%fused_computation.218 | loop fusion | bytes 16 | tf_op jit(solution)/shard_map/slice | solution.py:64
  17.7 1.5 %fusion.162 = (s32[1,1]{1,0:T(1,128)}, s32[1,1]{1,0:T(1,128)}, s32[1,1]{1,0:T(1,128)}, s32[1,1]{1,0:T(1,128)}) fusion(s32[1,4]{1,0:T(1,128)} %param.17), kind=kLoop, calls=%fused_computation.217 | loop fusion | bytes 32 | tf_op jit(solution)/shard_map/slice | solution.py:124
  21.8 1.0 reshape.247
  22.9 1.2 reshape.248
  24.9 1.3 %fusion.32 = f32[4,256,256]{1,2,0:T(8,128)S(1)} fusion(f32[4,256]{1,0:T(4,128)} %bitcast.255, pred[256,256]{0,1:T(8,128)(4,1)S(1)} %get-tuple-element.7, bf16[256,128]{1,0:T(8,128)(2,1)} %param.12, bf16[256,512]{1,0:T(8,128)(2,1)} %param.11), kind=kOutput, calls=%fused_computation.54 | convolution fusion | flops 67895296 | bytes 1445888 | tf_op jit(solution)/shard_map/qhd,kd->hqk/dot_general | solution.py:54
  26.3 1.3 %fusion.33 = bf16[4,256,256]{1,2,0:T(8,128)(2,1)S(1)} fusion(f32[4,256,256]{1,2,0:T(8,128)S(1)} %fusion.32, f32[4,256]{1,0:T(4,128)S(1)} %copy.30, s32[]{:T(128)} %bitcast.5, s32[256]{0:T(256)S(1)} %get-tuple-element.16, s32[4,256]{1,0:T(4,128)S(1)} %broadcast_add_fusion, bf16[256,128]{1,0:T(8,128)(2,1)S(1)} %copy-done.6, bf16[256,512]{1,0:T(8,128)(2,1)S(1)} %copy-done.4), kind=kOutput, calls=%fused_computation.55 | convolution fusion | flops 71565312 | bytes 1909764 | tf_op jit(solution)/shard_map/qhd,kd->hqk/dot_general | solution.py:68
  27.9 1.5 %collective-permute-start.6 = (bf16[256,128]{1,0:T(8,128)(2,1)S(1)}, bf16[256,128]{1,0:T(8,128)(2,1)S(1)}, u32[]{:S(2)}, u32[]{:S(2)}) collective-permute-start(bf16[256,128]{1,0:T(8,128)(2,1)S(1)} %fusion.43), channel_id=1, source_target_pairs={{0,4},{4,8},{8,12},{12,16},{16,20},{20,24},{24,28},{28,0},{1,5},{5... | collective-permute-start | bytes 196616 | tf_op jit(solution)/shard_map/ppermute | solution.py:19
  29.5 1.3 %fusion.44 = bf16[256,128]{1,0:T(8,128)(2,1)S(1)} fusion(f32[4,256,256]{1,2,0:T(8,128)S(1)} %fusion.32, s32[]{:T(128)} %bitcast.5, s32[256]{0:T(256)S(1)} %get-tuple-element.16, s32[4,256]{1,0:T(4,128)S(1)} %broadcast_add_fusion, bf16[256,512]{1,0:T(8,128)(2,1)S(1)} %copy-done.4), kind=kOutput, calls=%fused_computation.77 | convolution fusion | flops 71073792 | bytes 1381380 | tf_op jit(solution)/shard_map/hqk,qhd->kd/dot_general | solution.py:67
  30.7 1.6 %collective-permute-start.10 = (bf16[256,128]{1,0:T(8,128)(2,1)S(1)}, bf16[256,128]{1,0:T(8,128)(2,1)S(1)}, u32[]{:S(2)}, u32[]{:S(2)}) collective-permute-start(bf16[256,128]{1,0:T(8,128)(2,1)S(1)} %fusion.44), channel_id=1, source_target_pairs={{0,4},{4,8},{8,12},{12,16},{16,20},{20,24},{24,28},{28,0},{1,5},{5... | collective-permute-start | bytes 196616 | tf_op jit(solution)/shard_map/ppermute | solution.py:19
  35.0 1.3 %fusion.34 = bf16[4,256,256]{1,2,0:T(8,128)(2,1)S(1)} fusion(f32[4,256,256]{1,2,0:T(8,128)S(1)} %fusion.24, f32[4,256]{1,0:T(4,128)S(1)} %copy.30, s32[]{:T(128)} %bitcast.5, s32[256]{0:T(256)S(1)} %add_multiply_fusion.2, s32[4,256]{1,0:T(4,128)S(1)} %broadcast_add_fusion, bf16[256,128]{1,0:T(8,128)(2,1)S(1)} %collective-permute-done.1, ...), kind=kOutput, calls=%fused_computation.56 | convolution fusion | flops 71565312 | bytes 1909764 | tf_op jit(solution)/shard_map/qhd,kd->hqk/dot_general | solution.py:68
  36.6 1.5 %collective-permute-start.7 = (bf16[256,128]{1,0:T(8,128)(2,1)S(1)}, bf16[256,128]{1,0:T(8,128)(2,1)S(1)}, u32[]{:S(2)}, u32[]{:S(2)}) collective-permute-start(bf16[256,128]{1,0:T(8,128)(2,1)S(1)} %add_convert_fusion.5), channel_id=1, source_target_pairs={{0,4},{4,8},{8,12},{12,16},{16,20},{20,24},{24,28},{28,0},{1,5},{5... | collective-permute-start | bytes 196616 | tf_op jit(solution)/shard_map/ppermute | solution.py:19
  38.2 1.3 %add_convert_fusion.2 = bf16[256,128]{1,0:T(8,128)(2,1)S(1)} fusion(bf16[256,128]{1,0:T(8,128)(2,1)S(1)} %collective-permute-done.10, f32[4,256,256]{1,2,0:T(8,128)S(1)} %fusion.24, s32[]{:T(128)} %bitcast.5, s32[256]{0:T(256)S(1)} %add_multiply_fusion.2, s32[4,256]{1,0:T(4,128)S(1)} %broadcast_add_fusion, bf16[256,512]{1,0:T(8,128)(2,1)S(1)} %copy-done.4), kind=kOutput, calls=%fused_computation.141 | convolution fusion | flops 71139328 | bytes 1446916 | tf_op jit(solution)/shard_map/hqk,qhd->kd/dot_general | solution.py:67
  39.4 1.6 %collective-permute-start.11 = (bf16[256,128]{1,0:T(8,128)(2,1)S(1)}, bf16[256,128]{1,0:T(8,128)(2,1)S(1)}, u32[]{:S(2)}, u32[]{:S(2)}) collective-permute-start(bf16[256,128]{1,0:T(8,128)(2,1)S(1)} %add_convert_fusion.2), channel_id=1, source_target_pairs={{0,4},{4,8},{8,12},{12,16},{16,20},{20,24},{24,28},{28,0},{1,5},{5... | collective-permute-start | bytes 196616 | tf_op jit(solution)/shard_map/ppermute | solution.py:19
  41.0 3.4 %collective-permute-start.3 = (bf16[256,128]{1,0:T(8,128)(2,1)S(1)}, bf16[256,128]{1,0:T(8,128)(2,1)S(1)}, u32[]{:S(2)}, u32[]{:S(2)}) collective-permute-start(bf16[256,128]{1,0:T(8,128)(2,1)S(1)} %collective-permute-done.1), channel_id=1, source_target_pairs={{0,4},{4,8},{8,12},{12,16},{16,20},{20,24},{24,28},{1,5},{5,9},{9,... | collective-permute-start | bytes 196616 | tf_op jit(solution)/shard_map/ppermute | solution.py:13
  44.4 1.9 %collective-permute-start.2 = (bf16[256,128]{1,0:T(8,128)(2,1)S(1)}, bf16[256,128]{1,0:T(8,128)(2,1)S(1)}, u32[]{:S(2)}, u32[]{:S(2)}) collective-permute-start(bf16[256,128]{1,0:T(8,128)(2,1)S(1)} %collective-permute-done), channel_id=1, source_target_pairs={{0,4},{4,8},{8,12},{12,16},{16,20},{20,24},{24,28},{1,5},{5,9},{9,... | collective-permute-start | bytes 196616 | tf_op jit(solution)/shard_map/ppermute | solution.py:13
  46.7 1.6 %collective-permute-done.2 = bf16[256,128]{1,0:T(8,128)(2,1)S(1)} collective-permute-done((bf16[256,128]{1,0:T(8,128)(2,1)S(1)}, bf16[256,128]{1,0:T(8,128)(2,1)S(1)}, u32[]{:S(2)}, u32[]{:S(2)}) %collective-permute-start.2) | collective-permute-done | bytes 65568 | tf_op jit(solution)/shard_map/ppermute | solution.py:13
  48.7 1.3 %convolution_bitcast_fusion.1 = f32[256,128]{1,0:T(8,128)S(1)} fusion(f32[4,256,256]{1,2,0:T(8,128)S(1)} %fusion.16, s32[256]{0:T(256)S(1)} %add_multiply_fusion.1, s32[]{:T(128)} %bitcast.5, s32[4,256]{1,0:T(4,128)S(1)} %broadcast_add_fusion, bf16[256,512]{1,0:T(8,128)(2,1)S(1)} %copy-done.4), kind=kOutput, calls=%fused_computation.65 | convolution fusion | flops 71041024 | bytes 1446916 | tf_op jit(solution)/shard_map/hqk,qhd->kd/dot_general | solution.py:67
  49.9 1.3 %fusion.35 = bf16[4,256,256]{1,2,0:T(8,128)(2,1)S(1)} fusion(f32[4,256,256]{1,2,0:T(8,128)S(1)} %fusion.16, f32[4,256]{1,0:T(4,128)S(1)} %copy.30, s32[]{:T(128)} %bitcast.5, s32[256]{0:T(256)S(1)} %add_multiply_fusion.1, s32[4,256]{1,0:T(4,128)S(1)} %broadcast_add_fusion, bf16[256,128]{1,0:T(8,128)(2,1)S(1)} %collective-permute-done.3, ...), kind=kOutput, calls=%fused_computation.57 | convolution fusion | flops 71565312 | bytes 1909764 | tf_op jit(solution)/shard_map/qhd,kd->hqk/dot_general | solution.py:68
  51.6 2.4 %collective-permute-start.8 = (bf16[256,128]{1,0:T(8,128)(2,1)S(1)}, bf16[256,128]{1,0:T(8,128)(2,1)S(1)}, u32[]{:S(2)}, u32[]{:S(2)}) collective-permute-start(bf16[256,128]{1,0:T(8,128)(2,1)S(1)} %add_convert_fusion.4), channel_id=1, source_target_pairs={{0,4},{4,8},{8,12},{12,16},{16,20},{20,24},{24,28},{28,0},{1,5},{5... | collective-permute-start | bytes 196616 | tf_op jit(solution)/shard_map/ppermute | solution.py:19
  54.0 1.7 %collective-permute-start.12 = (bf16[256,128]{1,0:T(8,128)(2,1)S(1)}, bf16[256,128]{1,0:T(8,128)(2,1)S(1)}, u32[]{:S(2)}, u32[]{:S(2)}) collective-permute-start(bf16[256,128]{1,0:T(8,128)(2,1)S(1)} %add_convert_fusion.1), channel_id=1, source_target_pairs={{0,4},{4,8},{8,12},{12,16},{16,20},{20,24},{24,28},{28,0},{1,5},{5... | collective-permute-start | bytes 196616 | tf_op jit(solution)/shard_map/ppermute | solution.py:19
  55.8 3.4 %collective-permute-start.5 = (bf16[256,128]{1,0:T(8,128)(2,1)S(1)}, bf16[256,128]{1,0:T(8,128)(2,1)S(1)}, u32[]{:S(2)}, u32[]{:S(2)}) collective-permute-start(bf16[256,128]{1,0:T(8,128)(2,1)S(1)} %collective-permute-done.3), channel_id=1, source_target_pairs={{0,4},{4,8},{8,12},{12,16},{16,20},{20,24},{24,28},{1,5},{5,9},{9,... | collective-permute-start | bytes 196616 | tf_op jit(solution)/shard_map/ppermute | solution.py:13
  59.2 4.3 %collective-permute-start.4 = (bf16[256,128]{1,0:T(8,128)(2,1)S(1)}, bf16[256,128]{1,0:T(8,128)(2,1)S(1)}, u32[]{:S(2)}, u32[]{:S(2)}) collective-permute-start(bf16[256,128]{1,0:T(8,128)(2,1)S(1)} %collective-permute-done.2), channel_id=1, source_target_pairs={{0,4},{4,8},{8,12},{12,16},{16,20},{20,24},{24,28},{1,5},{5,9},{9,... | collective-permute-start | bytes 196616 | tf_op jit(solution)/shard_map/ppermute | solution.py:13
  63.7 1.6 %collective-permute-done.4 = bf16[256,128]{1,0:T(8,128)(2,1)S(1)} collective-permute-done((bf16[256,128]{1,0:T(8,128)(2,1)S(1)}, bf16[256,128]{1,0:T(8,128)(2,1)S(1)}, u32[]{:S(2)}, u32[]{:S(2)}) %collective-permute-start.4) | collective-permute-done | bytes 65568 | tf_op jit(solution)/shard_map/ppermute | solution.py:13
  65.7 1.3 %convolution_bitcast_fusion = f32[256,128]{1,0:T(8,128)S(1)} fusion(f32[4,256,256]{1,2,0:T(8,128)S(1)} %fusion.8, s32[256]{0:T(256)S(1)} %add_multiply_fusion, s32[]{:T(128)} %bitcast.5, s32[4,256]{1,0:T(4,128)S(1)} %broadcast_add_fusion, bf16[256,512]{1,0:T(8,128)(2,1)S(1)} %copy-done.4), kind=kOutput, calls=%fused_computation.64 | convolution fusion | flops 71041024 | bytes 1446916 | tf_op jit(solution)/shard_map/hqk,qhd->kd/dot_general | solution.py:67
  67.0 1.5 %fusion.36 = bf16[4,256,256]{1,2,0:T(8,128)(2,1)S(1)} fusion(f32[4,256,256]{1,2,0:T(8,128)S(1)} %fusion.8, f32[4,256]{1,0:T(4,128)S(1)} %copy.30, s32[]{:T(128)} %bitcast.5, s32[256]{0:T(256)S(1)} %add_multiply_fusion, s32[4,256]{1,0:T(4,128)S(1)} %broadcast_add_fusion, bf16[256,128]{1,0:T(8,128)(2,1)S(1)} %collective-permute-done.5, ...), kind=kOutput, calls=%fused_computation.58 | convolution fusion | flops 71565312 | bytes 1909764 | tf_op jit(solution)/shard_map/qhd,kd->hqk/dot_general | solution.py:68
  68.8 1.4 %collective-permute-start.9 = (bf16[256,128]{1,0:T(8,128)(2,1)S(1)}, bf16[256,128]{1,0:T(8,128)(2,1)S(1)}, u32[]{:S(2)}, u32[]{:S(2)}) collective-permute-start(bf16[256,128]{1,0:T(8,128)(2,1)S(1)} %add_convert_fusion.3), channel_id=1, source_target_pairs={{0,20},{4,24},{8,28},{12,0},{16,4},{20,8},{24,12},{28,16},{1,21},{... | collective-permute-start | bytes 196616 | tf_op jit(solution)/shard_map/ppermute | solution.py:19
  70.3 3.7 %collective-permute-start.13 = (bf16[256,128]{1,0:T(8,128)(2,1)S(1)}, bf16[256,128]{1,0:T(8,128)(2,1)S(1)}, u32[]{:S(2)}, u32[]{:S(2)}) collective-permute-start(bf16[256,128]{1,0:T(8,128)(2,1)S(1)} %add_convert_fusion), channel_id=1, source_target_pairs={{0,20},{4,24},{8,28},{12,0},{16,4},{20,8},{24,12},{28,16},{1,21},{... | collective-permute-start | bytes 196616 | tf_op jit(solution)/shard_map/ppermute | solution.py:19
  74.2 1.3 %fusion.164 = f32[256,4096]{1,0:T(8,128)S(1)} fusion(bf16[256,512]{0,1:T(8,128)(2,1)S(1)} %bitcast.253, bf16[4096,512]{1,0:T(8,128)(2,1)S(1)} %copy-done.1), kind=kOutput, calls=%fused_computation.219 | convolution fusion | flops 1073741824 | bytes 8650752 | tf_op jit(solution)/shard_map/dot_general | solution.py:153
  76.8 2.0 %fusion = bf16[256,4096]{1,0:T(8,128)(2,1)} fusion(f32[256,4096]{1,0:T(8,128)S(1)} %convolution_add_fusion.1, bf16[256,128]{1,0:T(8,128)(2,1)S(1)} %collective-permute-done.13, bf16[4096,128]{1,0:T(8,128)(2,1)S(1)} %copy-done.2), kind=kOutput, calls=%fused_computation.2 | convolution fusion | flops 270532608 | bytes 7405568 | tf_op jit(solution)/shard_map/dot_general | solution.py:159
  78.8 33.3 %reduce-scatter.2.cloned.1.call-done = bf16[256,1024]{1,0:T(8,128)(2,1)} async-done(((bf16[256,4096]{1,0:T(8,128)(2,1)}), bf16[256,1024]{1,0:T(8,128)(2,1)}) %reduce-scatter.2.cloned.1.call-update) | async-done | bytes 524304 | tf_op jit(solution)/shard_map/reduce_scatter | solution.py:162
  (58 shorter events, 8.8 us)
Async XLA Ops:
  6.5 69.0 %copy-start = (bf16[4096,128]{1,0:T(8,128)(2,1)S(1)}, bf16[4096,128]{1,0:T(8,128)(2,1)}, u32[]{:S(2)}) copy-start(bf16[4096,128]{1,0:T(8,128)(2,1)} %param.20) | copy-start | bytes 3145732
  6.5 19.7 %copy-start.6 = (bf16[256,128]{1,0:T(8,128)(2,1)S(1)}, bf16[256,128]{1,0:T(8,128)(2,1)}, u32[]{:S(2)}) copy-start(bf16[256,128]{1,0:T(8,128)(2,1)} %param.13) | copy-start | bytes 196612
  6.5 19.7 %copy-start.4 = (bf16[256,512]{1,0:T(8,128)(2,1)S(1)}, bf16[256,512]{1,0:T(8,128)(2,1)}, u32[]{:S(2)}) copy-start(bf16[256,512]{1,0:T(8,128)(2,1)} %param.15) | copy-start | bytes 786436
  6.5 105.6 %reduce-scatter.2.cloned.1.call-start = ((), (), s32[]{:S(2)}) async-start(), calls=%async_computation.1 | async-start | bytes 2621440 | tf_op jit(solution)/shard_map/reduce_scatter | solution.py:162
  6.5 28.5 %collective-permute-start.1 = (bf16[256,128]{1,0:T(8,128)(2,1)}, bf16[256,128]{1,0:T(8,128)(2,1)S(1)}, u32[]{:S(2)}, u32[]{:S(2)}) collective-permute-start(bf16[256,128]{1,0:T(8,128)(2,1)} %param.13), channel_id=1, source_target_pairs={{0,4},{4,8},{8,12},{12,16},{16,20},{20,24},{24,28},{1,5},{5,9},{9,... | collective-permute-start | bytes 196616 | tf_op jit(solution)/shard_map/ppermute | solution.py:13
  11.5 23.1 %collective-permute-start = (bf16[256,128]{1,0:T(8,128)(2,1)}, bf16[256,128]{1,0:T(8,128)(2,1)S(1)}, u32[]{:S(2)}, u32[]{:S(2)}) collective-permute-start(bf16[256,128]{1,0:T(8,128)(2,1)} %param.12), channel_id=1, source_target_pairs={{0,4},{4,8},{8,12},{12,16},{16,20},{20,24},{24,28},{1,5},{5,9},{9,... | collective-permute-start | bytes 196616 | tf_op jit(solution)/shard_map/ppermute | solution.py:13
  22.9 4.8 %copy-start.3 = (bf16[256,512]{1,0:T(8,128)(2,1)S(1)}, bf16[256,512]{1,0:T(8,128)(2,1)}, u32[]{:S(2)}) copy-start(bf16[256,512]{1,0:T(8,128)(2,1)} %param.11) | copy-start | bytes 786436
  26.3 7.4 %copy-start.5 = (bf16[256,128]{1,0:T(8,128)(2,1)S(1)}, bf16[256,128]{1,0:T(8,128)(2,1)}, u32[]{:S(2)}) copy-start(bf16[256,128]{1,0:T(8,128)(2,1)} %param.12) | copy-start | bytes 196612
  27.6 7.0 %copy-start.7 = (f32[256,4]{0,1:T(4,128)S(1)}, f32[256,4]{0,1:T(4,128)}, u32[]{:S(2)}) copy-start(f32[256,4]{0,1:T(4,128)} %param.16) | copy-start | bytes 12292
  27.9 8.4 %collective-permute-start.6 = (bf16[256,128]{1,0:T(8,128)(2,1)S(1)}, bf16[256,128]{1,0:T(8,128)(2,1)S(1)}, u32[]{:S(2)}, u32[]{:S(2)}) collective-permute-start(bf16[256,128]{1,0:T(8,128)(2,1)S(1)} %fusion.43), channel_id=1, source_target_pairs={{0,4},{4,8},{8,12},{12,16},{16,20},{20,24},{24,28},{28,0},{1,5},{5... | collective-permute-start | bytes 196616 | tf_op jit(solution)/shard_map/ppermute | solution.py:19
  30.7 7.4 %collective-permute-start.10 = (bf16[256,128]{1,0:T(8,128)(2,1)S(1)}, bf16[256,128]{1,0:T(8,128)(2,1)S(1)}, u32[]{:S(2)}, u32[]{:S(2)}) collective-permute-start(bf16[256,128]{1,0:T(8,128)(2,1)S(1)} %fusion.44), channel_id=1, source_target_pairs={{0,4},{4,8},{8,12},{12,16},{16,20},{20,24},{24,28},{28,0},{1,5},{5... | collective-permute-start | bytes 196616 | tf_op jit(solution)/shard_map/ppermute | solution.py:19
  36.6 14.9 %collective-permute-start.7 = (bf16[256,128]{1,0:T(8,128)(2,1)S(1)}, bf16[256,128]{1,0:T(8,128)(2,1)S(1)}, u32[]{:S(2)}, u32[]{:S(2)}) collective-permute-start(bf16[256,128]{1,0:T(8,128)(2,1)S(1)} %add_convert_fusion.5), channel_id=1, source_target_pairs={{0,4},{4,8},{8,12},{12,16},{16,20},{20,24},{24,28},{28,0},{1,5},{5... | collective-permute-start | bytes 196616 | tf_op jit(solution)/shard_map/ppermute | solution.py:19
  39.4 14.6 %collective-permute-start.11 = (bf16[256,128]{1,0:T(8,128)(2,1)S(1)}, bf16[256,128]{1,0:T(8,128)(2,1)S(1)}, u32[]{:S(2)}, u32[]{:S(2)}) collective-permute-start(bf16[256,128]{1,0:T(8,128)(2,1)S(1)} %add_convert_fusion.2), channel_id=1, source_target_pairs={{0,4},{4,8},{8,12},{12,16},{16,20},{20,24},{24,28},{28,0},{1,5},{5... | collective-permute-start | bytes 196616 | tf_op jit(solution)/shard_map/ppermute | solution.py:19
  41.0 8.9 %collective-permute-start.3 = (bf16[256,128]{1,0:T(8,128)(2,1)S(1)}, bf16[256,128]{1,0:T(8,128)(2,1)S(1)}, u32[]{:S(2)}, u32[]{:S(2)}) collective-permute-start(bf16[256,128]{1,0:T(8,128)(2,1)S(1)} %collective-permute-done.1), channel_id=1, source_target_pairs={{0,4},{4,8},{8,12},{12,16},{16,20},{20,24},{24,28},{1,5},{5,9},{9,... | collective-permute-start | bytes 196616 | tf_op jit(solution)/shard_map/ppermute | solution.py:13
  44.4 3.8 %collective-permute-start.2 = (bf16[256,128]{1,0:T(8,128)(2,1)S(1)}, bf16[256,128]{1,0:T(8,128)(2,1)S(1)}, u32[]{:S(2)}, u32[]{:S(2)}) collective-permute-start(bf16[256,128]{1,0:T(8,128)(2,1)S(1)} %collective-permute-done), channel_id=1, source_target_pairs={{0,4},{4,8},{8,12},{12,16},{16,20},{20,24},{24,28},{1,5},{5,9},{9,... | collective-permute-start | bytes 196616 | tf_op jit(solution)/shard_map/ppermute | solution.py:13
  51.6 17.2 %collective-permute-start.8 = (bf16[256,128]{1,0:T(8,128)(2,1)S(1)}, bf16[256,128]{1,0:T(8,128)(2,1)S(1)}, u32[]{:S(2)}, u32[]{:S(2)}) collective-permute-start(bf16[256,128]{1,0:T(8,128)(2,1)S(1)} %add_convert_fusion.4), channel_id=1, source_target_pairs={{0,4},{4,8},{8,12},{12,16},{16,20},{20,24},{24,28},{28,0},{1,5},{5... | collective-permute-start | bytes 196616 | tf_op jit(solution)/shard_map/ppermute | solution.py:19
  54.0 16.2 %collective-permute-start.12 = (bf16[256,128]{1,0:T(8,128)(2,1)S(1)}, bf16[256,128]{1,0:T(8,128)(2,1)S(1)}, u32[]{:S(2)}, u32[]{:S(2)}) collective-permute-start(bf16[256,128]{1,0:T(8,128)(2,1)S(1)} %add_convert_fusion.1), channel_id=1, source_target_pairs={{0,4},{4,8},{8,12},{12,16},{16,20},{20,24},{24,28},{28,0},{1,5},{5... | collective-permute-start | bytes 196616 | tf_op jit(solution)/shard_map/ppermute | solution.py:19
  55.8 11.3 %collective-permute-start.5 = (bf16[256,128]{1,0:T(8,128)(2,1)S(1)}, bf16[256,128]{1,0:T(8,128)(2,1)S(1)}, u32[]{:S(2)}, u32[]{:S(2)}) collective-permute-start(bf16[256,128]{1,0:T(8,128)(2,1)S(1)} %collective-permute-done.3), channel_id=1, source_target_pairs={{0,4},{4,8},{8,12},{12,16},{16,20},{20,24},{24,28},{1,5},{5,9},{9,... | collective-permute-start | bytes 196616 | tf_op jit(solution)/shard_map/ppermute | solution.py:13
  59.2 6.2 %collective-permute-start.4 = (bf16[256,128]{1,0:T(8,128)(2,1)S(1)}, bf16[256,128]{1,0:T(8,128)(2,1)S(1)}, u32[]{:S(2)}, u32[]{:S(2)}) collective-permute-start(bf16[256,128]{1,0:T(8,128)(2,1)S(1)} %collective-permute-done.2), channel_id=1, source_target_pairs={{0,4},{4,8},{8,12},{12,16},{16,20},{20,24},{24,28},{1,5},{5,9},{9,... | collective-permute-start | bytes 196616 | tf_op jit(solution)/shard_map/ppermute | solution.py:13
  67.0 7.2 %copy-start.1 = (bf16[4096,512]{1,0:T(8,128)(2,1)S(1)}, bf16[4096,512]{1,0:T(8,128)(2,1)}, u32[]{:S(2)}) copy-start(bf16[4096,512]{1,0:T(8,128)(2,1)} %param.19) | copy-start | bytes 12582916
  68.8 6.7 %collective-permute-start.9 = (bf16[256,128]{1,0:T(8,128)(2,1)S(1)}, bf16[256,128]{1,0:T(8,128)(2,1)S(1)}, u32[]{:S(2)}, u32[]{:S(2)}) collective-permute-start(bf16[256,128]{1,0:T(8,128)(2,1)S(1)} %add_convert_fusion.3), channel_id=1, source_target_pairs={{0,20},{4,24},{8,28},{12,0},{16,4},{20,8},{24,12},{28,16},{1,21},{... | collective-permute-start | bytes 196616 | tf_op jit(solution)/shard_map/ppermute | solution.py:19
  70.3 6.0 %collective-permute-start.13 = (bf16[256,128]{1,0:T(8,128)(2,1)S(1)}, bf16[256,128]{1,0:T(8,128)(2,1)S(1)}, u32[]{:S(2)}, u32[]{:S(2)}) collective-permute-start(bf16[256,128]{1,0:T(8,128)(2,1)S(1)} %add_convert_fusion), channel_id=1, source_target_pairs={{0,20},{4,24},{8,28},{12,0},{16,4},{20,8},{24,12},{28,16},{1,21},{... | collective-permute-start | bytes 196616 | tf_op jit(solution)/shard_map/ppermute | solution.py:19
  75.5 1.2 %copy-start.2 = (bf16[4096,128]{1,0:T(8,128)(2,1)S(1)}, bf16[4096,128]{1,0:T(8,128)(2,1)}, u32[]{:S(2)}) copy-start(bf16[4096,128]{1,0:T(8,128)(2,1)} %param.21) | copy-start | bytes 3145732
Sparse Core Ops, SparseCore 0:
  79.0 33.1 reduce-scatter.1
where the time goes:
time: 120 us; the launch traced here: 119 us
  starting transfers between devices  37 us (31%)
  waiting for transfers between devices  36.6 us (30%)
  matrix products  19.2 us (16%)
  between operations  16.6 us (14%)
  local copies, waits for them, and re-layouts  5.55 us (5%)
  other arithmetic  4.11 us (3%)
    reduce_scatter x1, waiting for transfers between devices, on_device(): lax.psum_scatter(partial_term.astype(jnp.bfloat16), 'tp', scatter_dimensi...  33.3 us
    ppermute x6, starting transfers between devices, shifted(): return lax.ppermute(array, axis, pairs)  21.5 us
    ppermute x8, starting transfers between devices, passed_along(): return lax.ppermute(value, axis, pairs)  15.5 us
    dot_general x4, matrix products, pair_grads(): jnp.einsum('qhd,kd->hqk', grad_out, value_blk, preferred_element_type=jnp...  5.43 us
    dot_general x4, matrix products, pair_grads(): jnp.einsum('hqk,qhd->kd', dropped, grad_out, preferred_element_type=jnp.f...  5.05 us
    ppermute x6, waiting for transfers between devices, shifted(): return lax.ppermute(array, axis, pairs)  3.23 us
    dot_general x4, matrix products, pair_grads(): jnp.einsum('qhd,kd->hqk', query_blk, key_blk, preferred_element_type=jnp....  2.44 us
  transfers between devices with their start and end apart: 15, of which 3 were waited for; matrix products, arithmetic and copies ran while one was open for 22% of the time, Pallas kernels for 0%

commit v1 on v0

v1 whole, which is shorter than its diff:
```python
import functools
import math

import jax
import jax.numpy as jnp
from jax import lax
from jax.experimental import pallas as pl
from jax.experimental.pallas import tpu as pltpu
from jax.sharding import PartitionSpec as P

keep_level = 103
keep_scale = 1024.0 / 921.0
log2_e = math.log2(math.e)
f32, bf16, i32 = jnp.float32, jnp.bfloat16, jnp.int32
in_vmem = pl.BlockSpec(memory_space=pltpu.VMEM)
in_smem = pl.BlockSpec(memory_space=pltpu.SMEM)
chunks = 2


def cyclic(array, axis, by):
    count = lax.axis_size(axis)
    return lax.ppermute(array, axis, [(i, (i + by) % count) for i in range(count)])


def other_core(array):
    count = lax.axis_size("tp")
    return lax.ppermute(array, "tp", [(i, i ^ 1) for i in range(count)])


def dot(left, right, left_dim, right_dim):
    return lax.dot_general(
        left, right, (((left_dim,), (right_dim,)), ((), ())), preferred_element_type=f32
    )


def keep_mask(mixed):
    mixed = mixed ^ lax.shift_right_logical(mixed, i32(15))
    mixed = mixed * i32(739982445)
    mixed = mixed ^ lax.shift_right_logical(mixed, i32(12))
    mixed = mixed * i32(695872825)
    mixed = mixed ^ lax.shift_right_logical(mixed, i32(15))
    return (mixed & i32(1023)) >= i32(keep_level)


def block_grads(offset, window, heads, counter_ref, key, value, query_ref, grad_ref, rows_ref):
    rows, width = key.shape
    block_id = lax.axis_index("ctx")
    first_head = lax.axis_index("tp") * heads
    seed, base = counter_ref[0], counter_ref[1]
    key_index = lax.broadcasted_iota(i32, (rows, rows), 0)
    query_index = lax.broadcasted_iota(i32, (rows, rows), 1)
    key_part = (key_index + (base + (block_id - offset) * rows)) * i32(19349663)
    query_part = (
        lax.broadcasted_iota(i32, (1, rows), 1) + (base + block_id * rows)
    ) * i32(73856093) + seed
    key_t = key.T
    scale = log2_e * width**-0.5
    key_sum = value_sum = None
    query_parts = []
    for head in range(heads):
        cols = pl.ds(head * width, width)
        query, grad = query_ref[:, cols], grad_ref[:, cols]
        log_norm = rows_ref[pl.ds(head, 1), :]
        row_delta = rows_ref[pl.ds(heads + head, 1), :]
        kept = keep_mask(key_part + (query_part + (first_head + head) * i32(83492791)))
        probs = jnp.exp2(dot(key, query, 1, 1) * scale - log_norm)
        spacing = query_index - key_index
        if offset == 0:
            probs = jnp.where(spacing >= 0, probs, f32(0.0))
        if (offset + 1) * rows > window:
            probs = jnp.where(spacing < window - offset * rows, probs, f32(0.0))
        dropped = jnp.where(kept, probs, f32(0.0)).astype(bf16)
        grad_probs = dot(value, grad, 1, 1)
        grad_scores = (
            probs * (jnp.where(kept, grad_probs, f32(0.0)) - row_delta)
        ).astype(bf16)
        value_add = dot(dropped, grad, 1, 0)
        key_add = dot(grad_scores, query, 1, 0)
        key_sum = key_add if head == 0 else key_sum + key_add
        value_sum = value_add if head == 0 else value_sum + value_add
        query_parts.append(dot(key_t, grad_scores, 1, 0))
    return key_sum, value_sum, query_parts


def own_kernel(
    window, heads, counter_ref, key_ref, value_ref, query_ref, grad_ref, output_ref, norm_ref,
    rows_ref, total_ref, sums_ref,
):
    rows, width = key_ref.shape
    lane = lax.broadcasted_iota(i32, (rows, 128), 1)
    packed = jnp.zeros((rows, 128), f32)
    for head in range(heads):
        cols = pl.ds(head * width, width)
        delta = jnp.sum(
            grad_ref[:, cols].astype(f32) * output_ref[:, cols].astype(f32), axis=1, keepdims=True
        )
        packed = jnp.where(lane == heads + head, delta * f32(1.0 / keep_scale), packed)
        packed = jnp.where(lane == head, norm_ref[:, head : head + 1] * f32(log2_e), packed)
    rows_ref[...] = packed.T[: 2 * heads]
    key_sum, value_sum, query_parts = block_grads(
        0, window, heads, counter_ref, key_ref[...], value_ref[...], query_ref, grad_ref, rows_ref
    )
    grad_scale = keep_scale * width**-0.5
    sums_ref[:, :width] = key_sum * f32(grad_scale)
    sums_ref[:, width:] = value_sum * f32(keep_scale)
    for head, part in enumerate(query_parts):
        total_ref[:, pl.ds(head * rows, rows)] = part


def pair_kernel(
    offset, window, heads, last, counter_ref, mask_ref, key_value_ref, query_ref, grad_ref,
    rows_ref, before_ref, total_ref, sums_ref,
):
    rows = key_value_ref.shape[0]
    width = key_value_ref.shape[1] // 2
    active = (lax.axis_index("ctx") >= offset) & (mask_ref[0, offset] == 1)
    grad_scale = keep_scale * width**-0.5

    @pl.when(active)
    def _():
        key_sum, value_sum, query_parts = block_grads(
            offset, window, heads, counter_ref, key_value_ref[:, :width], key_value_ref[:, width:],
            query_ref, grad_ref, rows_ref,
        )
        sums_ref[:, :width] = (key_sum * f32(grad_scale)).astype(bf16)
        sums_ref[:, width:] = (value_sum * f32(keep_scale)).astype(bf16)
        for head, part in enumerate(query_parts):
            cols = pl.ds(head * rows, rows)
            if last:
                total_ref[:, pl.ds(head * width, width)] = (
                    (before_ref[:, cols] + part).T * f32(grad_scale)
                ).astype(bf16)
            else:
                total_ref[:, cols] = before_ref[:, cols] + part

    @pl.when(jnp.logical_not(active))
    def _():
        sums_ref[...] = jnp.zeros(sums_ref.shape, bf16)
        for head in range(heads):
            cols = pl.ds(head * rows, rows)
            if last:
                total_ref[:, pl.ds(head * width, width)] = (
                    before_ref[:, cols].T * f32(grad_scale)
                ).astype(bf16)
            else:
                total_ref[:, cols] = before_ref[:, cols]


def project_kernel(at_ref, *refs):
    count = (len(refs) - 1) // 2
    total = None
    for left, right in zip(refs[:count], refs[count:-1]):
        part = dot(left[...], right[...], 1, 1)
        total = part if total is None else total + part
    refs[-1][...] = total.astype(bf16)


def project(at, step, cols, lefts, rights):
    rows = lefts[0].shape[0]
    return pl.pallas_call(
        project_kernel,
        grid_spec=pltpu.PrefetchScalarGridSpec(
            num_scalar_prefetch=1,
            grid=(cols // step,),
            in_specs=[pl.BlockSpec(left.shape, lambda i, at: (0, 0)) for left in lefts]
            + [pl.BlockSpec((step, right.shape[1]), lambda i, at: (at[0] + i, 0)) for right in rights],
            out_specs=pl.BlockSpec((rows, step), lambda i, at: (0, i)),
        ),
        out_shape=jax.ShapeDtypeStruct((rows, cols), bf16),
        compiler_params=pltpu.CompilerParams(vmem_limit_bytes=32 * 2**20),
        name="project",
    )(at, *lefts, *rights)


def on_device(
    queries,
    keys,
    values,
    outputs,
    out_grad,
    log_norm,
    block_mask,
    counter_base,
    q_weight,
    k_weight,
    v_weight,
):
    rows, width = keys.shape
    heads = log_norm.shape[1]
    steps = block_mask.shape[1]
    window = 3 * rows + rows // 2
    tp_size = lax.axis_size("tp")
    tp_id = lax.axis_index("tp")
    params = pltpu.CompilerParams(vmem_limit_bytes=48 * 2**20)

    key_value = jnp.concatenate([keys, values], axis=1)
    arrived = {offset: cyclic(key_value, "ctx", offset) for offset in range(1, steps)}
    weights = (q_weight, k_weight, v_weight)
    other_weights = tuple(other_core(weight) for weight in weights)

    row_values, total, own_sums = pl.pallas_call(
        functools.partial(own_kernel, window, heads),
        in_specs=[in_smem] + [in_vmem] * 6,
        out_specs=[in_vmem] * 3,
        out_shape=[
            jax.ShapeDtypeStruct((2 * heads, rows), f32),
            jax.ShapeDtypeStruct((width, heads * rows), f32),
            jax.ShapeDtypeStruct((rows, 2 * width), f32),
        ],
        compiler_params=params,
        name="own_block",
    )(counter_base, keys, values, queries, out_grad, outputs, log_norm)

    returned = []
    for offset in range(1, steps):
        last = offset == steps - 1
        total, sums = pl.pallas_call(
            functools.partial(pair_kernel, offset, window, heads, last),
            in_specs=[in_smem] * 2 + [in_vmem] * 5,
            out_specs=[in_vmem] * 2,
            out_shape=[
                jax.ShapeDtypeStruct((rows, heads * width), bf16)
                if last
                else jax.ShapeDtypeStruct((width, heads * rows), f32),
                jax.ShapeDtypeStruct((rows, 2 * width), bf16),
            ],
            compiler_params=params,
            name="block_back_%d" % offset,
        )(counter_base, block_mask, arrived[offset], queries, out_grad, row_values, total)
        returned.append(cyclic(sums, "ctx", -offset))
    grad_query = total
    other_query = other_core(grad_query)
    sums = own_sums
    for item in returned:
        sums = sums + item.astype(f32)
    sums = sums.astype(bf16)
    other_sums = other_core(sums)

    lefts = [grad_query, other_query, sums, other_sums]
    key_value_w = [
        jnp.concatenate([pair[0], pair[1]], axis=1)
        for pair in ((k_weight, v_weight), other_weights[1:])
    ]
    rights = [q_weight, other_weights[0], *key_value_w]
    cols = q_weight.shape[0] // tp_size
    piece = cols // chunks
    step = min(piece, 256)
    mine = None
    sent = []
    for hop in range(2, tp_size, 2):
        target = lax.rem(tp_id + hop, tp_size)
        parts = []
        for chunk in range(chunks):
            at = (target * (cols // step) + chunk * (piece // step)).astype(i32).reshape(1)
            part = project(at, step, piece, lefts, rights)
            parts.append(cyclic(part, "tp", hop))
        sent.append(parts)
    at = (tp_id * (cols // step)).astype(i32).reshape(1)
    mine = project(at, step, cols, lefts, rights).astype(f32)
    for parts in sent:
        mine = mine + jnp.concatenate(parts, axis=1).astype(f32)
    return mine.astype(bf16)


def solution(mesh):
    return jax.shard_map(
        on_device,
        mesh=mesh,
        in_specs=(
            P("ctx", "tp"),
            P("ctx", "tp"),
            P("ctx", "tp"),
            P("ctx", "tp"),
            P("ctx", "tp"),
            P("ctx", "tp"),
            P("ctx", None),
            P(),
            P(None, "tp"),
            P(None, "tp"),
            P(None, "tp"),
        ),
        out_specs=P("ctx", "tp"),
        check_vma=False,
    )
```

time: 120 us -> 64.3 us (0.54)
  waiting for transfers between devices: 36.6 us -> 6.57 us
  matrix products: 19.2 us -> 0 us
  between operations: 16.6 us -> 0.25 us
  local copies, waits for them, and re-layouts: 5.55 us -> 17.5 us
  Pallas kernels: 0 us -> 11.4 us
  starting transfers between devices: 37 us -> 26.7 us
  other arithmetic: 4.11 us -> 2.06 us
    reduce_scatter x1 -> x0, waiting for transfers between devices: 33.3 us -> none  [on_device(): lax.psum_scatter(partial_term.astype(jnp.bfloat16), 'tp', scatter_dimensi...]
    dot_general x23 -> x0, matrix products: 19.2 us -> none  [the longest x4 5.43 us: pair_grads(): jnp.einsum('qhd,kd->hqk', grad_out, value_blk, preferred_element_type=jnp...]
    unnamed x16 -> x34, local copies, waits for them, and re-layouts: 0.5 us -> 14.9 us
    pallas_call x0 -> x7, Pallas kernels: none -> 11.4 us  [the longest x3 7.14 us: project(): pl.pallas_call(project_kernel, grid_spec=pltpu.PrefetchScalarGridSpec(num...]
    ppermute x14 -> x13, starting transfers between devices: 37 us -> 26.7 us  [the longest x8 25.5 us: cyclic(): lax.ppermute(array, axis, [(i, (i + by) % count) for i in range(count)])]
    ppermute x14 -> x13, waiting for transfers between devices: 3.25 us -> 6.57 us  [the longest x8 6.55 us: cyclic(): lax.ppermute(array, axis, [(i, (i + by) % count) for i in range(count)])]
    slice x2 -> x0, local copies, waits for them, and re-layouts: 2.8 us -> none  [the longest x1 1.48 us: on_device(): active = (source >= 0) & (mask_row[offset] == 1)]
    mul x5 -> x0, other arithmetic: 2.61 us -> none  [the longest x3 1.95 us: keep_mask(): key_pos[None, None, :] * 19349663]
  transfers between devices with their start and end apart: 15 -> 13, of which waited for: 3 -> 3; matrix products, arithmetic and copies ran while one was open for 22% -> 9% of each run, Pallas kernels for 0% -> 14%
where the time goes in v1:
time: 64.3 us; the launch traced here: 64.4 us
  starting transfers between devices  26.7 us (42%)
  local copies, waits for them, and re-layouts  17.5 us (27%)
  Pallas kernels  11.4 us (18%)
  waiting for transfers between devices  6.57 us (10%)
  other arithmetic  2.06 us (3%)
    ppermute x8, starting transfers between devices, cyclic(): lax.ppermute(array, axis, [(i, (i + by) % count) for i in range(count)])  25.5 us
    unnamed x34, local copies, waits for them, and re-layouts  14.9 us
    pallas_call x3, Pallas kernels, project(): pl.pallas_call(project_kernel, grid_spec=pltpu.PrefetchScalarGridSpec(num...  7.14 us
    ppermute x8, waiting for transfers between devices, cyclic(): lax.ppermute(array, axis, [(i, (i + by) % count) for i in range(count)])  6.55 us
    pallas_call x1, Pallas kernels, on_device(): pl.pallas_call(functools.partial(own_kernel, window, heads), in_specs=[in...  2.27 us
    convert_element_type x1, other arithmetic, on_device(): return mine.astype(bf16)  2.01 us
    pallas_call x3, Pallas kernels, on_device(): pl.pallas_call(functools.partial(pair_kernel, offset, window, heads, last...  1.96 us
    concatenate x2, local copies, waits for them, and re-layouts, on_device(): jnp.concatenate([pair[0], pair[1]], axis=1)  1.72 us
  transfers between devices with their start and end apart: 13, of which 3 were waited for; matrix products, arithmetic and copies ran while one was open for 9% of the time, Pallas kernels for 14%

profile of v1, /device:TPU:0, one launch (start us, length us, event | category | flops | bytes accessed | tf_op | source)
XLA Modules:
  0.0 64.4 jit_solution(4824275125937637425)
XLA Ops:
  0.5 0.9 %constant_dynamic-update-slice_fusion.1 = bf16[256,256]{1,0:T(8,128)(2,1)S(1)} fusion(bf16[256,128]{1,0:T(8,128)(2,1)} %key_ref.1), kind=kLoop, calls=%fused_computation.3 | loop fusion | bytes 131072
  1.3 0.9 %constant_dynamic-update-slice_fusion = bf16[256,256]{1,0:T(8,128)(2,1)S(1)} fusion(bf16[256,256]{1,0:T(8,128)(2,1)S(1)} %constant_dynamic-update-slice_fusion.1, bf16[256,128]{1,0:T(8,128)(2,1)} %value_ref.1), kind=kLoop, calls=%fused_computation.2 | loop fusion | bytes 131072 | tf_op jit(solution)/shard_map/concatenate | solution.py:196
  2.2 2.5 %collective-permute-start.2 = (bf16[256,256]{1,0:T(8,128)(2,1)S(1)}, bf16[256,256]{1,0:T(8,128)(2,1)S(1)}, u32[]{:S(2)}, u32[]{:S(2)}) collective-permute-start(bf16[256,256]{1,0:T(8,128)(2,1)S(1)} %constant_dynamic-update-slice_fusion), channel_id=1, source_target_pairs={{0,4},{4,8},{8,12},{12,16},{16,20},{20,24},{24,28},{28,0},{1,5},{5... | collective-permute-start | bytes 393224 | tf_op jit(solution)/shard_map/ppermute | solution.py:22
  4.7 1.6 %collective-permute-start.1 = (bf16[256,256]{1,0:T(8,128)(2,1)S(1)}, bf16[256,256]{1,0:T(8,128)(2,1)S(1)}, u32[]{:S(2)}, u32[]{:S(2)}) collective-permute-start(bf16[256,256]{1,0:T(8,128)(2,1)S(1)} %constant_dynamic-update-slice_fusion), channel_id=1, source_target_pairs={{0,8},{4,12},{8,16},{12,20},{16,24},{20,28},{24,0},{28,4},{1,9},{5... | collective-permute-start | bytes 393224 | tf_op jit(solution)/shard_map/ppermute | solution.py:22
  6.3 2.6 %collective-permute-start = (bf16[256,256]{1,0:T(8,128)(2,1)S(1)}, bf16[256,256]{1,0:T(8,128)(2,1)S(1)}, u32[]{:S(2)}, u32[]{:S(2)}) collective-permute-start(bf16[256,256]{1,0:T(8,128)(2,1)S(1)} %constant_dynamic-update-slice_fusion), channel_id=1, source_target_pairs={{0,12},{4,16},{8,20},{12,24},{16,28},{20,0},{24,4},{28,8},{1,13},{... | collective-permute-start | bytes 393224 | tf_op jit(solution)/shard_map/ppermute | solution.py:22
  8.9 0.8 %copy.12.norm_ref = f32[256,4]{1,0:T(8,128)S(1)} copy(f32[256,4]{0,1:T(4,128)} %param.16) | data formatting | bytes 8192 | tf_op args[5]
  9.7 0.9 %copy-done.4 = bf16[256,512]{1,0:T(8,128)(2,1)S(1)} copy-done((bf16[256,512]{1,0:T(8,128)(2,1)S(1)}, bf16[256,512]{1,0:T(8,128)(2,1)}, u32[]{:S(2)}) %copy-start.4) | copy-done | bytes 262168
  10.6 0.9 %copy-done.6 = bf16[256,512]{1,0:T(8,128)(2,1)S(1)} copy-done((bf16[256,512]{1,0:T(8,128)(2,1)S(1)}, bf16[256,512]{1,0:T(8,128)(2,1)}, u32[]{:S(2)}) %copy-start.6) | copy-done | bytes 262168
  11.6 0.9 %copy-done.8 = bf16[256,512]{1,0:T(8,128)(2,1)S(1)} copy-done((bf16[256,512]{1,0:T(8,128)(2,1)S(1)}, bf16[256,512]{1,0:T(8,128)(2,1)}, u32[]{:S(2)}) %copy-start.8) | copy-done | bytes 262168
  12.5 0.8 %copy-done.9 = bf16[256,128]{1,0:T(8,128)(2,1)S(1)} copy-done((bf16[256,128]{1,0:T(8,128)(2,1)S(1)}, bf16[256,128]{1,0:T(8,128)(2,1)}, u32[]{:S(2)}) %copy-start.9) | copy-done | bytes 65560
  13.4 0.8 %copy-done.10 = bf16[256,128]{1,0:T(8,128)(2,1)S(1)} copy-done((bf16[256,128]{1,0:T(8,128)(2,1)S(1)}, bf16[256,128]{1,0:T(8,128)(2,1)}, u32[]{:S(2)}) %copy-start.10) | copy-done | bytes 65560
  14.2 0.7 %copy-done.11 = s32[2]{0:T(128)S(1)} copy-done((s32[2]{0:T(128)S(1)}, s32[2]{0:T(128)}, u32[]{:S(2)}) %copy-start.11) | copy-done | bytes 32
  14.9 2.3 %own_block.1 = (f32[8,256]{1,0:T(8,128)S(1)}, f32[128,1024]{1,0:T(8,128)S(1)}, f32[256,256]{1,0:T(8,128)S(1)}) custom-call(s32[2]{0:T(128)S(1)} %copy-done.11, bf16[256,128]{1,0:T(8,128)(2,1)S(1)} %copy-done.9, bf16[256,128]{1,0:T(8,128)(2,1)S(1)} %copy-done.10, bf16[256,512]{1,0:T(8,128)(2,1)S(1)} %copy-done.4, bf16[256,512]{1,0:T(8,128)(2,1)S(1)} %copy-done.6, ...), custom_call_target="tpu_custom_call" | custom-call | tf_op jit(solution)/shard_map/own_block/pallas_call | solution.py:201
  17.7 0.9 %copy-done.5 = bf16[256,512]{1,0:T(8,128)(2,1)S(1)} copy-done((bf16[256,512]{1,0:T(8,128)(2,1)S(1)}, bf16[256,512]{1,0:T(8,128)(2,1)}, u32[]{:S(2)}) %copy-start.5) | copy-done | bytes 262168
  18.7 0.9 %copy-done.7 = bf16[256,512]{1,0:T(8,128)(2,1)S(1)} copy-done((bf16[256,512]{1,0:T(8,128)(2,1)S(1)}, bf16[256,512]{1,0:T(8,128)(2,1)}, u32[]{:S(2)}) %copy-start.7) | copy-done | bytes 262168
  19.6 0.7 %copy-done.12 = s32[1,4]{1,0:T(1,128)S(1)} copy-done((s32[1,4]{1,0:T(1,128)S(1)}, s32[1,4]{1,0:T(1,128)}, u32[]{:S(2)}) %copy-start.12) | copy-done | bytes 40
  21.5 0.8 %block_back_3.1 = (bf16[256,512]{1,0:T(8,128)(2,1)S(1)}, bf16[256,256]{1,0:T(8,128)(2,1)S(1)}) custom-call(s32[2]{0:T(128)S(1)} %copy-done.11, s32[1,4]{1,0:T(1,128)S(1)} %copy-done.12, bf16[256,256]{1,0:T(8,128)(2,1)S(1)} %collective-permute-done.key_value_ref, bf16[256,512]{1,0:T(8,128)(2,1)S(1)} %copy-done.5, bf16[256,512]{1,0:T(8,128)(2,1)S(1)} %copy-done.7, ...), custom_call_target="tpu_custom_call" | custom-call | tf_op jit(solution)/shard_map/block_back_3/pallas_call | solution.py:217
  22.3 3.8 %collective-permute-start.6 = (bf16[256,256]{1,0:T(8,128)(2,1)S(1)}, bf16[256,256]{1,0:T(8,128)(2,1)S(1)}, u32[]{:S(2)}, u32[]{:S(2)}) collective-permute-start(bf16[256,256]{1,0:T(8,128)(2,1)S(1)} %get-tuple-element.22), channel_id=1, source_target_pairs={{0,20},{4,24},{8,28},{12,0},{16,4},{20,8},{24,12},{28,16},{1,21},{... | collective-permute-start | bytes 393224 | tf_op jit(solution)/shard_map/ppermute | solution.py:22
  26.3 2.3 %collective-permute-start.5 = (bf16[256,256]{1,0:T(8,128)(2,1)S(1)}, bf16[256,256]{1,0:T(8,128)(2,1)S(1)}, u32[]{:S(2)}, u32[]{:S(2)}) collective-permute-start(bf16[256,256]{1,0:T(8,128)(2,1)S(1)} %get-tuple-element.21), channel_id=1, source_target_pairs={{0,24},{4,28},{8,0},{12,4},{16,8},{20,12},{24,16},{28,20},{1,25},{... | collective-permute-start | bytes 393224 | tf_op jit(solution)/shard_map/ppermute | solution.py:22
  28.6 0.7 %collective-permute-done.6 = bf16[256,256]{1,0:T(8,128)(2,1)S(1)} collective-permute-done((bf16[256,256]{1,0:T(8,128)(2,1)S(1)}, bf16[256,256]{1,0:T(8,128)(2,1)S(1)}, u32[]{:S(2)}, u32[]{:S(2)}) %collective-permute-start.6) | collective-permute-done | bytes 131104 | tf_op jit(solution)/shard_map/ppermute | solution.py:22
  29.2 10.6 %collective-permute-start.4 = (bf16[256,256]{1,0:T(8,128)(2,1)S(1)}, bf16[256,256]{1,0:T(8,128)(2,1)S(1)}, u32[]{:S(2)}, u32[]{:S(2)}) collective-permute-start(bf16[256,256]{1,0:T(8,128)(2,1)S(1)} %get-tuple-element.20), channel_id=1, source_target_pairs={{0,28},{4,0},{8,4},{12,8},{16,12},{20,16},{24,20},{28,24},{1,29},{... | collective-permute-start | bytes 393224 | tf_op jit(solution)/shard_map/ppermute | solution.py:22
  40.2 2.6 %collective-permute-done.4 = bf16[256,256]{1,0:T(8,128)(2,1)S(1)} collective-permute-done((bf16[256,256]{1,0:T(8,128)(2,1)S(1)}, bf16[256,256]{1,0:T(8,128)(2,1)S(1)}, u32[]{:S(2)}, u32[]{:S(2)}) %collective-permute-start.4) | collective-permute-done | bytes 131104 | tf_op jit(solution)/shard_map/ppermute | solution.py:22
  42.9 1.6 %constant_dynamic-update-slice_fusion.5 = bf16[4096,256]{1,0:T(8,128)(2,1)S(1)} fusion(bf16[4096,128]{1,0:T(8,128)(2,1)} %collective-permute-done.9), kind=kLoop, calls=%fused_computation.7 | loop fusion | bytes 2097152
  44.5 1.5 %constant_dynamic-update-slice_fusion.4.refs_7_ = bf16[4096,256]{1,0:T(8,128)(2,1)S(1)} fusion(bf16[4096,256]{1,0:T(8,128)(2,1)S(1)} %constant_dynamic-update-slice_fusion.5, bf16[4096,128]{1,0:T(8,128)(2,1)} %collective-permute-done.10), kind=kLoop, calls=%fused_computation.6 | loop fusion | bytes 2097152 | tf_op jit(solution)/shard_map/concatenate | solution.py:241
  46.0 2.1 %project.4 = bf16[256,512]{1,0:T(8,128)(2,1)S(1)} custom-call(s32[1]{0:T(128)} %bitcast.1.at_ref, bf16[256,512]{1,0:T(8,128)(2,1)S(1)} %get-tuple-element.18.refs_0_, bf16[256,512]{1,0:T(8,128)(2,1)S(1)} %collective-permute-done.3.refs_1_, bf16[256,256]{1,0:T(8,128)(2,1)S(1)} %add_convert_fusion.1.refs_2_, ...), custom_call_target="tpu_custom_call" | custom-call | tf_op jit(solution)/shard_map/project/pallas_call | solution.py:160
  48.1 1.6 %collective-permute-start.11 = (bf16[256,512]{1,0:T(8,128)(2,1)S(1)}, bf16[256,512]{1,0:T(8,128)(2,1)}, u32[]{:S(2)}, u32[]{:S(2)}) collective-permute-start(bf16[256,512]{1,0:T(8,128)(2,1)S(1)} %project.4), channel_id=1, source_target_pairs={{0,2},{1,3},{2,0},{3,1},{4,6},{5,7},{6,4},{7,5},{8,10},{9,11},{10,... | collective-permute-start | bytes 786440 | tf_op jit(solution)/shard_map/ppermute | solution.py:22
  49.7 1.8 %project.5 = bf16[256,512]{1,0:T(8,128)(2,1)S(1)} custom-call(s32[1]{0:T(128)} %bitcast.2.at_ref, bf16[256,512]{1,0:T(8,128)(2,1)S(1)} %get-tuple-element.18.refs_0_, bf16[256,512]{1,0:T(8,128)(2,1)S(1)} %collective-permute-done.3.refs_1_, bf16[256,256]{1,0:T(8,128)(2,1)S(1)} %add_convert_fusion.1.refs_2_, ...), custom_call_target="tpu_custom_call" | custom-call | tf_op jit(solution)/shard_map/project/pallas_call | solution.py:160
  52.1 2.2 %copy-done.1 = bf16[4096,512]{1,0:T(8,128)(2,1)S(1)} copy-done((bf16[4096,512]{1,0:T(8,128)(2,1)S(1)}, bf16[4096,512]{1,0:T(8,128)(2,1)}, u32[]{:S(2)}) %copy-start.1) | copy-done | bytes 4194328
  54.3 1.6 %copy-done.3 = bf16[4096,256]{1,0:T(8,128)(2,1)S(1)} copy-done((bf16[4096,256]{1,0:T(8,128)(2,1)S(1)}, bf16[4096,256]{1,0:T(8,128)(2,1)}, u32[]{:S(2)}) %copy-start.3) | copy-done | bytes 2097176
  55.9 3.2 %project.3 = bf16[256,1024]{1,0:T(8,128)(2,1)S(1)} custom-call(s32[1]{0:T(128)} %bitcast.at_ref, bf16[256,512]{1,0:T(8,128)(2,1)S(1)} %get-tuple-element.18.refs_0_, bf16[256,512]{1,0:T(8,128)(2,1)S(1)} %collective-permute-done.3.refs_1_, bf16[256,256]{1,0:T(8,128)(2,1)S(1)} %add_convert_fusion.1.refs_2_, ...), custom_call_target="tpu_custom_call" | custom-call | tf_op jit(solution)/shard_map/project/pallas_call | solution.py:160
  59.1 3.3 %collective-permute-done.12 = bf16[256,512]{1,0:T(8,128)(2,1)} collective-permute-done((bf16[256,512]{1,0:T(8,128)(2,1)S(1)}, bf16[256,512]{1,0:T(8,128)(2,1)}, u32[]{:S(2)}, u32[]{:S(2)}) %collective-permute-start.12) | collective-permute-done | bytes 262176 | tf_op jit(solution)/shard_map/ppermute | solution.py:22
  62.4 2.0 %add_convert_fusion = bf16[256,1024]{1,0:T(8,128)(2,1)} fusion(bf16[256,1024]{1,0:T(8,128)(2,1)S(1)} %project.3, bf16[256,512]{1,0:T(8,128)(2,1)} %collective-permute-done.12, bf16[256,512]{1,0:T(8,128)(2,1)} %collective-permute-done.11), kind=kLoop, calls=%fused_computation | loop fusion | flops 1835008 | bytes 1572864 | tf_op jit(solution)/shard_map/convert_element_type | solution.py:262
  (40 shorter events, 3.5 us)
Async XLA Ops:
  0.0 46.0 %collective-permute-start.8 = (bf16[4096,512]{1,0:T(8,128)(2,1)}, bf16[4096,512]{1,0:T(8,128)(2,1)}, u32[]{:S(2)}, u32[]{:S(2)}) collective-permute-start(bf16[4096,512]{1,0:T(8,128)(2,1)} %refs_4_.5), channel_id=1, source_target_pairs={{0,1},{1,0},{2,3},{3,2},{4,5},{5,4},{6,7},{7,6},{8,9},{9,8},{10,11... | collective-permute-start | bytes 12582920 | tf_op jit(solution)/shard_map/ppermute | solution.py:27
  2.2 15.0 %collective-permute-start.2 = (bf16[256,256]{1,0:T(8,128)(2,1)S(1)}, bf16[256,256]{1,0:T(8,128)(2,1)S(1)}, u32[]{:S(2)}, u32[]{:S(2)}) collective-permute-start(bf16[256,256]{1,0:T(8,128)(2,1)S(1)} %constant_dynamic-update-slice_fusion), channel_id=1, source_target_pairs={{0,4},{4,8},{8,12},{12,16},{16,20},{20,24},{24,28},{28,0},{1,5},{5... | collective-permute-start | bytes 393224 | tf_op jit(solution)/shard_map/ppermute | solution.py:22
  4.7 16.2 %collective-permute-start.1 = (bf16[256,256]{1,0:T(8,128)(2,1)S(1)}, bf16[256,256]{1,0:T(8,128)(2,1)S(1)}, u32[]{:S(2)}, u32[]{:S(2)}) collective-permute-start(bf16[256,256]{1,0:T(8,128)(2,1)S(1)} %constant_dynamic-update-slice_fusion), channel_id=1, source_target_pairs={{0,8},{4,12},{8,16},{12,20},{16,24},{20,28},{24,0},{28,4},{1,9},{5... | collective-permute-start | bytes 393224 | tf_op jit(solution)/shard_map/ppermute | solution.py:22
  6.3 15.2 %collective-permute-start = (bf16[256,256]{1,0:T(8,128)(2,1)S(1)}, bf16[256,256]{1,0:T(8,128)(2,1)S(1)}, u32[]{:S(2)}, u32[]{:S(2)}) collective-permute-start(bf16[256,256]{1,0:T(8,128)(2,1)S(1)} %constant_dynamic-update-slice_fusion), channel_id=1, source_target_pairs={{0,12},{4,16},{8,20},{12,24},{16,28},{20,0},{24,4},{28,8},{1,13},{... | collective-permute-start | bytes 393224 | tf_op jit(solution)/shard_map/ppermute | solution.py:22
  8.8 34.1 %collective-permute-start.9 = (bf16[4096,128]{1,0:T(8,128)(2,1)}, bf16[4096,128]{1,0:T(8,128)(2,1)}, u32[]{:S(2)}, u32[]{:S(2)}) collective-permute-start(bf16[4096,128]{1,0:T(8,128)(2,1)} %param.20), channel_id=1, source_target_pairs={{0,1},{1,0},{2,3},{3,2},{4,5},{5,4},{6,7},{7,6},{8,9},{9,8},{10,11... | collective-permute-start | bytes 3145736 | tf_op jit(solution)/shard_map/ppermute | solution.py:27
  9.7 1.0 %copy-start.4 = (bf16[256,512]{1,0:T(8,128)(2,1)S(1)}, bf16[256,512]{1,0:T(8,128)(2,1)}, u32[]{:S(2)}) copy-start(bf16[256,512]{1,0:T(8,128)(2,1)} %query_ref.7) | copy-start | bytes 786436
  10.6 0.9 %copy-start.6 = (bf16[256,512]{1,0:T(8,128)(2,1)S(1)}, bf16[256,512]{1,0:T(8,128)(2,1)}, u32[]{:S(2)}) copy-start(bf16[256,512]{1,0:T(8,128)(2,1)} %grad_ref.7) | copy-start | bytes 786436
  11.6 0.9 %copy-start.8 = (bf16[256,512]{1,0:T(8,128)(2,1)S(1)}, bf16[256,512]{1,0:T(8,128)(2,1)}, u32[]{:S(2)}) copy-start(bf16[256,512]{1,0:T(8,128)(2,1)} %output_ref.1) | copy-start | bytes 786436
  12.5 0.8 %copy-start.9 = (bf16[256,128]{1,0:T(8,128)(2,1)S(1)}, bf16[256,128]{1,0:T(8,128)(2,1)}, u32[]{:S(2)}) copy-start(bf16[256,128]{1,0:T(8,128)(2,1)} %key_ref.1) | copy-start | bytes 196612
  13.4 0.8 %copy-start.10 = (bf16[256,128]{1,0:T(8,128)(2,1)S(1)}, bf16[256,128]{1,0:T(8,128)(2,1)}, u32[]{:S(2)}) copy-start(bf16[256,128]{1,0:T(8,128)(2,1)} %value_ref.1) | copy-start | bytes 196612
  14.2 0.7 %copy-start.11 = (s32[2]{0:T(128)S(1)}, s32[2]{0:T(128)}, u32[]{:S(2)}) copy-start(s32[2]{0:T(128)} %counter_ref.7) | copy-start | bytes 28
  14.9 11.2 %copy-start.13 = (bf16[4096,128]{1,0:T(8,128)(2,1)S(1)}, bf16[4096,128]{1,0:T(8,128)(2,1)}, u32[]{:S(2)}) copy-start(bf16[4096,128]{1,0:T(8,128)(2,1)} %param.20) | copy-start | bytes 3145732
  17.2 27.3 %collective-permute-start.10 = (bf16[4096,128]{1,0:T(8,128)(2,1)}, bf16[4096,128]{1,0:T(8,128)(2,1)}, u32[]{:S(2)}, u32[]{:S(2)}) collective-permute-start(bf16[4096,128]{1,0:T(8,128)(2,1)} %param.21), channel_id=1, source_target_pairs={{0,1},{1,0},{2,3},{3,2},{4,5},{5,4},{6,7},{7,6},{8,9},{9,8},{10,11... | collective-permute-start | bytes 3145736 | tf_op jit(solution)/shard_map/ppermute | solution.py:27
  17.7 0.9 %copy-start.5 = (bf16[256,512]{1,0:T(8,128)(2,1)S(1)}, bf16[256,512]{1,0:T(8,128)(2,1)}, u32[]{:S(2)}) copy-start(bf16[256,512]{1,0:T(8,128)(2,1)} %query_ref.7) | copy-start | bytes 786436
  18.7 0.9 %copy-start.7 = (bf16[256,512]{1,0:T(8,128)(2,1)S(1)}, bf16[256,512]{1,0:T(8,128)(2,1)}, u32[]{:S(2)}) copy-start(bf16[256,512]{1,0:T(8,128)(2,1)} %grad_ref.7) | copy-start | bytes 786436
  19.6 0.7 %copy-start.12 = (s32[1,4]{1,0:T(1,128)S(1)}, s32[1,4]{1,0:T(1,128)}, u32[]{:S(2)}) copy-start(s32[1,4]{1,0:T(1,128)} %mask_ref.5) | copy-start | bytes 52
  20.9 18.9 %copy-start.14 = (bf16[4096,128]{1,0:T(8,128)(2,1)S(1)}, bf16[4096,128]{1,0:T(8,128)(2,1)}, u32[]{:S(2)}) copy-start(bf16[4096,128]{1,0:T(8,128)(2,1)} %param.21) | copy-start | bytes 3145732
  22.3 6.9 %collective-permute-start.6 = (bf16[256,256]{1,0:T(8,128)(2,1)S(1)}, bf16[256,256]{1,0:T(8,128)(2,1)S(1)}, u32[]{:S(2)}, u32[]{:S(2)}) collective-permute-start(bf16[256,256]{1,0:T(8,128)(2,1)S(1)} %get-tuple-element.22), channel_id=1, source_target_pairs={{0,20},{4,24},{8,28},{12,0},{16,4},{20,8},{24,12},{28,16},{1,21},{... | collective-permute-start | bytes 393224 | tf_op jit(solution)/shard_map/ppermute | solution.py:22
  26.3 13.8 %collective-permute-start.5 = (bf16[256,256]{1,0:T(8,128)(2,1)S(1)}, bf16[256,256]{1,0:T(8,128)(2,1)S(1)}, u32[]{:S(2)}, u32[]{:S(2)}) collective-permute-start(bf16[256,256]{1,0:T(8,128)(2,1)S(1)} %get-tuple-element.21), channel_id=1, source_target_pairs={{0,24},{4,28},{8,0},{12,4},{16,8},{20,12},{24,16},{28,20},{1,25},{... | collective-permute-start | bytes 393224 | tf_op jit(solution)/shard_map/ppermute | solution.py:22
  29.2 13.5 %collective-permute-start.4 = (bf16[256,256]{1,0:T(8,128)(2,1)S(1)}, bf16[256,256]{1,0:T(8,128)(2,1)S(1)}, u32[]{:S(2)}, u32[]{:S(2)}) collective-permute-start(bf16[256,256]{1,0:T(8,128)(2,1)S(1)} %get-tuple-element.20), channel_id=1, source_target_pairs={{0,28},{4,0},{8,4},{12,8},{16,12},{20,16},{24,20},{28,24},{1,29},{... | collective-permute-start | bytes 393224 | tf_op jit(solution)/shard_map/ppermute | solution.py:22
  40.1 5.9 %collective-permute-start.3 = (bf16[256,512]{1,0:T(8,128)(2,1)S(1)}, bf16[256,512]{1,0:T(8,128)(2,1)S(1)}, u32[]{:S(2)}, u32[]{:S(2)}) collective-permute-start(bf16[256,512]{1,0:T(8,128)(2,1)S(1)} %get-tuple-element.18.refs_0_), channel_id=1, source_target_pairs={{0,1},{1,0},{2,3},{3,2},{4,5},{5,4},{6,7},{7,6},{8,9},{9,8},{10,11... | collective-permute-start | bytes 786440 | tf_op jit(solution)/shard_map/ppermute | solution.py:27
  42.8 3.2 %copy-start = (bf16[4096,512]{1,0:T(8,128)(2,1)S(1)}, bf16[4096,512]{1,0:T(8,128)(2,1)}, u32[]{:S(2)}) copy-start(bf16[4096,512]{1,0:T(8,128)(2,1)} %refs_4_.5) | copy-start | bytes 12582916
  42.8 3.1 %collective-permute-start.7 = (bf16[256,256]{1,0:T(8,128)(2,1)S(1)}, bf16[256,256]{1,0:T(8,128)(2,1)S(1)}, u32[]{:S(2)}, u32[]{:S(2)}) collective-permute-start(bf16[256,256]{1,0:T(8,128)(2,1)S(1)} %add_convert_fusion.1.refs_2_), channel_id=1, source_target_pairs={{0,1},{1,0},{2,3},{3,2},{4,5},{5,4},{6,7},{7,6},{8,9},{9,8},{10,11... | collective-permute-start | bytes 393224 | tf_op jit(solution)/shard_map/ppermute | solution.py:27
  46.0 3.7 %copy-start.2 = (bf16[4096,256]{1,0:T(8,128)(2,1)}, bf16[4096,256]{1,0:T(8,128)(2,1)S(1)}, u32[]{:S(2)}) copy-start(bf16[4096,256]{1,0:T(8,128)(2,1)S(1)} %constant_dynamic-update-slice_fusion.4.refs_7_) | copy-start | bytes 6291460
  48.1 11.0 %collective-permute-start.11 = (bf16[256,512]{1,0:T(8,128)(2,1)S(1)}, bf16[256,512]{1,0:T(8,128)(2,1)}, u32[]{:S(2)}, u32[]{:S(2)}) collective-permute-start(bf16[256,512]{1,0:T(8,128)(2,1)S(1)} %project.4), channel_id=1, source_target_pairs={{0,2},{1,3},{2,0},{3,1},{4,6},{5,7},{6,4},{7,5},{8,10},{9,11},{10,... | collective-permute-start | bytes 786440 | tf_op jit(solution)/shard_map/ppermute | solution.py:22
  51.5 10.9 %collective-permute-start.12 = (bf16[256,512]{1,0:T(8,128)(2,1)S(1)}, bf16[256,512]{1,0:T(8,128)(2,1)}, u32[]{:S(2)}, u32[]{:S(2)}) collective-permute-start(bf16[256,512]{1,0:T(8,128)(2,1)S(1)} %project.5), channel_id=1, source_target_pairs={{0,2},{1,3},{2,0},{3,1},{4,6},{5,7},{6,4},{7,5},{8,10},{9,11},{10,... | collective-permute-start | bytes 786440 | tf_op jit(solution)/shard_map/ppermute | solution.py:22
  52.1 2.2 %copy-start.1 = (bf16[4096,512]{1,0:T(8,128)(2,1)S(1)}, bf16[4096,512]{1,0:T(8,128)(2,1)}, u32[]{:S(2)}) copy-start(bf16[4096,512]{1,0:T(8,128)(2,1)} %refs_4_.5) | copy-start | bytes 12582916
  54.3 1.6 %copy-start.3 = (bf16[4096,256]{1,0:T(8,128)(2,1)S(1)}, bf16[4096,256]{1,0:T(8,128)(2,1)}, u32[]{:S(2)}) copy-start(bf16[4096,256]{1,0:T(8,128)(2,1)} %copy-done.2) | copy-start | bytes 6291460

commit v2 on v1

v2 whole, which is shorter than its diff:
```python
import functools
import math

import jax
import jax.numpy as jnp
from jax import lax
from jax.experimental import pallas as pl
from jax.experimental.pallas import tpu as pltpu
from jax.sharding import PartitionSpec as P

keep_level = 103
keep_scale = 1024.0 / 921.0
log2_e = math.log2(math.e)
f32, bf16, i32 = jnp.float32, jnp.bfloat16, jnp.int32
in_vmem = pl.BlockSpec(memory_space=pltpu.VMEM)
in_hbm = pl.BlockSpec(memory_space=pltpu.HBM)
in_smem = pl.BlockSpec(memory_space=pltpu.SMEM)


def from_hbm(array):
    return pltpu.with_memory_space_constraint(array, pltpu.HBM)


def cyclic(array, axis, by):
    count = lax.axis_size(axis)
    return lax.ppermute(array, axis, [(i, (i + by) % count) for i in range(count)])


def other_core(array):
    count = lax.axis_size("tp")
    return lax.ppermute(array, "tp", [(i, i ^ 1) for i in range(count)])


def dot(left, right, left_dim, right_dim):
    return lax.dot_general(
        left, right, (((left_dim,), (right_dim,)), ((), ())), preferred_element_type=f32
    )


def keep_mask(mixed):
    mixed = mixed ^ lax.shift_right_logical(mixed, i32(15))
    mixed = mixed * i32(739982445)
    mixed = mixed ^ lax.shift_right_logical(mixed, i32(12))
    mixed = mixed * i32(695872825)
    mixed = mixed ^ lax.shift_right_logical(mixed, i32(15))
    return (mixed & i32(1023)) >= i32(keep_level)


def block_grads(offset, window, heads, key, value, query_ref, grad_ref, mix_ref, norm_ref, delta_ref):
    rows, width = key.shape
    key_index = lax.broadcasted_iota(i32, (rows, rows), 0)
    query_index = lax.broadcasted_iota(i32, (rows, rows), 1)
    key_part = (key_index - offset * rows) * i32(19349663)
    key_t = key.T
    scale = log2_e * width**-0.5
    key_sum = value_sum = None
    query_parts = []
    for head in range(heads):
        cols = pl.ds(head * width, width)
        query, grad = query_ref[:, cols], grad_ref[:, cols]
        log_norm = norm_ref[pl.ds(offset * heads + head, 1), :]
        row_delta = delta_ref[pl.ds(head, 1), :]
        kept = keep_mask(key_part + mix_ref[pl.ds(head, 1), :])
        probs = jnp.exp2(dot(key, query, 1, 1) * scale - log_norm)
        spacing = query_index - key_index
        if offset == 0:
            probs = jnp.where(spacing >= 0, probs, f32(0.0))
        if (offset + 1) * rows > window:
            probs = jnp.where(spacing < window - offset * rows, probs, f32(0.0))
        dropped = jnp.where(kept, probs, f32(0.0)).astype(bf16)
        grad_probs = dot(value, grad, 1, 1)
        grad_scores = (
            probs * (jnp.where(kept, grad_probs, f32(0.0)) - row_delta)
        ).astype(bf16)
        value_add = dot(dropped, grad, 1, 0)
        key_add = dot(grad_scores, query, 1, 0)
        key_sum = key_add if head == 0 else key_sum + key_add
        value_sum = value_add if head == 0 else value_sum + value_add
        query_parts.append(dot(key_t, grad_scores, 1, 0))
    return key_sum, value_sum, query_parts


def load_kernel(
    heads, key_hbm, value_hbm, query_hbm, grad_hbm, output_hbm, norm_hbm, counter_hbm, mask_hbm,
    key_value, query, grad, output, mix_ref, rows_ref, norm_ref, counter_ref, mask_ref, sems,
):
    rows = key_hbm.shape[0]
    copies = [
        pltpu.make_async_copy(source, target, sems.at[i])
        for i, (source, target) in enumerate(
            (
                (key_hbm, key_value.at[pl.ds(0, rows)]),
                (value_hbm, key_value.at[pl.ds(rows, rows)]),
                (counter_hbm, counter_ref),
                (mask_hbm, mask_ref),
                (norm_hbm, norm_ref),
                (query_hbm, query),
                (grad_hbm, grad),
                (output_hbm, output),
            )
        )
    ]
    for copy in copies:
        copy.start()
    for copy in copies:
        copy.wait()
    block_id = lax.axis_index("ctx")
    first_head = lax.axis_index("tp") * heads
    base = counter_ref[1] + block_id * rows
    common = base * i32(19349663) + counter_ref[0]
    query_pos = lax.broadcasted_iota(i32, (1, rows), 1) + base
    for head in range(heads):
        mix_ref[pl.ds(head, 1), :] = query_pos * i32(73856093) + (
            common + (first_head + head) * i32(83492791)
        )
    norms = norm_ref[...] * f32(log2_e)
    for offset in range(mask_ref.shape[1]):
        active = (block_id >= offset) & (mask_ref[0, offset] == 1)
        rows_ref[pl.ds(offset * heads, heads), :] = jnp.where(active, norms, f32(jnp.inf))


def own_kernel(
    window, heads, key_value_ref, query_ref, grad_ref, output_ref, mix_ref, norm_ref, delta_ref,
    total_ref, sums_ref,
):
    rows, width = key_value_ref.shape[0] // 2, key_value_ref.shape[1]
    lane = lax.broadcasted_iota(i32, (rows, 128), 1)
    packed = jnp.zeros((rows, 128), f32)
    for head in range(heads):
        cols = pl.ds(head * width, width)
        delta = jnp.sum(
            grad_ref[:, cols].astype(f32) * output_ref[:, cols].astype(f32), axis=1, keepdims=True
        )
        packed = jnp.where(lane == head, delta * f32(1.0 / keep_scale), packed)
    delta_ref[...] = packed.T[: delta_ref.shape[0]]
    key_sum, value_sum, query_parts = block_grads(
        0, window, heads, key_value_ref[:rows], key_value_ref[rows:], query_ref, grad_ref, mix_ref,
        norm_ref, delta_ref,
    )
    grad_scale = keep_scale * width**-0.5
    sums_ref[:rows] = key_sum * f32(grad_scale)
    sums_ref[rows:] = value_sum * f32(keep_scale)
    for head, part in enumerate(query_parts):
        total_ref[:, pl.ds(head * rows, rows)] = part


def pair_kernel(
    offset, window, heads, last, key_value_ref, query_ref, grad_ref, mix_ref, norm_ref, delta_ref,
    before_ref, total_ref, sums_ref,
):
    rows, width = key_value_ref.shape[0] // 2, key_value_ref.shape[1]
    grad_scale = keep_scale * width**-0.5
    key_sum, value_sum, query_parts = block_grads(
        offset, window, heads, key_value_ref[:rows], key_value_ref[rows:], query_ref, grad_ref,
        mix_ref, norm_ref, delta_ref,
    )
    sums_ref[:rows] = (key_sum * f32(grad_scale)).astype(bf16)
    sums_ref[rows:] = (value_sum * f32(keep_scale)).astype(bf16)
    for head, part in enumerate(query_parts):
        cols = pl.ds(head * rows, rows)
        if last:
            total_ref[:, pl.ds(head * width, width)] = (
                (before_ref[:, cols] + part).T * f32(grad_scale)
            ).astype(bf16)
        else:
            total_ref[:, cols] = before_ref[:, cols] + part


def project_kernel(hop, flip, start, added, query_ref, sums_ref, wq_ref, wk_ref, wv_ref, *refs):
    count = lax.axis_size("tp")
    me = lax.axis_index("tp")
    if flip:
        me = me + 1 - 2 * lax.rem(me, 2)
    out_ref = refs[-1]
    rows, cols = out_ref.shape
    first = lax.rem(me + hop, count) * (wq_ref.shape[0] // count) + start
    at = pl.ds(pl.multiple_of(first, 128), cols)
    total = dot(query_ref[...], wq_ref[at, :], 1, 1)
    total = total + dot(sums_ref[:rows], wk_ref[at, :], 1, 1)
    total = total + dot(sums_ref[rows:], wv_ref[at, :], 1, 1)
    for ref in refs[:added]:
        total = total + ref[...].astype(f32)
    out_ref[...] = total.astype(out_ref.dtype)


def project(hop, flip, start, cols, operands, added, after, dtype, params):
    rows, depth = operands[0].shape[0], sum(item.shape[1] for item in operands[2:])
    return pl.pallas_call(
        functools.partial(project_kernel, hop, flip, start, len(added)),
        in_specs=[in_vmem] * (len(operands) + len(added) + len(after)),
        out_specs=in_vmem,
        out_shape=jax.ShapeDtypeStruct((rows, cols), dtype),
        compiler_params=params,
        cost_estimate=cost(2 * rows * cols * depth),
        name="project",
    )(*operands, *added, *after)


def add_kernel(left_ref, right_ref, out_ref):
    out_ref[...] = (left_ref[...] + right_ref[...].astype(f32)).astype(out_ref.dtype)


def finish_kernel(first, hops, mine_ref, *refs):
    out_hbm, held, sem = refs[-3:]
    at = pl.ds(first, held.shape[1])
    total = mine_ref[:, at]
    for ref in refs[:hops]:
        total = total + ref[...].astype(f32)
    held[...] = total.astype(bf16)
    copy = pltpu.make_async_copy(held, out_hbm.at[:, at], sem)
    copy.start()
    copy.wait()


def cost(flops):
    return pl.CostEstimate(flops=flops, bytes_accessed=flops // 400, transcendentals=0)


def on_device(
    queries,
    keys,
    values,
    outputs,
    out_grad,
    log_norm,
    block_mask,
    counter_base,
    q_weight,
    k_weight,
    v_weight,
):
    rows, width = keys.shape
    heads = log_norm.shape[1]
    steps = block_mask.shape[1]
    window = 3 * rows + rows // 2
    tp_size = lax.axis_size("tp")
    params = pltpu.CompilerParams(vmem_limit_bytes=16 * 2**20)

    shape = jax.ShapeDtypeStruct
    key_value, query, grad, output, mix, norms = pl.pallas_call(
        functools.partial(load_kernel, heads),
        in_specs=[in_hbm] * 8,
        out_specs=[in_vmem] * 6,
        out_shape=[
            shape((2 * rows, width), bf16),
            *[shape(queries.shape, bf16)] * 3,
            shape((heads, rows), i32),
            shape((steps * heads, rows), f32),
        ],
        scratch_shapes=[
            pltpu.VMEM((heads, rows), f32),
            pltpu.SMEM(counter_base.shape, i32),
            pltpu.SMEM(block_mask.shape, i32),
            pltpu.SemaphoreType.DMA((8,)),
        ],
        compiler_params=params,
        cost_estimate=pl.CostEstimate(flops=0, bytes_accessed=0, transcendentals=0),
        name="load",
    )(*map(from_hbm, (keys, values, queries, out_grad, outputs, log_norm.T, counter_base, block_mask)))
    order = range(steps - 1, 0, -1)
    arrived = {offset: cyclic(key_value, "ctx", offset) for offset in order}
    block_cost = cost(20 * heads * rows * rows * width)

    deltas, total, own_sums = pl.pallas_call(
        functools.partial(own_kernel, window, heads),
        in_specs=[in_vmem] * 6,
        out_specs=[in_vmem] * 3,
        out_shape=[
            shape((heads, rows), f32),
            shape((width, heads * rows), f32),
            shape((2 * rows, width), f32),
        ],
        compiler_params=params,
        cost_estimate=block_cost,
        name="own_block",
    )(key_value, query, grad, output, mix, norms)

    returned = []
    for offset in order:
        last = offset == order[-1]
        total, sums = pl.pallas_call(
            functools.partial(pair_kernel, offset, window, heads, last),
            in_specs=[in_vmem] * 7,
            out_specs=[in_vmem] * 2,
            out_shape=[
                shape((rows, heads * width), bf16) if last else shape((width, heads * rows), f32),
                shape((2 * rows, width), bf16),
            ],
            compiler_params=params,
            cost_estimate=block_cost,
            name="block_back_%d" % offset,
        )(arrived[offset], query, grad, mix, norms, deltas, total)
        returned.append(cyclic(sums, "ctx", -offset))
    grad_query = total
    sums = own_sums
    for item in returned:
        sums = pl.pallas_call(
            add_kernel,
            in_specs=[in_vmem] * 2,
            out_specs=in_vmem,
            out_shape=shape(sums.shape, bf16 if item is returned[-1] else f32),
            compiler_params=params,
            cost_estimate=block_cost,
            name="add_returned",
        )(sums, item)
    operands = (grad_query, sums, q_weight, k_weight, v_weight)
    cols = q_weight.shape[0] // tp_size
    sizes = [cols // 2] * 2
    starts = [sum(sizes[:i]) for i in range(len(sizes))]
    hops = tp_size // 2 - 1
    places = [(i, hop) for i in range(len(sizes)) for hop in range(2, tp_size, 2)]
    swapped, terms, after = [], [], ()
    for i, hop in places:
        part = project(hop, True, starts[i], sizes[i], operands, (), after, bf16, params)
        swapped.append(other_core(part))
        after = (part,)
    for (i, hop), item in zip(places, swapped):
        part = project(hop, False, starts[i], sizes[i], operands, (item,), after, bf16, params)
        terms.append(part)
        after = (part,)
        if len(terms) == 1:
            part = project(0, True, 0, cols, operands, (), after, bf16, params)
            other = other_core(part)
            after = (part,)
    sent = [cyclic(term, "tp", hop) for (_, hop), term in zip(places, terms)]
    mine = project(0, False, 0, cols, operands, (other,), tuple(sent[:1]), f32, params)
    out = ()
    for i, size in enumerate(sizes):
        out = pl.pallas_call(
            functools.partial(finish_kernel, starts[i], hops),
            in_specs=[in_vmem] * (1 + hops) + [in_hbm] * len(out),
            out_specs=in_hbm,
            out_shape=shape((rows, cols), bf16),
            input_output_aliases={1 + hops: 0} if out else {},
            scratch_shapes=[pltpu.VMEM((rows, size), bf16), pltpu.SemaphoreType.DMA],
            compiler_params=params,
            cost_estimate=cost(10**6),
            name="finish",
        )(mine, *sent[i * hops : (i + 1) * hops], *out)
        out = (out,)
    return out[0]


def solution(mesh):
    return jax.shard_map(
        on_device,
        mesh=mesh,
        in_specs=(
            P("ctx", "tp"),
            P("ctx", "tp"),
            P("ctx", "tp"),
            P("ctx", "tp"),
            P("ctx", "tp"),
            P("ctx", "tp"),
            P("ctx", None),
            P(),
            P(None, "tp"),
            P(None, "tp"),
            P(None, "tp"),
        ),
        out_specs=P("ctx", "tp"),
        check_vma=False,
    )
```

time: 64.3 us -> 47.2 us (0.73)
  waiting for transfers between devices: 6.57 us -> 24.1 us
  local copies, waits for them, and re-layouts: 17.5 us -> 0.02 us
  starting transfers between devices: 26.7 us -> 11.3 us
  other arithmetic: 2.06 us -> 0 us
    ppermute x8, waiting for transfers between devices: 6.55 us -> 22.4 us  [cyclic(): lax.ppermute(array, axis, [(i, (i + by) % count) for i in range(count)])]
    unnamed x34 -> x6, local copies, waits for them, and re-layouts: 14.9 us -> 0.02 us
    ppermute x8, starting transfers between devices: 25.5 us -> 10.6 us  [cyclic(): lax.ppermute(array, axis, [(i, (i + by) % count) for i in range(count)])]
    concatenate x3 -> x0, local copies, waits for them, and re-layouts: 2.58 us -> none  [the longest x2 1.72 us: on_device(): jnp.concatenate([pair[0], pair[1]], axis=1)]
    convert_element_type x2 -> x0, other arithmetic: 2.06 us -> none  [the longest x1 2.01 us: on_device(): return mine.astype(bf16)]
    pallas_call x3, Pallas kernels: 1.96 us -> 3.97 us  [on_device(): pl.pallas_call(functools.partial(pair_kernel, offset, window, heads, last...]
    ppermute x5 -> x3, waiting for transfers between devices: 0.01 us -> 1.7 us  [other_core(): return lax.ppermute(array, 'tp', [(i, i ^ 1) for i in range(count)])]
    pallas_call x3 -> x12, Pallas kernels: 7.14 us -> 6.07 us  [the longest x6 3.19 us: project(): pl.pallas_call(functools.partial(project_kernel, hop, flip, start, len(ad...]
  transfers between devices with their start and end apart: 13 -> 11, of which waited for: 3 -> 8; matrix products, arithmetic and copies ran while one was open for 9% -> 0% of each run, Pallas kernels for 14% -> 17%
where the time goes in v2:
time: 47.2 us; the launch traced here: 47 us
  waiting for transfers between devices  24.1 us (51%)
  Pallas kernels  11.5 us (24%)
  starting transfers between devices  11.3 us (24%)
    ppermute x8, waiting for transfers between devices, cyclic(): lax.ppermute(array, axis, [(i, (i + by) % count) for i in range(count)])  22.4 us
    ppermute x8, starting transfers between devices, cyclic(): lax.ppermute(array, axis, [(i, (i + by) % count) for i in range(count)])  10.6 us
    pallas_call x3, Pallas kernels, on_device(): pl.pallas_call(functools.partial(pair_kernel, offset, window, heads, last...  3.97 us
    pallas_call x6, Pallas kernels, project(): pl.pallas_call(functools.partial(project_kernel, hop, flip, start, len(ad...  3.19 us
    ppermute x3, waiting for transfers between devices, other_core(): return lax.ppermute(array, 'tp', [(i, i ^ 1) for i in range(count)])  1.7 us
    pallas_call x2, Pallas kernels, on_device(): pl.pallas_call(functools.partial(finish_kernel, starts[i], hops), in_spec...  1.51 us
    pallas_call x1, Pallas kernels, on_device(): pl.pallas_call(functools.partial(own_kernel, window, heads), in_specs=[in...  1.43 us
    pallas_call x1, Pallas kernels, on_device(): pl.pallas_call(functools.partial(load_kernel, heads), in_specs=[in_hbm] *...  1.29 us
  transfers between devices with their start and end apart: 11, of which 8 were waited for; matrix products, arithmetic and copies ran while one was open for 0% of the time, Pallas kernels for 17%

profile of v2, /device:TPU:0, one launch (start us, length us, event | category | flops | bytes accessed | tf_op | source)
XLA Modules:
  0.0 47.0 jit_solution(2521304289789010337)
XLA Ops:
  0.0 1.3 %load.1 = (bf16[512,128]{1,0:T(8,128)(2,1)S(1)}, bf16[256,512]{1,0:T(8,128)(2,1)S(1)}, bf16[256,512]{1,0:T(8,128)(2,1)S(1)}, bf16[256,512]{1,0:T(8,128)(2,1)S(1)...) custom-call(bf16[256,128]{1,0:T(8,128)(2,1)} %key_hbm.1, bf16[256,128]{1,0:T(8,128)(2,1)} %value_hbm.1, ...), custom_call_target="tpu_custom_call" | custom-call | tf_op jit(solution)/shard_map/load/pallas_call | solution.py:240
  1.3 4.0 %collective-permute-start.2 = (bf16[512,128]{1,0:T(8,128)(2,1)S(1)}, bf16[512,128]{1,0:T(8,128)(2,1)S(1)}, u32[]{:S(2)}, u32[]{:S(2)}) collective-permute-start(bf16[512,128]{1,0:T(8,128)(2,1)S(1)} %get-tuple-element.20.key_value_ref), channel_id=1, source_target_pairs={{0,12},{4,16},{8,20},{12,24},{16,28},{20,0},{24,4},{28,8},{1,13},{... | collective-permute-start | bytes 393224 | tf_op jit(solution)/shard_map/ppermute | solution.py:26
  5.3 1.6 %collective-permute-start.1 = (bf16[512,128]{1,0:T(8,128)(2,1)S(1)}, bf16[512,128]{1,0:T(8,128)(2,1)S(1)}, u32[]{:S(2)}, u32[]{:S(2)}) collective-permute-start(bf16[512,128]{1,0:T(8,128)(2,1)S(1)} %get-tuple-element.20.key_value_ref), channel_id=1, source_target_pairs={{0,8},{4,12},{8,16},{12,20},{16,24},{20,28},{24,0},{28,4},{1,9},{5... | collective-permute-start | bytes 393224 | tf_op jit(solution)/shard_map/ppermute | solution.py:26
  6.9 1.5 %collective-permute-start = (bf16[512,128]{1,0:T(8,128)(2,1)S(1)}, bf16[512,128]{1,0:T(8,128)(2,1)S(1)}, u32[]{:S(2)}, u32[]{:S(2)}) collective-permute-start(bf16[512,128]{1,0:T(8,128)(2,1)S(1)} %get-tuple-element.20.key_value_ref), channel_id=1, source_target_pairs={{0,4},{4,8},{8,12},{12,16},{16,20},{20,24},{24,28},{28,0},{1,5},{5... | collective-permute-start | bytes 393224 | tf_op jit(solution)/shard_map/ppermute | solution.py:26
  8.4 1.4 %own_block.1 = (f32[4,256]{1,0:T(4,128)S(1)}, f32[128,1024]{1,0:T(8,128)S(1)}, f32[512,128]{1,0:T(8,128)S(1)}) custom-call(bf16[512,128]{1,0:T(8,128)(2,1)S(1)} %get-tuple-element.20.key_value_ref, bf16[256,512]{1,0:T(8,128)(2,1)S(1)} %get-tuple-element.21.query_ref, bf16[256,512]{1,0:T(8,128)(2,1)S(1)} %get-tuple-element.22.grad_ref, ...), custom_call_target="tpu_custom_call" | custom-call | flops 671088640 | bytes 1677721 | tf_op jit(solution)/shard_map/own_block/pallas_call | solution.py:264
  9.9 8.4 %collective-permute-done.2.key_value_ref = bf16[512,128]{1,0:T(8,128)(2,1)S(1)} collective-permute-done((bf16[512,128]{1,0:T(8,128)(2,1)S(1)}, bf16[512,128]{1,0:T(8,128)(2,1)S(1)}, u32[]{:S(2)}, u32[]{:S(2)}) %collective-permute-start.2) | collective-permute-done | bytes 131104 | tf_op jit(solution)/shard_map/ppermute | solution.py:26
  18.2 1.3 %block_back_3.1 = (f32[128,1024]{1,0:T(8,128)S(1)}, bf16[512,128]{1,0:T(8,128)(2,1)S(1)}) custom-call(bf16[512,128]{1,0:T(8,128)(2,1)S(1)} %collective-permute-done.2.key_value_ref, bf16[256,512]{1,0:T(8,128)(2,1)S(1)} %get-tuple-element.21.query_ref, bf16[256,512]{1,0:T(8,128)(2,1)S(1)} %get-tuple-element.22.grad_ref, ...), custom_call_target="tpu_custom_call" | custom-call | flops 671088640 | bytes 1677721 | tf_op jit(solution)/shard_map/block_back_3/pallas_call | solution.py:281
  19.5 0.1 collective-permute-start.3
  19.6 1.3 %block_back_2.1 = (f32[128,1024]{1,0:T(8,128)S(1)}, bf16[512,128]{1,0:T(8,128)(2,1)S(1)}) custom-call(bf16[512,128]{1,0:T(8,128)(2,1)S(1)} %collective-permute-done.1.key_value_ref, bf16[256,512]{1,0:T(8,128)(2,1)S(1)} %get-tuple-element.21.query_ref, bf16[256,512]{1,0:T(8,128)(2,1)S(1)} %get-tuple-element.22.grad_ref, ...), custom_call_target="tpu_custom_call" | custom-call | flops 671088640 | bytes 1677721 | tf_op jit(solution)/shard_map/block_back_2/pallas_call | solution.py:281
  20.9 0.1 collective-permute-start.4
  21.0 1.4 %block_back_1.1 = (bf16[256,512]{1,0:T(8,128)(2,1)S(1)}, bf16[512,128]{1,0:T(8,128)(2,1)S(1)}) custom-call(bf16[512,128]{1,0:T(8,128)(2,1)S(1)} %collective-permute-done.key_value_ref, bf16[256,512]{1,0:T(8,128)(2,1)S(1)} %get-tuple-element.21.query_ref, bf16[256,512]{1,0:T(8,128)(2,1)S(1)} %get-tuple-element.22.grad_ref, ...), custom_call_target="tpu_custom_call" | custom-call | flops 671088640 | bytes 1677721 | tf_op jit(solution)/shard_map/block_back_1/pallas_call | solution.py:281
  22.4 1.0 %collective-permute-start.5 = (bf16[512,128]{1,0:T(8,128)(2,1)S(1)}, bf16[512,128]{1,0:T(8,128)(2,1)S(1)}, u32[]{:S(2)}, u32[]{:S(2)}) collective-permute-start(bf16[512,128]{1,0:T(8,128)(2,1)S(1)} %get-tuple-element.34), channel_id=1, source_target_pairs={{0,28},{4,0},{8,4},{12,8},{16,12},{20,16},{24,20},{28,24},{1,29},{... | collective-permute-start | bytes 393224 | tf_op jit(solution)/shard_map/ppermute | solution.py:26
  23.4 3.2 %collective-permute-done.3.right_ref = bf16[512,128]{1,0:T(8,128)(2,1)S(1)} collective-permute-done((bf16[512,128]{1,0:T(8,128)(2,1)S(1)}, bf16[512,128]{1,0:T(8,128)(2,1)S(1)}, u32[]{:S(2)}, u32[]{:S(2)}) %collective-permute-start.3) | collective-permute-done | bytes 131104 | tf_op jit(solution)/shard_map/ppermute | solution.py:26
  26.7 0.6 %collective-permute-done.4.right_ref = bf16[512,128]{1,0:T(8,128)(2,1)S(1)} collective-permute-done((bf16[512,128]{1,0:T(8,128)(2,1)S(1)}, bf16[512,128]{1,0:T(8,128)(2,1)S(1)}, u32[]{:S(2)}, u32[]{:S(2)}) %collective-permute-start.4) | collective-permute-done | bytes 131104 | tf_op jit(solution)/shard_map/ppermute | solution.py:26
  27.3 1.1 %collective-permute-done.5.right_ref = bf16[512,128]{1,0:T(8,128)(2,1)S(1)} collective-permute-done((bf16[512,128]{1,0:T(8,128)(2,1)S(1)}, bf16[512,128]{1,0:T(8,128)(2,1)S(1)}, u32[]{:S(2)}, u32[]{:S(2)}) %collective-permute-start.5) | collective-permute-done | bytes 131104 | tf_op jit(solution)/shard_map/ppermute | solution.py:26
  28.5 0.5 project.6.refs_0_
  29.0 0.1 collective-permute-start.6
  29.0 0.5 project.7.refs_1_
  29.5 1.1 %collective-permute-done.6.refs_0_ = bf16[256,512]{1,0:T(8,128)(2,1)S(1)} collective-permute-done((bf16[256,512]{1,0:T(8,128)(2,1)S(1)}, bf16[256,512]{1,0:T(8,128)(2,1)S(1)}, u32[]{:S(2)}, u32[]{:S(2)}) %collective-permute-start.6) | collective-permute-done | bytes 262176 | tf_op jit(solution)/shard_map/ppermute | solution.py:31
  30.6 0.4 project.8.refs_0_
  31.0 0.7 %project.9.refs_1_ = bf16[256,1024]{1,0:T(8,128)(2,1)S(1)} custom-call(bf16[256,512]{1,0:T(8,128)(2,1)S(1)} %get-tuple-element.30.query_ref, bf16[512,128]{1,0:T(8,128)(2,1)S(1)} %add_returned.5.sums_ref, bf16[4096,512]{1,0:T(8,128)(2,1)S(1)} %copy-done, bf16[4096,128]{1,0:T(8,128)(2,1)S(1)} %copy-done.1, bf16[4096,128]{1,0:T(8,128)(2,1)S(1)} %copy-done.2, ...), custom_call_target="tpu_custom_call" | custom-call | flops 402653184 | bytes 1006632 | tf_op jit(solution)/shard_map/project/pallas_call | solution.py:188
  31.7 0.2 collective-permute-start.7
  31.9 0.4 collective-permute-start.9
  32.3 1.1 %collective-permute-start.8 = (bf16[256,512]{1,0:T(8,128)(2,1)S(1)}, bf16[256,512]{1,0:T(8,128)(2,1)S(1)}, u32[]{:S(2)}, u32[]{:S(2)}) collective-permute-start(bf16[256,512]{1,0:T(8,128)(2,1)S(1)} %project.8.refs_0_), channel_id=1, source_target_pairs={{0,2},{1,3},{2,0},{3,1},{4,6},{5,7},{6,4},{7,5},{8,10},{9,11},{10,... | collective-permute-start | bytes 786440 | tf_op jit(solution)/shard_map/ppermute | solution.py:26
  33.5 0.6 %collective-permute-done.9.refs_0_ = bf16[256,512]{1,0:T(8,128)(2,1)S(1)} collective-permute-done((bf16[256,512]{1,0:T(8,128)(2,1)S(1)}, bf16[256,512]{1,0:T(8,128)(2,1)S(1)}, u32[]{:S(2)}, u32[]{:S(2)}) %collective-permute-start.9) | collective-permute-done | bytes 262176 | tf_op jit(solution)/shard_map/ppermute | solution.py:31
  34.1 0.4 project.11
  34.5 1.2 %collective-permute-start.10 = (bf16[256,512]{1,0:T(8,128)(2,1)S(1)}, bf16[256,512]{1,0:T(8,128)(2,1)S(1)}, u32[]{:S(2)}, u32[]{:S(2)}) collective-permute-start(bf16[256,512]{1,0:T(8,128)(2,1)S(1)} %project.11), channel_id=1, source_target_pairs={{0,2},{1,3},{2,0},{3,1},{4,6},{5,7},{6,4},{7,5},{8,10},{9,11},{10,... | collective-permute-start | bytes 786440 | tf_op jit(solution)/shard_map/ppermute | solution.py:26
  35.7 5.7 %collective-permute-done.8.refs_1_.refs_0_ = bf16[256,512]{1,0:T(8,128)(2,1)S(1)} collective-permute-done((bf16[256,512]{1,0:T(8,128)(2,1)S(1)}, bf16[256,512]{1,0:T(8,128)(2,1)S(1)}, u32[]{:S(2)}, u32[]{:S(2)}) %collective-permute-start.8) | collective-permute-done | bytes 262176 | tf_op jit(solution)/shard_map/ppermute | solution.py:26
  41.5 0.7 %project.10.mine_ref = f32[256,1024]{1,0:T(8,128)S(1)} custom-call(bf16[256,512]{1,0:T(8,128)(2,1)S(1)} %get-tuple-element.30.query_ref, bf16[512,128]{1,0:T(8,128)(2,1)S(1)} %add_returned.5.sums_ref, bf16[4096,512]{1,0:T(8,128)(2,1)S(1)} %copy-done, bf16[4096,128]{1,0:T(8,128)(2,1)S(1)} %copy-done.1, bf16[4096,128]{1,0:T(8,128)(2,1)S(1)} %copy-done.2, ...), custom_call_target="tpu_custom_call" | custom-call | flops 402653184 | bytes 1006632 | tf_op jit(solution)/shard_map/project/pallas_call | solution.py:188
  42.2 0.8 %finish.2.refs_1_ = bf16[256,1024]{1,0:T(8,128)(2,1)} custom-call(f32[256,1024]{1,0:T(8,128)S(1)} %project.10.mine_ref, bf16[256,512]{1,0:T(8,128)(2,1)S(1)} %collective-permute-done.8.refs_1_.refs_0_), custom_call_target="tpu_custom_call" | custom-call | flops 1000000 | bytes 2500 | tf_op jit(solution)/shard_map/finish/pallas_call | solution.py:329
  42.9 3.3 %collective-permute-done.10.refs_0_ = bf16[256,512]{1,0:T(8,128)(2,1)S(1)} collective-permute-done((bf16[256,512]{1,0:T(8,128)(2,1)S(1)}, bf16[256,512]{1,0:T(8,128)(2,1)S(1)}, u32[]{:S(2)}, u32[]{:S(2)}) %collective-permute-start.10) | collective-permute-done | bytes 262176 | tf_op jit(solution)/shard_map/ppermute | solution.py:26
  46.3 0.8 %finish.3 = bf16[256,1024]{1,0:T(8,128)(2,1)} custom-call(f32[256,1024]{1,0:T(8,128)S(1)} %project.10.mine_ref, bf16[256,512]{1,0:T(8,128)(2,1)S(1)} %collective-permute-done.10.refs_0_, bf16[256,1024]{1,0:T(8,128)(2,1)} %finish.2.refs_1_), custom_call_target="tpu_custom_call", output_to_operand_aliasing={{}: (2, {})} | custom-call | flops 1000000 | bytes 2500 | tf_op jit(solution)/shard_map/finish/pallas_call | solution.py:329
  (12 shorter events, 0.1 us)
Async XLA Ops:
  1.3 16.9 %collective-permute-start.2 = (bf16[512,128]{1,0:T(8,128)(2,1)S(1)}, bf16[512,128]{1,0:T(8,128)(2,1)S(1)}, u32[]{:S(2)}, u32[]{:S(2)}) collective-permute-start(bf16[512,128]{1,0:T(8,128)(2,1)S(1)} %get-tuple-element.20.key_value_ref), channel_id=1, source_target_pairs={{0,12},{4,16},{8,20},{12,24},{16,28},{20,0},{24,4},{28,8},{1,13},{... | collective-permute-start | bytes 393224 | tf_op jit(solution)/shard_map/ppermute | solution.py:26
  5.3 14.3 %collective-permute-start.1 = (bf16[512,128]{1,0:T(8,128)(2,1)S(1)}, bf16[512,128]{1,0:T(8,128)(2,1)S(1)}, u32[]{:S(2)}, u32[]{:S(2)}) collective-permute-start(bf16[512,128]{1,0:T(8,128)(2,1)S(1)} %get-tuple-element.20.key_value_ref), channel_id=1, source_target_pairs={{0,8},{4,12},{8,16},{12,20},{16,24},{20,28},{24,0},{28,4},{1,9},{5... | collective-permute-start | bytes 393224 | tf_op jit(solution)/shard_map/ppermute | solution.py:26
  6.9 14.1 %collective-permute-start = (bf16[512,128]{1,0:T(8,128)(2,1)S(1)}, bf16[512,128]{1,0:T(8,128)(2,1)S(1)}, u32[]{:S(2)}, u32[]{:S(2)}) collective-permute-start(bf16[512,128]{1,0:T(8,128)(2,1)S(1)} %get-tuple-element.20.key_value_ref), channel_id=1, source_target_pairs={{0,4},{4,8},{8,12},{12,16},{16,20},{20,24},{24,28},{28,0},{1,5},{5... | collective-permute-start | bytes 393224 | tf_op jit(solution)/shard_map/ppermute | solution.py:26
  19.5 7.1 %collective-permute-start.3 = (bf16[512,128]{1,0:T(8,128)(2,1)S(1)}, bf16[512,128]{1,0:T(8,128)(2,1)S(1)}, u32[]{:S(2)}, u32[]{:S(2)}) collective-permute-start(bf16[512,128]{1,0:T(8,128)(2,1)S(1)} %get-tuple-element.32), channel_id=1, source_target_pairs={{0,20},{4,24},{8,28},{12,0},{16,4},{20,8},{24,12},{28,16},{1,21},{... | collective-permute-start | bytes 393224 | tf_op jit(solution)/shard_map/ppermute | solution.py:26
  20.9 6.4 %collective-permute-start.4 = (bf16[512,128]{1,0:T(8,128)(2,1)S(1)}, bf16[512,128]{1,0:T(8,128)(2,1)S(1)}, u32[]{:S(2)}, u32[]{:S(2)}) collective-permute-start(bf16[512,128]{1,0:T(8,128)(2,1)S(1)} %get-tuple-element.33), channel_id=1, source_target_pairs={{0,24},{4,28},{8,0},{12,4},{16,8},{20,12},{24,16},{28,20},{1,25},{... | collective-permute-start | bytes 393224 | tf_op jit(solution)/shard_map/ppermute | solution.py:26
  22.4 6.1 %copy-start = (bf16[4096,512]{1,0:T(8,128)(2,1)S(1)}, bf16[4096,512]{1,0:T(8,128)(2,1)}, u32[]{:S(2)}) copy-start(bf16[4096,512]{1,0:T(8,128)(2,1)} %wq_ref.11) | copy-start | bytes 12582916
  22.4 6.1 %copy-start.1 = (bf16[4096,128]{1,0:T(8,128)(2,1)S(1)}, bf16[4096,128]{1,0:T(8,128)(2,1)}, u32[]{:S(2)}) copy-start(bf16[4096,128]{1,0:T(8,128)(2,1)} %wk_ref.11) | copy-start | bytes 3145732
  22.4 6.1 %copy-start.2 = (bf16[4096,128]{1,0:T(8,128)(2,1)S(1)}, bf16[4096,128]{1,0:T(8,128)(2,1)}, u32[]{:S(2)}) copy-start(bf16[4096,128]{1,0:T(8,128)(2,1)} %wv_ref.11) | copy-start | bytes 3145732
  22.4 6.0 %collective-permute-start.5 = (bf16[512,128]{1,0:T(8,128)(2,1)S(1)}, bf16[512,128]{1,0:T(8,128)(2,1)S(1)}, u32[]{:S(2)}, u32[]{:S(2)}) collective-permute-start(bf16[512,128]{1,0:T(8,128)(2,1)S(1)} %get-tuple-element.34), channel_id=1, source_target_pairs={{0,28},{4,0},{8,4},{12,8},{16,12},{20,16},{24,20},{28,24},{1,29},{... | collective-permute-start | bytes 393224 | tf_op jit(solution)/shard_map/ppermute | solution.py:26
  29.0 1.6 %collective-permute-start.6 = (bf16[256,512]{1,0:T(8,128)(2,1)S(1)}, bf16[256,512]{1,0:T(8,128)(2,1)S(1)}, u32[]{:S(2)}, u32[]{:S(2)}) collective-permute-start(bf16[256,512]{1,0:T(8,128)(2,1)S(1)} %project.6.refs_0_), channel_id=1, source_target_pairs={{0,1},{1,0},{2,3},{3,2},{4,5},{5,4},{6,7},{7,6},{8,9},{9,8},{10,11... | collective-permute-start | bytes 786440 | tf_op jit(solution)/shard_map/ppermute | solution.py:31
  31.7 9.7 %collective-permute-start.7 = (bf16[256,1024]{1,0:T(8,128)(2,1)S(1)}, bf16[256,1024]{1,0:T(8,128)(2,1)S(1)}, u32[]{:S(2)}, u32[]{:S(2)}) collective-permute-start(bf16[256,1024]{1,0:T(8,128)(2,1)S(1)} %project.9.refs_1_), channel_id=1, source_target_pairs={{0,1},{1,0},{2,3},{3,2},{4,5},{5,4},{6,7},{7,6},{8,9},{9,8},{10,11... | collective-permute-start | bytes 1572872 | tf_op jit(solution)/shard_map/ppermute | solution.py:31
  31.9 2.1 %collective-permute-start.9 = (bf16[256,512]{1,0:T(8,128)(2,1)S(1)}, bf16[256,512]{1,0:T(8,128)(2,1)S(1)}, u32[]{:S(2)}, u32[]{:S(2)}) collective-permute-start(bf16[256,512]{1,0:T(8,128)(2,1)S(1)} %project.7.refs_1_), channel_id=1, source_target_pairs={{0,1},{1,0},{2,3},{3,2},{4,5},{5,4},{6,7},{7,6},{8,9},{9,8},{10,11... | collective-permute-start | bytes 786440 | tf_op jit(solution)/shard_map/ppermute | solution.py:31
  32.3 9.2 %collective-permute-start.8 = (bf16[256,512]{1,0:T(8,128)(2,1)S(1)}, bf16[256,512]{1,0:T(8,128)(2,1)S(1)}, u32[]{:S(2)}, u32[]{:S(2)}) collective-permute-start(bf16[256,512]{1,0:T(8,128)(2,1)S(1)} %project.8.refs_0_), channel_id=1, source_target_pairs={{0,2},{1,3},{2,0},{3,1},{4,6},{5,7},{6,4},{7,5},{8,10},{9,11},{10,... | collective-permute-start | bytes 786440 | tf_op jit(solution)/shard_map/ppermute | solution.py:26
  34.5 11.7 %collective-permute-start.10 = (bf16[256,512]{1,0:T(8,128)(2,1)S(1)}, bf16[256,512]{1,0:T(8,128)(2,1)S(1)}, u32[]{:S(2)}, u32[]{:S(2)}) collective-permute-start(bf16[256,512]{1,0:T(8,128)(2,1)S(1)} %project.11), channel_id=1, source_target_pairs={{0,2},{1,3},{2,0},{3,1},{4,6},{5,7},{6,4},{7,5},{8,10},{9,11},{10,... | collective-permute-start | bytes 786440 | tf_op jit(solution)/shard_map/ppermute | solution.py:26

commit v3 on v2

--- a/solution.py
+++ b/solution.py
@@ -21,14 +21,17 @@
     return pltpu.with_memory_space_constraint(array, pltpu.HBM)
 
 
-def cyclic(array, axis, by):
+def moved(array, axis, place):
     count = lax.axis_size(axis)
-    return lax.ppermute(array, axis, [(i, (i + by) % count) for i in range(count)])
+    return lax.ppermute(array, axis, [(i, place(i) % count) for i in range(count)])
 
 
 def other_core(array):
-    count = lax.axis_size("tp")
-    return lax.ppermute(array, "tp", [(i, i ^ 1) for i in range(count)])
+    return moved(array, "tp", lambda i: i ^ 1)
+
+
+def by_parity(even, odd):
+    return jnp.where(lax.rem(lax.axis_index("ctx"), 2) == 1, odd, even)
 
 
 def dot(left, right, left_dim, right_dim):
@@ -46,8 +49,9 @@
     return (mixed & i32(1023)) >= i32(keep_level)
 
 
-def block_grads(offset, window, heads, key, value, query_ref, grad_ref, mix_ref, norm_ref, delta_ref):
+def block_grads(offsets, window, heads, key, value, query_ref, grad_ref, mix_ref, norm_ref, delta_ref):
     rows, width = key.shape
+    offset = offsets[0] if offsets[0] == offsets[1] else by_parity(*offsets)
     key_index = lax.broadcasted_iota(i32, (rows, rows), 0)
     query_index = lax.broadcasted_iota(i32, (rows, rows), 1)
     key_part = (key_index - offset * rows) * i32(19349663)
@@ -63,9 +67,9 @@
         kept = keep_mask(key_part + mix_ref[pl.ds(head, 1), :])
         probs = jnp.exp2(dot(key, query, 1, 1) * scale - log_norm)
         spacing = query_index - key_index
-        if offset == 0:
+        if 0 in offsets:
             probs = jnp.where(spacing >= 0, probs, f32(0.0))
-        if (offset + 1) * rows > window:
+        if (max(offsets) + 1) * rows > window:
             probs = jnp.where(spacing < window - offset * rows, probs, f32(0.0))
         dropped = jnp.where(kept, probs, f32(0.0)).astype(bf16)
         grad_probs = dot(value, grad, 1, 1)
@@ -119,10 +123,19 @@
         rows_ref[pl.ds(offset * heads, heads), :] = jnp.where(active, norms, f32(jnp.inf))
 
 
+def with_copies(loads, results, refs):
+    copies = []
+    for i, (start, size) in enumerate(loads):
+        source = refs[i]
+        copies.append(pltpu.make_async_copy(source, refs[len(loads) + results + i], refs[-1].at[i]))
+        copies[-1].start()
+    return refs[len(loads) : len(loads) + results], copies
+
+
 def own_kernel(
-    window, heads, key_value_ref, query_ref, grad_ref, output_ref, mix_ref, norm_ref, delta_ref,
-    total_ref, sums_ref,
+    window, heads, loads, key_value_ref, query_ref, grad_ref, output_ref, mix_ref, norm_ref, *refs
 ):
+    (delta_ref, total_ref, sums_ref), copies = with_copies(loads, 3, refs)
     rows, width = key_value_ref.shape[0] // 2, key_value_ref.shape[1]
     lane = lax.broadcasted_iota(i32, (rows, 128), 1)
     packed = jnp.zeros((rows, 128), f32)
@@ -134,7 +147,7 @@
         packed = jnp.where(lane == head, delta * f32(1.0 / keep_scale), packed)
     delta_ref[...] = packed.T[: delta_ref.shape[0]]
     key_sum, value_sum, query_parts = block_grads(
-        0, window, heads, key_value_ref[:rows], key_value_ref[rows:], query_ref, grad_ref, mix_ref,
+        (0, 0), window, heads, key_value_ref[:rows], key_value_ref[rows:], query_ref, grad_ref, mix_ref,
         norm_ref, delta_ref,
     )
     grad_scale = keep_scale * width**-0.5
@@ -142,16 +155,19 @@
     sums_ref[rows:] = value_sum * f32(keep_scale)
     for head, part in enumerate(query_parts):
         total_ref[:, pl.ds(head * rows, rows)] = part
+    for copy in copies:
+        copy.wait()
 
 
 def pair_kernel(
-    offset, window, heads, last, key_value_ref, query_ref, grad_ref, mix_ref, norm_ref, delta_ref,
-    before_ref, total_ref, sums_ref,
+    offsets, window, heads, loads, last, key_value_ref, query_ref, grad_ref, mix_ref, norm_ref, delta_ref,
+    before_ref, *refs,
 ):
+    (total_ref, sums_ref), copies = with_copies(loads, 2, refs)
     rows, width = key_value_ref.shape[0] // 2, key_value_ref.shape[1]
     grad_scale = keep_scale * width**-0.5
     key_sum, value_sum, query_parts = block_grads(
-        offset, window, heads, key_value_ref[:rows], key_value_ref[rows:], query_ref, grad_ref,
+        offsets, window, heads, key_value_ref[:rows], key_value_ref[rows:], query_ref, grad_ref,
         mix_ref, norm_ref, delta_ref,
     )
     sums_ref[:rows] = (key_sum * f32(grad_scale)).astype(bf16)
@@ -164,50 +180,63 @@
             ).astype(bf16)
         else:
             total_ref[:, cols] = before_ref[:, cols] + part
-
-
-def project_kernel(hop, flip, start, added, query_ref, sums_ref, wq_ref, wk_ref, wv_ref, *refs):
-    count = lax.axis_size("tp")
+    for copy in copies:
+        copy.wait()
+
+
+def query_term_kernel(query_ref, wq_ref, out_ref):
+    places, _, cols = out_ref.shape
+    query = query_ref[...]
+    for place in range(places):
+        out_ref[place] = dot(query, wq_ref[pl.ds(place * cols, cols), :], 1, 1)
+
+
+def term_kernel(pieces, added, sums_ref, term_ref, wk_ref, wv_ref, *refs):
+    count, rows, block = term_ref.shape
     me = lax.axis_index("tp")
-    if flip:
-        me = me + 1 - 2 * lax.rem(me, 2)
     out_ref = refs[-1]
-    rows, cols = out_ref.shape
-    first = lax.rem(me + hop, count) * (wq_ref.shape[0] // count) + start
-    at = pl.ds(pl.multiple_of(first, 128), cols)
-    total = dot(query_ref[...], wq_ref[at, :], 1, 1)
-    total = total + dot(sums_ref[:rows], wk_ref[at, :], 1, 1)
-    total = total + dot(sums_ref[rows:], wv_ref[at, :], 1, 1)
-    for ref in refs[:added]:
-        total = total + ref[...].astype(f32)
-    out_ref[...] = total.astype(out_ref.dtype)
-
-
-def project(hop, flip, start, cols, operands, added, after, dtype, params):
-    rows, depth = operands[0].shape[0], sum(item.shape[1] for item in operands[2:])
+    keys, values = sums_ref[:rows], sums_ref[rows:]
+    done = 0
+    for hop, flip, start, cols in pieces:
+        place = lax.rem((me + 1 - 2 * lax.rem(me, 2) if flip else me) + hop, count)
+        at = pl.ds(pl.multiple_of(place * block + start, 128), cols)
+        total = term_ref[place, :, pl.ds(start, cols)]
+        total = total + dot(keys, wk_ref[at, :], 1, 1) + dot(values, wv_ref[at, :], 1, 1)
+        if added is not None:
+            total = total + refs[0][:, pl.ds(added + done, cols)].astype(f32)
+        out_ref[:, pl.ds(done, cols)] = total.astype(out_ref.dtype)
+        done += cols
+
+
+def term(pieces, operands, added, after, dtype, flops, params):
+    rows = operands[1].shape[1]
+    first, extra = (None, ()) if added is None else (added[1], added[:1])
     return pl.pallas_call(
-        functools.partial(project_kernel, hop, flip, start, len(added)),
-        in_specs=[in_vmem] * (len(operands) + len(added) + len(after)),
+        functools.partial(term_kernel, pieces, first),
+        in_specs=[in_vmem] * (len(operands) + len(extra) + len(after)),
         out_specs=in_vmem,
-        out_shape=jax.ShapeDtypeStruct((rows, cols), dtype),
+        out_shape=jax.ShapeDtypeStruct((rows, sum(piece[3] for piece in pieces)), dtype),
         compiler_params=params,
-        cost_estimate=cost(2 * rows * cols * depth),
-        name="project",
-    )(*operands, *added, *after)
-
-
-def add_kernel(left_ref, right_ref, out_ref):
+        cost_estimate=cost(flops),
+        name="term",
+    )(*operands, *extra, *after)
+
+
+def add_kernel(left_ref, right_ref, *refs):
+    out_ref = refs[-1]
     out_ref[...] = (left_ref[...] + right_ref[...].astype(f32)).astype(out_ref.dtype)
 
 
-def finish_kernel(first, hops, mine_ref, *refs):
+def finish_kernel(first, hops, low_ref, high_ref, *refs):
     out_hbm, held, sem = refs[-3:]
-    at = pl.ds(first, held.shape[1])
-    total = mine_ref[:, at]
-    for ref in refs[:hops]:
-        total = total + ref[...].astype(f32)
-    held[...] = total.astype(bf16)
-    copy = pltpu.make_async_copy(held, out_hbm.at[:, at], sem)
+    half, size = low_ref.shape[1], held.shape[1]
+    for start in range(first, first + size, 128):
+        ref, at = (low_ref, start) if start < half else (high_ref, start - half)
+        total = ref[:, pl.ds(at, 128)]
+        for ref in refs[:hops]:
+            total = total + ref[:, pl.ds(start - first, 128)].astype(f32)
+        held[:, pl.ds(start - first, 128)] = total.astype(bf16)
+    copy = pltpu.make_async_copy(held, out_hbm.at[:, pl.ds(first, size)], sem)
     copy.start()
     copy.wait()
 
@@ -257,86 +286,126 @@
         cost_estimate=pl.CostEstimate(flops=0, bytes_accessed=0, transcendentals=0),
         name="load",
     )(*map(from_hbm, (keys, values, queries, out_grad, outputs, log_norm.T, counter_base, block_mask)))
-    order = range(steps - 1, 0, -1)
-    arrived = {offset: cyclic(key_value, "ctx", offset) for offset in order}
+    straight = moved(key_value, "ctx", lambda i: i + 2)
+    mixed = moved(key_value, "ctx", lambda i: i + 3 if i % 2 else i + 1)
     block_cost = cost(20 * heads * rows * rows * width)
 
-    deltas, total, own_sums = pl.pallas_call(
-        functools.partial(own_kernel, window, heads),
-        in_specs=[in_vmem] * 6,
-        out_specs=[in_vmem] * 3,
+    all_rows = (0, q_weight.shape[0])
+    loads = (
+        ((q_weight,), (all_rows,)),
+        ((k_weight, v_weight), (all_rows,) * 2),
+        ((), ()),
+        ((), ()),
+    )
+
+    def loaded(load):
+        return [shape((size, item.shape[1]), bf16) for item, (_, size) in zip(*load)]
+
+    deltas, total, sums, *q_low = pl.pallas_call(
+        functools.partial(own_kernel, window, heads, loads[0][1]),
+        in_specs=[in_vmem] * 6 + [in_hbm] * len(loads[0][0]),
+        out_specs=[in_vmem] * (3 + len(loads[0][0])),
         out_shape=[
             shape((heads, rows), f32),
             shape((width, heads * rows), f32),
             shape((2 * rows, width), f32),
+            *loaded(loads[0]),
         ],
+        scratch_shapes=[pltpu.SemaphoreType.DMA((len(loads[0][0]),))],
         compiler_params=params,
-        cost_estimate=block_cost,
+        cost_estimate=cost(10**6),
         name="own_block",
-    )(key_value, query, grad, output, mix, norms)
-
-    returned = []
-    for offset in order:
-        last = offset == order[-1]
-        total, sums = pl.pallas_call(
-            functools.partial(pair_kernel, offset, window, heads, last),
-            in_specs=[in_vmem] * 7,
-            out_specs=[in_vmem] * 2,
+    )(key_value, query, grad, output, mix, norms, *map(from_hbm, loads[0][0]))
+
+    straight, deltas = lax.optimization_barrier((straight, deltas))
+    crossed = moved(straight, "ctx", lambda i: i ^ 1)
+    returned, held = [], [*q_low]
+    for load, offsets, arrived in zip(
+        loads[1:], ((2, 2), (3, 1), (1, 3)), (straight, mixed, crossed)
+    ):
+        last = offsets == (1, 3)
+        total, parts, *more = pl.pallas_call(
+            functools.partial(pair_kernel, offsets, window, heads, load[1], last),
+            in_specs=[in_vmem] * 7 + [in_hbm] * len(load[0]),
+            out_specs=[in_vmem] * (2 + len(load[0])),
             out_shape=[
                 shape((rows, heads * width), bf16) if last else shape((width, heads * rows), f32),
                 shape((2 * rows, width), bf16),
+                *loaded(load),
             ],
+            scratch_shapes=[pltpu.SemaphoreType.DMA((len(load[0]),))] * (len(load[0]) > 0),
             compiler_params=params,
-            cost_estimate=block_cost,
-            name="block_back_%d" % offset,
-        )(arrived[offset], query, grad, mix, norms, deltas, total)
-        returned.append(cyclic(sums, "ctx", -offset))
-    grad_query = total
-    sums = own_sums
+            cost_estimate=cost(10**6),
+            name="block_back_%d%d" % offsets,
+        )(arrived, query, grad, mix, norms, deltas, total, *map(from_hbm, load[0]))
+        held.extend(more)
+        even, odd = offsets
+        returned.append(moved(parts, "ctx", lambda i: i - (odd if i % 2 else even)))
+
+    cols = q_weight.shape[0] // tp_size
+    query_term = pl.pallas_call(
+        query_term_kernel,
+        in_specs=[in_vmem] * 2,
+        out_specs=in_vmem,
+        out_shape=shape((tp_size, rows, cols), f32),
+        compiler_params=params,
+        cost_estimate=block_cost,
+        name="query_term",
+    )(total, held[0])
     for item in returned:
+        final = item is returned[-1]
         sums = pl.pallas_call(
             add_kernel,
-            in_specs=[in_vmem] * 2,
+            in_specs=[in_vmem] * (3 if final else 2),
             out_specs=in_vmem,
-            out_shape=shape(sums.shape, bf16 if item is returned[-1] else f32),
+            out_shape=shape(sums.shape, bf16 if final else f32),
             compiler_params=params,
             cost_estimate=block_cost,
             name="add_returned",
-        )(sums, item)
-    operands = (grad_query, sums, q_weight, k_weight, v_weight)
-    cols = q_weight.shape[0] // tp_size
-    sizes = [cols // 2] * 2
-    starts = [sum(sizes[:i]) for i in range(len(sizes))]
-    hops = tp_size // 2 - 1
-    places = [(i, hop) for i in range(len(sizes)) for hop in range(2, tp_size, 2)]
-    swapped, terms, after = [], [], ()
-    for i, hop in places:
-        part = project(hop, True, starts[i], sizes[i], operands, (), after, bf16, params)
-        swapped.append(other_core(part))
+        )(sums, item, *((query_term,) if final else ()))
+
+    operands = (sums, query_term, *held[1:])
+    hops = range(2, tp_size, 2)
+    sizes = (cols * 5 // 8, cols * 3 // 8) if cols % 1024 == 0 else (cols // 2,) * 2
+    starts = (0, sizes[0])
+    low, high = 10**6, block_cost.flops
+
+    def swapped_term(places, after):
+        pieces = [(hop, True, start, size) for hop, start, size in places]
+        part = term(pieces, operands, None, after, bf16, low, params)
+        return part, other_core(part)
+
+    swapped, after = [], ()
+    for i in range(2):
+        part, item = swapped_term([(hop, starts[i], sizes[i]) for hop in hops], after)
+        swapped.append(item)
         after = (part,)
-    for (i, hop), item in zip(places, swapped):
-        part = project(hop, False, starts[i], sizes[i], operands, (item,), after, bf16, params)
-        terms.append(part)
-        after = (part,)
-        if len(terms) == 1:
-            part = project(0, True, 0, cols, operands, (), after, bf16, params)
-            other = other_core(part)
+    part, swapped_low = swapped_term([(0, 0, cols // 2)], after)
+    part, swapped_high = swapped_term([(0, cols // 2, cols // 2)], (part,))
+    sent, after = [[], []], (part,)
+    for i in range(2):
+        for j, hop in enumerate(hops):
+            piece = ((hop, False, starts[i], sizes[i]),)
+            part = term(piece, operands, (swapped[i], j * sizes[i]), after, bf16, low, params)
+            sent[i].append(moved(part, "tp", lambda k: k + hop))
             after = (part,)
-    sent = [cyclic(term, "tp", hop) for (_, hop), term in zip(places, terms)]
-    mine = project(0, False, 0, cols, operands, (other,), tuple(sent[:1]), f32, params)
+    mine = [
+        term(((0, False, j * (cols // 2), cols // 2),), operands, (item, 0), tuple(sent[0][:1]), f32, 10 * high, params)
+        for j, item in enumerate((swapped_low, swapped_high))
+    ]
     out = ()
-    for i, size in enumerate(sizes):
+    for i in range(2):
         out = pl.pallas_call(
-            functools.partial(finish_kernel, starts[i], hops),
-            in_specs=[in_vmem] * (1 + hops) + [in_hbm] * len(out),
+            functools.partial(finish_kernel, starts[i], len(hops)),
+            in_specs=[in_vmem] * (2 + len(hops)) + [in_hbm] * len(out),
             out_specs=in_hbm,
             out_shape=shape((rows, cols), bf16),
-            input_output_aliases={1 + hops: 0} if out else {},
-            scratch_shapes=[pltpu.VMEM((rows, size), bf16), pltpu.SemaphoreType.DMA],
+            input_output_aliases={2 + len(hops): 0} if out else {},
+            scratch_shapes=[pltpu.VMEM((rows, sizes[i]), bf16), pltpu.SemaphoreType.DMA],
             compiler_params=params,
-            cost_estimate=cost(10**6),
+            cost_estimate=cost(low),
             name="finish",
-        )(mine, *sent[i * hops : (i + 1) * hops], *out)
+        )(*mine, *sent[i], *out)
         out = (out,)
     return out[0]
 

time: 47.2 us -> 43.8 us (0.928)
  waiting for transfers between devices: 24.1 us -> 14.6 us
  starting transfers between devices: 11.3 us -> 15.6 us
  Pallas kernels: 11.5 us -> 13.2 us
    ppermute x11 -> x12, waiting for transfers between devices: 24.1 us -> 14.6 us  [moved(): lax.ppermute(array, axis, [(i, place(i) % count) for i in range(count)])]
    ppermute x11 -> x12, starting transfers between devices: 11.3 us -> 15.6 us  [moved(): lax.ppermute(array, axis, [(i, place(i) % count) for i in range(count)])]
    pallas_call x15 -> x18, Pallas kernels: 10.2 us -> 11.9 us  [the longest x3 4.38 us: on_device(): pl.pallas_call(functools.partial(pair_kernel, offsets, window, heads, loa...]
  transfers between devices with their start and end apart: 11 -> 12, of which waited for: 8 -> 8; matrix products, arithmetic and copies ran while one was open for 0% -> 0% of each run, Pallas kernels for 17% -> 24%
where the time goes in v3:
time: 43.8 us; the launch traced here: 43.6 us
  starting transfers between devices  15.6 us (36%)
  waiting for transfers between devices  14.6 us (33%)
  Pallas kernels  13.2 us (30%)
    ppermute x12, starting transfers between devices, moved(): lax.ppermute(array, axis, [(i, place(i) % count) for i in range(count)])  15.6 us
    ppermute x12, waiting for transfers between devices, moved(): lax.ppermute(array, axis, [(i, place(i) % count) for i in range(count)])  14.6 us
    pallas_call x3, Pallas kernels, on_device(): pl.pallas_call(functools.partial(pair_kernel, offsets, window, heads, loa...  4.38 us
    pallas_call x8, Pallas kernels, term(): pl.pallas_call(functools.partial(term_kernel, pieces, first), in_specs=[i...  2.47 us
    pallas_call x1, Pallas kernels, on_device(): pl.pallas_call(functools.partial(own_kernel, window, heads, loads[0][1]),...  2.2 us
    pallas_call x2, Pallas kernels, on_device(): pl.pallas_call(functools.partial(finish_kernel, starts[i], len(hops)), in...  1.54 us
    pallas_call x1, Pallas kernels, on_device(): pl.pallas_call(functools.partial(load_kernel, heads), in_specs=[in_hbm] *...  1.29 us
    pallas_call x1, Pallas kernels, on_device(): pl.pallas_call(query_term_kernel, in_specs=[in_vmem] * 2, out_specs=in_vm...  1.28 us
  transfers between devices with their start and end apart: 12, of which 8 were waited for; matrix products, arithmetic and copies ran while one was open for 0% of the time, Pallas kernels for 24%

profile of v3, /device:TPU:0, one launch (start us, length us, event | category | flops | bytes accessed | tf_op | source)
XLA Modules:
  0.0 43.6 jit_solution(89645282214547529)
XLA Ops:
  0.0 1.3 %load.1 = (bf16[512,128]{1,0:T(8,128)(2,1)S(1)}, bf16[256,512]{1,0:T(8,128)(2,1)S(1)}, bf16[256,512]{1,0:T(8,128)(2,1)S(1)}, bf16[256,512]{1,0:T(8,128)(2,1)S(1)...) custom-call(bf16[256,128]{1,0:T(8,128)(2,1)} %key_hbm.1, bf16[256,128]{1,0:T(8,128)(2,1)} %value_hbm.1, ...), custom_call_target="tpu_custom_call" | custom-call | tf_op jit(solution)/shard_map/load/pallas_call | solution.py:269
  1.3 3.1 %collective-permute-start = (bf16[512,128]{1,0:T(8,128)(2,1)S(1)}, bf16[512,128]{1,0:T(8,128)(2,1)S(1)}, u32[]{:S(2)}, u32[]{:S(2)}) collective-permute-start(bf16[512,128]{1,0:T(8,128)(2,1)S(1)} %get-tuple-element.25.key_value_ref), channel_id=1, source_target_pairs={{0,8},{4,12},{8,16},{12,20},{16,24},{20,28},{24,0},{28,4},{1,9},{5... | collective-permute-start | bytes 393224 | tf_op jit(solution)/shard_map/ppermute | solution.py:26
  4.4 1.5 %collective-permute-start.2 = (bf16[512,128]{1,0:T(8,128)(2,1)S(1)}, bf16[512,128]{1,0:T(8,128)(2,1)S(1)}, u32[]{:S(2)}, u32[]{:S(2)}) collective-permute-start(bf16[512,128]{1,0:T(8,128)(2,1)S(1)} %get-tuple-element.25.key_value_ref), channel_id=1, source_target_pairs={{0,4},{4,16},{8,12},{12,24},{16,20},{20,0},{24,28},{28,8},{1,5},{5... | collective-permute-start | bytes 393224 | tf_op jit(solution)/shard_map/ppermute | solution.py:26
  5.9 2.2 %own_block.1 = (f32[4,256]{1,0:T(4,128)S(1)}, f32[128,1024]{1,0:T(8,128)S(1)}, f32[512,128]{1,0:T(8,128)S(1)}, bf16[4096,512]{1,0:T(8,128)(2,1)S(1)}) custom-call(bf16[512,128]{1,0:T(8,128)(2,1)S(1)} %get-tuple-element.25.key_value_ref, bf16[256,512]{1,0:T(8,128)(2,1)S(1)} %get-tuple-element.26.query_ref, bf16[256,512]{1,0:T(8,128)(2,1)S(1)} %get-tuple-element.27.grad_ref, ...), custom_call_target="tpu_custom_call" | custom-call | flops 1000000 | bytes 2500 | tf_op jit(solution)/shard_map/own_block/pallas_call | solution.py:304
  8.1 1.8 %collective-permute-done.key_value_ref = bf16[512,128]{1,0:T(8,128)(2,1)S(1)} collective-permute-done((bf16[512,128]{1,0:T(8,128)(2,1)S(1)}, bf16[512,128]{1,0:T(8,128)(2,1)S(1)}, u32[]{:S(2)}, u32[]{:S(2)}) %collective-permute-start) | collective-permute-done | bytes 131104 | tf_op jit(solution)/shard_map/ppermute | solution.py:26
  9.9 2.7 %collective-permute-start.4 = (bf16[512,128]{1,0:T(8,128)(2,1)S(1)}, bf16[512,128]{1,0:T(8,128)(2,1)S(1)}, u32[]{:S(2)}, u32[]{:S(2)}) collective-permute-start(bf16[512,128]{1,0:T(8,128)(2,1)S(1)} %collective-permute-done.key_value_ref), channel_id=1, source_target_pairs={{0,4},{4,0},{8,12},{12,8},{16,20},{20,16},{24,28},{28,24},{1,5},{5... | collective-permute-start | bytes 393224 | tf_op jit(solution)/shard_map/ppermute | solution.py:26
  12.6 1.6 %block_back_22.1 = (f32[128,1024]{1,0:T(8,128)S(1)}, bf16[512,128]{1,0:T(8,128)(2,1)S(1)}, bf16[4096,128]{1,0:T(8,128)(2,1)S(1)}, bf16[4096,128]{1,0:T(8,128)(2,1)S(1)}) custom-call(bf16[512,128]{1,0:T(8,128)(2,1)S(1)} %collective-permute-done.key_value_ref, bf16[256,512]{1,0:T(8,128)(2,1)S(1)} %get-tuple-element.26.query_ref, ...), custom_call_target="tpu_custom_call" | custom-call | flops 1000000 | bytes 2500 | tf_op jit(solution)/shard_map/block_back_22/pallas_call | solution.py:327
  14.1 1.2 %collective-permute-start.1 = (bf16[512,128]{1,0:T(8,128)(2,1)S(1)}, bf16[512,128]{1,0:T(8,128)(2,1)S(1)}, u32[]{:S(2)}, u32[]{:S(2)}) collective-permute-start(bf16[512,128]{1,0:T(8,128)(2,1)S(1)} %get-tuple-element.36), channel_id=1, source_target_pairs={{0,24},{4,28},{8,0},{12,4},{16,8},{20,12},{24,16},{28,20},{1,25},{... | collective-permute-start | bytes 393224 | tf_op jit(solution)/shard_map/ppermute | solution.py:26
  15.3 1.3 %collective-permute-done.2.key_value_ref = bf16[512,128]{1,0:T(8,128)(2,1)S(1)} collective-permute-done((bf16[512,128]{1,0:T(8,128)(2,1)S(1)}, bf16[512,128]{1,0:T(8,128)(2,1)S(1)}, u32[]{:S(2)}, u32[]{:S(2)}) %collective-permute-start.2) | collective-permute-done | bytes 131104 | tf_op jit(solution)/shard_map/ppermute | solution.py:26
  16.6 1.4 %block_back_31.1 = (f32[128,1024]{1,0:T(8,128)S(1)}, bf16[512,128]{1,0:T(8,128)(2,1)S(1)}) custom-call(bf16[512,128]{1,0:T(8,128)(2,1)S(1)} %collective-permute-done.2.key_value_ref, bf16[256,512]{1,0:T(8,128)(2,1)S(1)} %get-tuple-element.26.query_ref, bf16[256,512]{1,0:T(8,128)(2,1)S(1)} %get-tuple-element.27.grad_ref, ...), custom_call_target="tpu_custom_call" | custom-call | flops 1000000 | bytes 2500 | tf_op jit(solution)/shard_map/block_back_31/pallas_call | solution.py:327
  18.0 0.6 %collective-permute-start.3 = (bf16[512,128]{1,0:T(8,128)(2,1)S(1)}, bf16[512,128]{1,0:T(8,128)(2,1)S(1)}, u32[]{:S(2)}, u32[]{:S(2)}) collective-permute-start(bf16[512,128]{1,0:T(8,128)(2,1)S(1)} %get-tuple-element.38), channel_id=1, source_target_pairs={{0,20},{4,0},{8,28},{12,8},{16,4},{20,16},{24,12},{28,24},{1,21},{... | collective-permute-start | bytes 393224 | tf_op jit(solution)/shard_map/ppermute | solution.py:26
  18.6 1.5 %block_back_13.1 = (bf16[256,512]{1,0:T(8,128)(2,1)S(1)}, bf16[512,128]{1,0:T(8,128)(2,1)S(1)}) custom-call(bf16[512,128]{1,0:T(8,128)(2,1)S(1)} %collective-permute-done.4.key_value_ref, bf16[256,512]{1,0:T(8,128)(2,1)S(1)} %get-tuple-element.26.query_ref, bf16[256,512]{1,0:T(8,128)(2,1)S(1)} %get-tuple-element.27.grad_ref, ...), custom_call_target="tpu_custom_call" | custom-call | flops 1000000 | bytes 2500 | tf_op jit(solution)/shard_map/block_back_13/pallas_call | solution.py:327
  20.1 3.9 %collective-permute-start.5 = (bf16[512,128]{1,0:T(8,128)(2,1)S(1)}, bf16[512,128]{1,0:T(8,128)(2,1)S(1)}, u32[]{:S(2)}, u32[]{:S(2)}) collective-permute-start(bf16[512,128]{1,0:T(8,128)(2,1)S(1)} %get-tuple-element.40), channel_id=1, source_target_pairs={{0,28},{4,24},{8,4},{12,0},{16,12},{20,8},{24,20},{28,16},{1,29},{... | collective-permute-start | bytes 393224 | tf_op jit(solution)/shard_map/ppermute | solution.py:26
  23.9 1.3 %query_term.1.refs_0_.term_ref = f32[4,256,1024]{2,1,0:T(8,128)S(1)} custom-call(bf16[256,512]{1,0:T(8,128)(2,1)S(1)} %get-tuple-element.41.query_ref, bf16[4096,512]{1,0:T(8,128)(2,1)S(1)} %get-tuple-element.42.wq_ref), custom_call_target="tpu_custom_call" | custom-call | flops 671088640 | bytes 1677721 | tf_op jit(solution)/shard_map/query_term/pallas_call | solution.py:346
  25.3 0.9 %collective-permute-done.3.right_ref = bf16[512,128]{1,0:T(8,128)(2,1)S(1)} collective-permute-done((bf16[512,128]{1,0:T(8,128)(2,1)S(1)}, bf16[512,128]{1,0:T(8,128)(2,1)S(1)}, u32[]{:S(2)}, u32[]{:S(2)}) %collective-permute-start.3) | collective-permute-done | bytes 131104 | tf_op jit(solution)/shard_map/ppermute | solution.py:26
  26.2 0.3 collective-permute-done.5.right_ref
  26.5 0.3 term.8.refs_0_
  26.9 0.3 term.9.refs_0_
  27.2 0.3 term.10.refs_0_
  27.5 0.3 term.11.refs_1_
  27.8 0.7 %collective-permute-done.7.refs_0_ = bf16[256,640]{1,0:T(8,128)(2,1)S(1)} collective-permute-done((bf16[256,640]{1,0:T(8,128)(2,1)S(1)}, bf16[256,640]{1,0:T(8,128)(2,1)S(1)}, u32[]{:S(2)}, u32[]{:S(2)}) %collective-permute-start.7) | collective-permute-done | bytes 327712 | tf_op jit(solution)/shard_map/ppermute | solution.py:26
  28.5 0.3 term.12.refs_1_
  28.9 1.6 %collective-permute-start.8 = (bf16[256,640]{1,0:T(8,128)(2,1)S(1)}, bf16[256,640]{1,0:T(8,128)(2,1)S(1)}, u32[]{:S(2)}, u32[]{:S(2)}) collective-permute-start(bf16[256,640]{1,0:T(8,128)(2,1)S(1)} %term.12.refs_1_), channel_id=1, source_target_pairs={{0,2},{1,3},{2,0},{3,1},{4,6},{5,7},{6,4},{7,5},{8,10},{9,11},{10,... | collective-permute-start | bytes 983048 | tf_op jit(solution)/shard_map/ppermute | solution.py:26
  30.5 0.5 %collective-permute-start.10 = (bf16[256,384]{1,0:T(8,128)(2,1)S(1)}, bf16[256,384]{1,0:T(8,128)(2,1)S(1)}, u32[]{:S(2)}, u32[]{:S(2)}) collective-permute-start(bf16[256,384]{1,0:T(8,128)(2,1)S(1)} %term.9.refs_0_), channel_id=1, source_target_pairs={{0,1},{1,0},{2,3},{3,2},{4,5},{5,4},{6,7},{7,6},{8,9},{9,8},{10,11... | collective-permute-start | bytes 589832 | tf_op jit(solution)/shard_map/ppermute | solution.py:26
  31.0 1.3 %collective-permute-done.10.refs_0_ = bf16[256,384]{1,0:T(8,128)(2,1)S(1)} collective-permute-done((bf16[256,384]{1,0:T(8,128)(2,1)S(1)}, bf16[256,384]{1,0:T(8,128)(2,1)S(1)}, u32[]{:S(2)}, u32[]{:S(2)}) %collective-permute-start.10) | collective-permute-done | bytes 196640 | tf_op jit(solution)/shard_map/ppermute | solution.py:26
  32.6 0.6 %collective-permute-start.11 = (bf16[256,384]{1,0:T(8,128)(2,1)S(1)}, bf16[256,384]{1,0:T(8,128)(2,1)S(1)}, u32[]{:S(2)}, u32[]{:S(2)}) collective-permute-start(bf16[256,384]{1,0:T(8,128)(2,1)S(1)} %term.15), channel_id=1, source_target_pairs={{0,2},{1,3},{2,0},{3,1},{4,6},{5,7},{6,4},{7,5},{8,10},{9,11},{10,... | collective-permute-start | bytes 589832 | tf_op jit(solution)/shard_map/ppermute | solution.py:26
  33.1 6.4 %collective-permute-done.8.refs_1_.refs_0_ = bf16[256,640]{1,0:T(8,128)(2,1)S(1)} collective-permute-done((bf16[256,640]{1,0:T(8,128)(2,1)S(1)}, bf16[256,640]{1,0:T(8,128)(2,1)S(1)}, u32[]{:S(2)}, u32[]{:S(2)}) %collective-permute-start.8) | collective-permute-done | bytes 327712 | tf_op jit(solution)/shard_map/ppermute | solution.py:26
  39.5 0.3 term.13.low_ref
  39.8 0.3 term.14.high_ref
  40.1 0.8 %finish.2.refs_1_ = bf16[256,1024]{1,0:T(8,128)(2,1)} custom-call(f32[256,512]{1,0:T(8,128)S(1)} %term.13.low_ref, f32[256,512]{1,0:T(8,128)S(1)} %term.14.high_ref, bf16[256,640]{1,0:T(8,128)(2,1)S(1)} %collective-permute-done.8.refs_1_.refs_0_), custom_call_target="tpu_custom_call" | custom-call | flops 1000000 | bytes 2500 | tf_op jit(solution)/shard_map/finish/pallas_call | solution.py:398
  40.9 2.0 %collective-permute-done.11.refs_0_ = bf16[256,384]{1,0:T(8,128)(2,1)S(1)} collective-permute-done((bf16[256,384]{1,0:T(8,128)(2,1)S(1)}, bf16[256,384]{1,0:T(8,128)(2,1)S(1)}, u32[]{:S(2)}, u32[]{:S(2)}) %collective-permute-start.11) | collective-permute-done | bytes 196640 | tf_op jit(solution)/shard_map/ppermute | solution.py:26
  42.9 0.7 %finish.3 = bf16[256,1024]{1,0:T(8,128)(2,1)} custom-call(f32[256,512]{1,0:T(8,128)S(1)} %term.13.low_ref, f32[256,512]{1,0:T(8,128)S(1)} %term.14.high_ref, bf16[256,384]{1,0:T(8,128)(2,1)S(1)} %collective-permute-done.11.refs_0_, bf16[256,1024]{1,0:T(8,128)(2,1)} %finish.2.refs_1_), custom_call_target="tpu_custom_call", output_to_operand_aliasing={{}: (3, {})} | custom-call | flops 1000000 | bytes 2500 | tf_op jit(solution)/shard_map/finish/pallas_call | solution.py:398
  (11 shorter events, 0.4 us)
Async XLA Ops:
  1.3 8.6 %collective-permute-start = (bf16[512,128]{1,0:T(8,128)(2,1)S(1)}, bf16[512,128]{1,0:T(8,128)(2,1)S(1)}, u32[]{:S(2)}, u32[]{:S(2)}) collective-permute-start(bf16[512,128]{1,0:T(8,128)(2,1)S(1)} %get-tuple-element.25.key_value_ref), channel_id=1, source_target_pairs={{0,8},{4,12},{8,16},{12,20},{16,24},{20,28},{24,0},{28,4},{1,9},{5... | collective-permute-start | bytes 393224 | tf_op jit(solution)/shard_map/ppermute | solution.py:26
  4.4 12.2 %collective-permute-start.2 = (bf16[512,128]{1,0:T(8,128)(2,1)S(1)}, bf16[512,128]{1,0:T(8,128)(2,1)S(1)}, u32[]{:S(2)}, u32[]{:S(2)}) collective-permute-start(bf16[512,128]{1,0:T(8,128)(2,1)S(1)} %get-tuple-element.25.key_value_ref), channel_id=1, source_target_pairs={{0,4},{4,16},{8,12},{12,24},{16,20},{20,0},{24,28},{28,8},{1,5},{5... | collective-permute-start | bytes 393224 | tf_op jit(solution)/shard_map/ppermute | solution.py:26
  9.9 8.7 %collective-permute-start.4 = (bf16[512,128]{1,0:T(8,128)(2,1)S(1)}, bf16[512,128]{1,0:T(8,128)(2,1)S(1)}, u32[]{:S(2)}, u32[]{:S(2)}) collective-permute-start(bf16[512,128]{1,0:T(8,128)(2,1)S(1)} %collective-permute-done.key_value_ref), channel_id=1, source_target_pairs={{0,4},{4,0},{8,12},{12,8},{16,20},{20,16},{24,28},{28,24},{1,5},{5... | collective-permute-start | bytes 393224 | tf_op jit(solution)/shard_map/ppermute | solution.py:26
  14.1 11.1 %collective-permute-start.1 = (bf16[512,128]{1,0:T(8,128)(2,1)S(1)}, bf16[512,128]{1,0:T(8,128)(2,1)S(1)}, u32[]{:S(2)}, u32[]{:S(2)}) collective-permute-start(bf16[512,128]{1,0:T(8,128)(2,1)S(1)} %get-tuple-element.36), channel_id=1, source_target_pairs={{0,24},{4,28},{8,0},{12,4},{16,8},{20,12},{24,16},{28,20},{1,25},{... | collective-permute-start | bytes 393224 | tf_op jit(solution)/shard_map/ppermute | solution.py:26
  18.0 8.1 %collective-permute-start.3 = (bf16[512,128]{1,0:T(8,128)(2,1)S(1)}, bf16[512,128]{1,0:T(8,128)(2,1)S(1)}, u32[]{:S(2)}, u32[]{:S(2)}) collective-permute-start(bf16[512,128]{1,0:T(8,128)(2,1)S(1)} %get-tuple-element.38), channel_id=1, source_target_pairs={{0,20},{4,0},{8,28},{12,8},{16,4},{20,16},{24,12},{28,24},{1,21},{... | collective-permute-start | bytes 393224 | tf_op jit(solution)/shard_map/ppermute | solution.py:26
  20.1 6.4 %collective-permute-start.5 = (bf16[512,128]{1,0:T(8,128)(2,1)S(1)}, bf16[512,128]{1,0:T(8,128)(2,1)S(1)}, u32[]{:S(2)}, u32[]{:S(2)}) collective-permute-start(bf16[512,128]{1,0:T(8,128)(2,1)S(1)} %get-tuple-element.40), channel_id=1, source_target_pairs={{0,28},{4,24},{8,4},{12,0},{16,12},{20,8},{24,20},{28,16},{1,29},{... | collective-permute-start | bytes 393224 | tf_op jit(solution)/shard_map/ppermute | solution.py:26
  26.8 1.7 %collective-permute-start.7 = (bf16[256,640]{1,0:T(8,128)(2,1)S(1)}, bf16[256,640]{1,0:T(8,128)(2,1)S(1)}, u32[]{:S(2)}, u32[]{:S(2)}) collective-permute-start(bf16[256,640]{1,0:T(8,128)(2,1)S(1)} %term.8.refs_0_), channel_id=1, source_target_pairs={{0,1},{1,0},{2,3},{3,2},{4,5},{5,4},{6,7},{7,6},{8,9},{9,8},{10,11... | collective-permute-start | bytes 983048 | tf_op jit(solution)/shard_map/ppermute | solution.py:26
  28.9 10.6 %collective-permute-start.8 = (bf16[256,640]{1,0:T(8,128)(2,1)S(1)}, bf16[256,640]{1,0:T(8,128)(2,1)S(1)}, u32[]{:S(2)}, u32[]{:S(2)}) collective-permute-start(bf16[256,640]{1,0:T(8,128)(2,1)S(1)} %term.12.refs_1_), channel_id=1, source_target_pairs={{0,2},{1,3},{2,0},{3,1},{4,6},{5,7},{6,4},{7,5},{8,10},{9,11},{10,... | collective-permute-start | bytes 983048 | tf_op jit(solution)/shard_map/ppermute | solution.py:26
  30.5 2.7 %collective-permute-start.6 = (bf16[256,512]{1,0:T(8,128)(2,1)S(1)}, bf16[256,512]{1,0:T(8,128)(2,1)S(1)}, u32[]{:S(2)}, u32[]{:S(2)}) collective-permute-start(bf16[256,512]{1,0:T(8,128)(2,1)S(1)} %term.10.refs_0_), channel_id=1, source_target_pairs={{0,1},{1,0},{2,3},{3,2},{4,5},{5,4},{6,7},{7,6},{8,9},{9,8},{10,11... | collective-permute-start | bytes 786440 | tf_op jit(solution)/shard_map/ppermute | solution.py:26
  30.5 1.8 %collective-permute-start.10 = (bf16[256,384]{1,0:T(8,128)(2,1)S(1)}, bf16[256,384]{1,0:T(8,128)(2,1)S(1)}, u32[]{:S(2)}, u32[]{:S(2)}) collective-permute-start(bf16[256,384]{1,0:T(8,128)(2,1)S(1)} %term.9.refs_0_), channel_id=1, source_target_pairs={{0,1},{1,0},{2,3},{3,2},{4,5},{5,4},{6,7},{7,6},{8,9},{9,8},{10,11... | collective-permute-start | bytes 589832 | tf_op jit(solution)/shard_map/ppermute | solution.py:26
  31.0 8.8 %collective-permute-start.9 = (bf16[256,512]{1,0:T(8,128)(2,1)S(1)}, bf16[256,512]{1,0:T(8,128)(2,1)S(1)}, u32[]{:S(2)}, u32[]{:S(2)}) collective-permute-start(bf16[256,512]{1,0:T(8,128)(2,1)S(1)} %term.11.refs_1_), channel_id=1, source_target_pairs={{0,1},{1,0},{2,3},{3,2},{4,5},{5,4},{6,7},{7,6},{8,9},{9,8},{10,11... | collective-permute-start | bytes 786440 | tf_op jit(solution)/shard_map/ppermute | solution.py:26
  32.6 10.3 %collective-permute-start.11 = (bf16[256,384]{1,0:T(8,128)(2,1)S(1)}, bf16[256,384]{1,0:T(8,128)(2,1)S(1)}, u32[]{:S(2)}, u32[]{:S(2)}) collective-permute-start(bf16[256,384]{1,0:T(8,128)(2,1)S(1)} %term.15), channel_id=1, source_target_pairs={{0,2},{1,3},{2,0},{3,1},{4,6},{5,7},{6,4},{7,5},{8,10},{9,11},{10,... | collective-permute-start | bytes 589832 | tf_op jit(solution)/shard_map/ppermute | solution.py:26

commit v4 on v3

--- a/solution.py
+++ b/solution.py
@@ -287,7 +287,9 @@
         name="load",
     )(*map(from_hbm, (keys, values, queries, out_grad, outputs, log_norm.T, counter_base, block_mask)))
     straight = moved(key_value, "ctx", lambda i: i + 2)
-    mixed = moved(key_value, "ctx", lambda i: i + 3 if i % 2 else i + 1)
+    count = lax.axis_size("ctx")
+    pairs = [(i, i + (3 if i % 2 else 1)) for i in range(count)]
+    mixed = lax.ppermute(key_value, "ctx", [pair for pair in pairs if pair[1] < count])
     block_cost = cost(20 * heads * rows * rows * width)
 
     all_rows = (0, q_weight.shape[0])
@@ -340,7 +342,10 @@
         )(arrived, query, grad, mix, norms, deltas, total, *map(from_hbm, load[0]))
         held.extend(more)
         even, odd = offsets
-        returned.append(moved(parts, "ctx", lambda i: i - (odd if i % 2 else even)))
+        shift = offsets == (1, 3)
+        returned.append(
+            moved(parts, "ctx", lambda i: i - 2 if shift and i < 2 else i - (odd if i % 2 else even))
+        )
 
     cols = q_weight.shape[0] // tp_size
     query_term = pl.pallas_call(

time: 43.8 us -> 42.5 us (0.970)
  waiting for transfers between devices: 14.6 us -> 12.7 us
    ppermute x0 -> x1, starting transfers between devices: none -> 3.39 us  [on_device(): lax.ppermute(key_value, 'ctx', [pair for pair in pairs if pair[1] < count])]
    ppermute x12 -> x11, starting transfers between devices: 15.6 us -> 12.6 us  [moved(): lax.ppermute(array, axis, [(i, place(i) % count) for i in range(count)])]
    ppermute x12 -> x11, waiting for transfers between devices: 14.6 us -> 12.7 us  [moved(): lax.ppermute(array, axis, [(i, place(i) % count) for i in range(count)])]
  transfers between devices with their start and end apart: 12 -> 12, of which waited for: 8 -> 5; matrix products, arithmetic and copies ran while one was open for 0% -> 0% of each run, Pallas kernels for 24% -> 25%
where the time goes in v4:
time: 42.5 us; the launch traced here: 42.2 us
  starting transfers between devices  16 us (38%)
  Pallas kernels  13.2 us (31%)
  waiting for transfers between devices  12.7 us (30%)
    ppermute x11, waiting for transfers between devices, moved(): lax.ppermute(array, axis, [(i, place(i) % count) for i in range(count)])  12.7 us
    ppermute x11, starting transfers between devices, moved(): lax.ppermute(array, axis, [(i, place(i) % count) for i in range(count)])  12.6 us
    pallas_call x3, Pallas kernels, on_device(): pl.pallas_call(functools.partial(pair_kernel, offsets, window, heads, loa...  4.38 us
    ppermute x1, starting transfers between devices, on_device(): lax.ppermute(key_value, 'ctx', [pair for pair in pairs if pair[1] < count])  3.39 us
    pallas_call x8, Pallas kernels, term(): pl.pallas_call(functools.partial(term_kernel, pieces, first), in_specs=[i...  2.47 us
    pallas_call x1, Pallas kernels, on_device(): pl.pallas_call(functools.partial(own_kernel, window, heads, loads[0][1]),...  2.2 us
    pallas_call x2, Pallas kernels, on_device(): pl.pallas_call(functools.partial(finish_kernel, starts[i], len(hops)), in...  1.54 us
    pallas_call x1, Pallas kernels, on_device(): pl.pallas_call(functools.partial(load_kernel, heads), in_specs=[in_hbm] *...  1.29 us
  transfers between devices with their start and end apart: 12, of which 5 were waited for; matrix products, arithmetic and copies ran while one was open for 0% of the time, Pallas kernels for 25%

profile of v4, /device:TPU:0, one launch (start us, length us, event | category | flops | bytes accessed | tf_op | source)
XLA Modules:
  0.0 42.2 jit_solution(17419026392589327402)
XLA Ops:
  0.0 1.3 %load.1 = (bf16[512,128]{1,0:T(8,128)(2,1)S(1)}, bf16[256,512]{1,0:T(8,128)(2,1)S(1)}, bf16[256,512]{1,0:T(8,128)(2,1)S(1)}, bf16[256,512]{1,0:T(8,128)(2,1)S(1)...) custom-call(bf16[256,128]{1,0:T(8,128)(2,1)} %key_hbm.1, bf16[256,128]{1,0:T(8,128)(2,1)} %value_hbm.1, ...), custom_call_target="tpu_custom_call" | custom-call | tf_op jit(solution)/shard_map/load/pallas_call | solution.py:269
  1.3 3.1 %collective-permute-start = (bf16[512,128]{1,0:T(8,128)(2,1)S(1)}, bf16[512,128]{1,0:T(8,128)(2,1)S(1)}, u32[]{:S(2)}, u32[]{:S(2)}) collective-permute-start(bf16[512,128]{1,0:T(8,128)(2,1)S(1)} %get-tuple-element.25.key_value_ref), channel_id=1, source_target_pairs={{0,8},{4,12},{8,16},{12,20},{16,24},{20,28},{24,0},{28,4},{1,9},{5... | collective-permute-start | bytes 393224 | tf_op jit(solution)/shard_map/ppermute | solution.py:26
  4.4 3.4 %collective-permute-start.2 = (bf16[512,128]{1,0:T(8,128)(2,1)S(1)}, bf16[512,128]{1,0:T(8,128)(2,1)S(1)}, u32[]{:S(2)}, u32[]{:S(2)}) collective-permute-start(bf16[512,128]{1,0:T(8,128)(2,1)S(1)} %get-tuple-element.25.key_value_ref), channel_id=1, source_target_pairs={{0,4},{4,16},{8,12},{12,24},{16,20},{24,28},{1,5},{5,17},{9,13},{1... | collective-permute-start | bytes 393224 | tf_op jit(solution)/shard_map/ppermute | solution.py:292
  7.8 2.2 %own_block.1 = (f32[4,256]{1,0:T(4,128)S(1)}, f32[128,1024]{1,0:T(8,128)S(1)}, f32[512,128]{1,0:T(8,128)S(1)}, bf16[4096,512]{1,0:T(8,128)(2,1)S(1)}) custom-call(bf16[512,128]{1,0:T(8,128)(2,1)S(1)} %get-tuple-element.25.key_value_ref, bf16[256,512]{1,0:T(8,128)(2,1)S(1)} %get-tuple-element.26.query_ref, bf16[256,512]{1,0:T(8,128)(2,1)S(1)} %get-tuple-element.27.grad_ref, ...), custom_call_target="tpu_custom_call" | custom-call | flops 1000000 | bytes 2500 | tf_op jit(solution)/shard_map/own_block/pallas_call | solution.py:306
  10.0 2.6 %collective-permute-start.4 = (bf16[512,128]{1,0:T(8,128)(2,1)S(1)}, bf16[512,128]{1,0:T(8,128)(2,1)S(1)}, u32[]{:S(2)}, u32[]{:S(2)}) collective-permute-start(bf16[512,128]{1,0:T(8,128)(2,1)S(1)} %collective-permute-done.key_value_ref), channel_id=1, source_target_pairs={{0,4},{4,0},{8,12},{12,8},{16,20},{20,16},{24,28},{28,24},{1,5},{5... | collective-permute-start | bytes 393224 | tf_op jit(solution)/shard_map/ppermute | solution.py:26
  12.6 1.6 %block_back_22.1 = (f32[128,1024]{1,0:T(8,128)S(1)}, bf16[512,128]{1,0:T(8,128)(2,1)S(1)}, bf16[4096,128]{1,0:T(8,128)(2,1)S(1)}, bf16[4096,128]{1,0:T(8,128)(2,1)S(1)}) custom-call(bf16[512,128]{1,0:T(8,128)(2,1)S(1)} %collective-permute-done.key_value_ref, bf16[256,512]{1,0:T(8,128)(2,1)S(1)} %get-tuple-element.26.query_ref, ...), custom_call_target="tpu_custom_call" | custom-call | flops 1000000 | bytes 2500 | tf_op jit(solution)/shard_map/block_back_22/pallas_call | solution.py:329
  14.2 0.6 %collective-permute-start.1 = (bf16[512,128]{1,0:T(8,128)(2,1)S(1)}, bf16[512,128]{1,0:T(8,128)(2,1)S(1)}, u32[]{:S(2)}, u32[]{:S(2)}) collective-permute-start(bf16[512,128]{1,0:T(8,128)(2,1)S(1)} %get-tuple-element.36), channel_id=1, source_target_pairs={{0,24},{4,28},{8,0},{12,4},{16,8},{20,12},{24,16},{28,20},{1,25},{... | collective-permute-start | bytes 393224 | tf_op jit(solution)/shard_map/ppermute | solution.py:26
  14.8 1.4 %block_back_31.1 = (f32[128,1024]{1,0:T(8,128)S(1)}, bf16[512,128]{1,0:T(8,128)(2,1)S(1)}) custom-call(bf16[512,128]{1,0:T(8,128)(2,1)S(1)} %collective-permute-done.2.key_value_ref, bf16[256,512]{1,0:T(8,128)(2,1)S(1)} %get-tuple-element.26.query_ref, bf16[256,512]{1,0:T(8,128)(2,1)S(1)} %get-tuple-element.27.grad_ref, ...), custom_call_target="tpu_custom_call" | custom-call | flops 1000000 | bytes 2500 | tf_op jit(solution)/shard_map/block_back_31/pallas_call | solution.py:329
  16.1 1.5 %collective-permute-start.3 = (bf16[512,128]{1,0:T(8,128)(2,1)S(1)}, bf16[512,128]{1,0:T(8,128)(2,1)S(1)}, u32[]{:S(2)}, u32[]{:S(2)}) collective-permute-start(bf16[512,128]{1,0:T(8,128)(2,1)S(1)} %get-tuple-element.38), channel_id=1, source_target_pairs={{0,20},{4,0},{8,28},{12,8},{16,4},{20,16},{24,12},{28,24},{1,21},{... | collective-permute-start | bytes 393224 | tf_op jit(solution)/shard_map/ppermute | solution.py:26
  17.6 1.4 %block_back_13.1 = (bf16[256,512]{1,0:T(8,128)(2,1)S(1)}, bf16[512,128]{1,0:T(8,128)(2,1)S(1)}) custom-call(bf16[512,128]{1,0:T(8,128)(2,1)S(1)} %collective-permute-done.4.key_value_ref, bf16[256,512]{1,0:T(8,128)(2,1)S(1)} %get-tuple-element.26.query_ref, bf16[256,512]{1,0:T(8,128)(2,1)S(1)} %get-tuple-element.27.grad_ref, ...), custom_call_target="tpu_custom_call" | custom-call | flops 1000000 | bytes 2500 | tf_op jit(solution)/shard_map/block_back_13/pallas_call | solution.py:329
  19.1 2.1 %collective-permute-start.5 = (bf16[512,128]{1,0:T(8,128)(2,1)S(1)}, bf16[512,128]{1,0:T(8,128)(2,1)S(1)}, u32[]{:S(2)}, u32[]{:S(2)}) collective-permute-start(bf16[512,128]{1,0:T(8,128)(2,1)S(1)} %get-tuple-element.40), channel_id=1, source_target_pairs={{0,24},{4,28},{8,4},{12,0},{16,12},{20,8},{24,20},{28,16},{1,25},{... | collective-permute-start | bytes 393224 | tf_op jit(solution)/shard_map/ppermute | solution.py:26
  21.2 1.3 %query_term.1.refs_0_.term_ref = f32[4,256,1024]{2,1,0:T(8,128)S(1)} custom-call(bf16[256,512]{1,0:T(8,128)(2,1)S(1)} %get-tuple-element.41.query_ref, bf16[4096,512]{1,0:T(8,128)(2,1)S(1)} %get-tuple-element.42.wq_ref), custom_call_target="tpu_custom_call" | custom-call | flops 671088640 | bytes 1677721 | tf_op jit(solution)/shard_map/query_term/pallas_call | solution.py:351
  22.6 0.0 collective-permute-done.3.right_ref
  22.6 2.4 %collective-permute-done.5.right_ref = bf16[512,128]{1,0:T(8,128)(2,1)S(1)} collective-permute-done((bf16[512,128]{1,0:T(8,128)(2,1)S(1)}, bf16[512,128]{1,0:T(8,128)(2,1)S(1)}, u32[]{:S(2)}, u32[]{:S(2)}) %collective-permute-start.5) | collective-permute-done | bytes 131104 | tf_op jit(solution)/shard_map/ppermute | solution.py:26
  25.0 0.4 term.8.refs_0_
  25.4 0.1 collective-permute-start.7
  25.5 0.3 term.9.refs_0_
  25.8 0.3 term.10.refs_0_
  26.1 0.3 term.11.refs_1_
  26.4 0.7 %collective-permute-done.7.refs_0_ = bf16[256,640]{1,0:T(8,128)(2,1)S(1)} collective-permute-done((bf16[256,640]{1,0:T(8,128)(2,1)S(1)}, bf16[256,640]{1,0:T(8,128)(2,1)S(1)}, u32[]{:S(2)}, u32[]{:S(2)}) %collective-permute-start.7) | collective-permute-done | bytes 327712 | tf_op jit(solution)/shard_map/ppermute | solution.py:26
  27.1 0.3 term.12.refs_1_
  27.4 1.6 %collective-permute-start.8 = (bf16[256,640]{1,0:T(8,128)(2,1)S(1)}, bf16[256,640]{1,0:T(8,128)(2,1)S(1)}, u32[]{:S(2)}, u32[]{:S(2)}) collective-permute-start(bf16[256,640]{1,0:T(8,128)(2,1)S(1)} %term.12.refs_1_), channel_id=1, source_target_pairs={{0,2},{1,3},{2,0},{3,1},{4,6},{5,7},{6,4},{7,5},{8,10},{9,11},{10,... | collective-permute-start | bytes 983048 | tf_op jit(solution)/shard_map/ppermute | solution.py:26
  29.0 0.5 %collective-permute-start.10 = (bf16[256,384]{1,0:T(8,128)(2,1)S(1)}, bf16[256,384]{1,0:T(8,128)(2,1)S(1)}, u32[]{:S(2)}, u32[]{:S(2)}) collective-permute-start(bf16[256,384]{1,0:T(8,128)(2,1)S(1)} %term.9.refs_0_), channel_id=1, source_target_pairs={{0,1},{1,0},{2,3},{3,2},{4,5},{5,4},{6,7},{7,6},{8,9},{9,8},{10,11... | collective-permute-start | bytes 589832 | tf_op jit(solution)/shard_map/ppermute | solution.py:26
  29.5 1.3 %collective-permute-done.10.refs_0_ = bf16[256,384]{1,0:T(8,128)(2,1)S(1)} collective-permute-done((bf16[256,384]{1,0:T(8,128)(2,1)S(1)}, bf16[256,384]{1,0:T(8,128)(2,1)S(1)}, u32[]{:S(2)}, u32[]{:S(2)}) %collective-permute-start.10) | collective-permute-done | bytes 196640 | tf_op jit(solution)/shard_map/ppermute | solution.py:26
  30.8 0.3 term.15
  31.1 0.6 %collective-permute-start.11 = (bf16[256,384]{1,0:T(8,128)(2,1)S(1)}, bf16[256,384]{1,0:T(8,128)(2,1)S(1)}, u32[]{:S(2)}, u32[]{:S(2)}) collective-permute-start(bf16[256,384]{1,0:T(8,128)(2,1)S(1)} %term.15), channel_id=1, source_target_pairs={{0,2},{1,3},{2,0},{3,1},{4,6},{5,7},{6,4},{7,5},{8,10},{9,11},{10,... | collective-permute-start | bytes 589832 | tf_op jit(solution)/shard_map/ppermute | solution.py:26
  31.7 6.4 %collective-permute-done.8.refs_1_.refs_0_ = bf16[256,640]{1,0:T(8,128)(2,1)S(1)} collective-permute-done((bf16[256,640]{1,0:T(8,128)(2,1)S(1)}, bf16[256,640]{1,0:T(8,128)(2,1)S(1)}, u32[]{:S(2)}, u32[]{:S(2)}) %collective-permute-start.8) | collective-permute-done | bytes 327712 | tf_op jit(solution)/shard_map/ppermute | solution.py:26
  38.0 0.3 term.13.low_ref
  38.4 0.3 term.14.high_ref
  38.7 0.8 %finish.2.refs_1_ = bf16[256,1024]{1,0:T(8,128)(2,1)} custom-call(f32[256,512]{1,0:T(8,128)S(1)} %term.13.low_ref, f32[256,512]{1,0:T(8,128)S(1)} %term.14.high_ref, bf16[256,640]{1,0:T(8,128)(2,1)S(1)} %collective-permute-done.8.refs_1_.refs_0_), custom_call_target="tpu_custom_call" | custom-call | flops 1000000 | bytes 2500 | tf_op jit(solution)/shard_map/finish/pallas_call | solution.py:403
  39.5 2.0 %collective-permute-done.11.refs_0_ = bf16[256,384]{1,0:T(8,128)(2,1)S(1)} collective-permute-done((bf16[256,384]{1,0:T(8,128)(2,1)S(1)}, bf16[256,384]{1,0:T(8,128)(2,1)S(1)}, u32[]{:S(2)}, u32[]{:S(2)}) %collective-permute-start.11) | collective-permute-done | bytes 196640 | tf_op jit(solution)/shard_map/ppermute | solution.py:26
  41.5 0.7 %finish.3 = bf16[256,1024]{1,0:T(8,128)(2,1)} custom-call(f32[256,512]{1,0:T(8,128)S(1)} %term.13.low_ref, f32[256,512]{1,0:T(8,128)S(1)} %term.14.high_ref, bf16[256,384]{1,0:T(8,128)(2,1)S(1)} %collective-permute-done.11.refs_0_, bf16[256,1024]{1,0:T(8,128)(2,1)} %finish.2.refs_1_), custom_call_target="tpu_custom_call", output_to_operand_aliasing={{}: (3, {})} | custom-call | flops 1000000 | bytes 2500 | tf_op jit(solution)/shard_map/finish/pallas_call | solution.py:403
  (11 shorter events, 0.1 us)
Async XLA Ops:
  1.3 8.7 %collective-permute-start = (bf16[512,128]{1,0:T(8,128)(2,1)S(1)}, bf16[512,128]{1,0:T(8,128)(2,1)S(1)}, u32[]{:S(2)}, u32[]{:S(2)}) collective-permute-start(bf16[512,128]{1,0:T(8,128)(2,1)S(1)} %get-tuple-element.25.key_value_ref), channel_id=1, source_target_pairs={{0,8},{4,12},{8,16},{12,20},{16,24},{20,28},{24,0},{28,4},{1,9},{5... | collective-permute-start | bytes 393224 | tf_op jit(solution)/shard_map/ppermute | solution.py:26
  4.4 10.4 %collective-permute-start.2 = (bf16[512,128]{1,0:T(8,128)(2,1)S(1)}, bf16[512,128]{1,0:T(8,128)(2,1)S(1)}, u32[]{:S(2)}, u32[]{:S(2)}) collective-permute-start(bf16[512,128]{1,0:T(8,128)(2,1)S(1)} %get-tuple-element.25.key_value_ref), channel_id=1, source_target_pairs={{0,4},{4,16},{8,12},{12,24},{16,20},{24,28},{1,5},{5,17},{9,13},{1... | collective-permute-start | bytes 393224 | tf_op jit(solution)/shard_map/ppermute | solution.py:292
  10.0 7.6 %collective-permute-start.4 = (bf16[512,128]{1,0:T(8,128)(2,1)S(1)}, bf16[512,128]{1,0:T(8,128)(2,1)S(1)}, u32[]{:S(2)}, u32[]{:S(2)}) collective-permute-start(bf16[512,128]{1,0:T(8,128)(2,1)S(1)} %collective-permute-done.key_value_ref), channel_id=1, source_target_pairs={{0,4},{4,0},{8,12},{12,8},{16,20},{20,16},{24,28},{28,24},{1,5},{5... | collective-permute-start | bytes 393224 | tf_op jit(solution)/shard_map/ppermute | solution.py:26
  14.2 8.3 %collective-permute-start.1 = (bf16[512,128]{1,0:T(8,128)(2,1)S(1)}, bf16[512,128]{1,0:T(8,128)(2,1)S(1)}, u32[]{:S(2)}, u32[]{:S(2)}) collective-permute-start(bf16[512,128]{1,0:T(8,128)(2,1)S(1)} %get-tuple-element.36), channel_id=1, source_target_pairs={{0,24},{4,28},{8,0},{12,4},{16,8},{20,12},{24,16},{28,20},{1,25},{... | collective-permute-start | bytes 393224 | tf_op jit(solution)/shard_map/ppermute | solution.py:26
  16.1 6.4 %collective-permute-start.3 = (bf16[512,128]{1,0:T(8,128)(2,1)S(1)}, bf16[512,128]{1,0:T(8,128)(2,1)S(1)}, u32[]{:S(2)}, u32[]{:S(2)}) collective-permute-start(bf16[512,128]{1,0:T(8,128)(2,1)S(1)} %get-tuple-element.38), channel_id=1, source_target_pairs={{0,20},{4,0},{8,28},{12,8},{16,4},{20,16},{24,12},{28,24},{1,21},{... | collective-permute-start | bytes 393224 | tf_op jit(solution)/shard_map/ppermute | solution.py:26
  19.1 5.9 %collective-permute-start.5 = (bf16[512,128]{1,0:T(8,128)(2,1)S(1)}, bf16[512,128]{1,0:T(8,128)(2,1)S(1)}, u32[]{:S(2)}, u32[]{:S(2)}) collective-permute-start(bf16[512,128]{1,0:T(8,128)(2,1)S(1)} %get-tuple-element.40), channel_id=1, source_target_pairs={{0,24},{4,28},{8,4},{12,0},{16,12},{20,8},{24,20},{28,16},{1,25},{... | collective-permute-start | bytes 393224 | tf_op jit(solution)/shard_map/ppermute | solution.py:26
  25.4 1.7 %collective-permute-start.7 = (bf16[256,640]{1,0:T(8,128)(2,1)S(1)}, bf16[256,640]{1,0:T(8,128)(2,1)S(1)}, u32[]{:S(2)}, u32[]{:S(2)}) collective-permute-start(bf16[256,640]{1,0:T(8,128)(2,1)S(1)} %term.8.refs_0_), channel_id=1, source_target_pairs={{0,1},{1,0},{2,3},{3,2},{4,5},{5,4},{6,7},{7,6},{8,9},{9,8},{10,11... | collective-permute-start | bytes 983048 | tf_op jit(solution)/shard_map/ppermute | solution.py:26
  27.4 10.6 %collective-permute-start.8 = (bf16[256,640]{1,0:T(8,128)(2,1)S(1)}, bf16[256,640]{1,0:T(8,128)(2,1)S(1)}, u32[]{:S(2)}, u32[]{:S(2)}) collective-permute-start(bf16[256,640]{1,0:T(8,128)(2,1)S(1)} %term.12.refs_1_), channel_id=1, source_target_pairs={{0,2},{1,3},{2,0},{3,1},{4,6},{5,7},{6,4},{7,5},{8,10},{9,11},{10,... | collective-permute-start | bytes 983048 | tf_op jit(solution)/shard_map/ppermute | solution.py:26
  29.0 2.7 %collective-permute-start.6 = (bf16[256,512]{1,0:T(8,128)(2,1)S(1)}, bf16[256,512]{1,0:T(8,128)(2,1)S(1)}, u32[]{:S(2)}, u32[]{:S(2)}) collective-permute-start(bf16[256,512]{1,0:T(8,128)(2,1)S(1)} %term.10.refs_0_), channel_id=1, source_target_pairs={{0,1},{1,0},{2,3},{3,2},{4,5},{5,4},{6,7},{7,6},{8,9},{9,8},{10,11... | collective-permute-start | bytes 786440 | tf_op jit(solution)/shard_map/ppermute | solution.py:26
  29.0 1.8 %collective-permute-start.10 = (bf16[256,384]{1,0:T(8,128)(2,1)S(1)}, bf16[256,384]{1,0:T(8,128)(2,1)S(1)}, u32[]{:S(2)}, u32[]{:S(2)}) collective-permute-start(bf16[256,384]{1,0:T(8,128)(2,1)S(1)} %term.9.refs_0_), channel_id=1, source_target_pairs={{0,1},{1,0},{2,3},{3,2},{4,5},{5,4},{6,7},{7,6},{8,9},{9,8},{10,11... | collective-permute-start | bytes 589832 | tf_op jit(solution)/shard_map/ppermute | solution.py:26
  29.5 8.8 %collective-permute-start.9 = (bf16[256,512]{1,0:T(8,128)(2,1)S(1)}, bf16[256,512]{1,0:T(8,128)(2,1)S(1)}, u32[]{:S(2)}, u32[]{:S(2)}) collective-permute-start(bf16[256,512]{1,0:T(8,128)(2,1)S(1)} %term.11.refs_1_), channel_id=1, source_target_pairs={{0,1},{1,0},{2,3},{3,2},{4,5},{5,4},{6,7},{7,6},{8,9},{9,8},{10,11... | collective-permute-start | bytes 786440 | tf_op jit(solution)/shard_map/ppermute | solution.py:26
  31.1 10.4 %collective-permute-start.11 = (bf16[256,384]{1,0:T(8,128)(2,1)S(1)}, bf16[256,384]{1,0:T(8,128)(2,1)S(1)}, u32[]{:S(2)}, u32[]{:S(2)}) collective-permute-start(bf16[256,384]{1,0:T(8,128)(2,1)S(1)} %term.15), channel_id=1, source_target_pairs={{0,2},{1,3},{2,0},{3,1},{4,6},{5,7},{6,4},{7,5},{8,10},{9,11},{10,... | collective-permute-start | bytes 589832 | tf_op jit(solution)/shard_map/ppermute | solution.py:26

commit v5 on v4

--- a/solution.py
+++ b/solution.py
@@ -125,17 +125,16 @@
 
 def with_copies(loads, results, refs):
     copies = []
-    for i, (start, size) in enumerate(loads):
-        source = refs[i]
-        copies.append(pltpu.make_async_copy(source, refs[len(loads) + results + i], refs[-1].at[i]))
+    for i in range(loads):
+        copies.append(pltpu.make_async_copy(refs[i], refs[loads + results + i], refs[-1].at[i]))
         copies[-1].start()
-    return refs[len(loads) : len(loads) + results], copies
+    return refs[loads : loads + results], copies
 
 
 def own_kernel(
-    window, heads, loads, key_value_ref, query_ref, grad_ref, output_ref, mix_ref, norm_ref, *refs
+    window, heads, key_value_ref, query_ref, grad_ref, output_ref, mix_ref, norm_ref, delta_ref,
+    total_ref, sums_ref,
 ):
-    (delta_ref, total_ref, sums_ref), copies = with_copies(loads, 3, refs)
     rows, width = key_value_ref.shape[0] // 2, key_value_ref.shape[1]
     lane = lax.broadcasted_iota(i32, (rows, 128), 1)
     packed = jnp.zeros((rows, 128), f32)
@@ -155,8 +154,6 @@
     sums_ref[rows:] = value_sum * f32(keep_scale)
     for head, part in enumerate(query_parts):
         total_ref[:, pl.ds(head * rows, rows)] = part
-    for copy in copies:
-        copy.wait()
 
 
 def pair_kernel(
@@ -184,24 +181,27 @@
         copy.wait()
 
 
-def query_term_kernel(query_ref, wq_ref, out_ref):
+def query_term_kernel(query_ref, wq_ref, wk_ref, wv_ref, out_ref, weight_ref):
+    width = wk_ref.shape[1]
+    weight_ref[:, :width] = wk_ref[...]
+    weight_ref[:, width:] = wv_ref[...]
     places, _, cols = out_ref.shape
     query = query_ref[...]
     for place in range(places):
         out_ref[place] = dot(query, wq_ref[pl.ds(place * cols, cols), :], 1, 1)
 
 
-def term_kernel(pieces, added, sums_ref, term_ref, wk_ref, wv_ref, *refs):
+def term_kernel(pieces, added, sums_ref, term_ref, weight_ref, *refs):
     count, rows, block = term_ref.shape
     me = lax.axis_index("tp")
     out_ref = refs[-1]
-    keys, values = sums_ref[:rows], sums_ref[rows:]
+    sums = sums_ref[...]
     done = 0
     for hop, flip, start, cols in pieces:
         place = lax.rem((me + 1 - 2 * lax.rem(me, 2) if flip else me) + hop, count)
         at = pl.ds(pl.multiple_of(place * block + start, 128), cols)
         total = term_ref[place, :, pl.ds(start, cols)]
-        total = total + dot(keys, wk_ref[at, :], 1, 1) + dot(values, wv_ref[at, :], 1, 1)
+        total = total + dot(sums, weight_ref[at, :], 1, 1)
         if added is not None:
             total = total + refs[0][:, pl.ds(added + done, cols)].astype(f32)
         out_ref[:, pl.ds(done, cols)] = total.astype(out_ref.dtype)
@@ -224,7 +224,17 @@
 
 def add_kernel(left_ref, right_ref, *refs):
     out_ref = refs[-1]
-    out_ref[...] = (left_ref[...] + right_ref[...].astype(f32)).astype(out_ref.dtype)
+    total = (left_ref[...] + right_ref[...].astype(f32)).astype(out_ref.dtype)
+    rows = out_ref.shape[0]
+    if rows == total.shape[0]:
+        out_ref[...] = total
+    else:
+        out_ref[...] = jnp.concatenate([total[:rows], total[rows:]], axis=1)
+
+
+def sum_kernel(first, left_ref, right_ref, out_ref):
+    at = pl.ds(first, out_ref.shape[1])
+    out_ref[...] = (left_ref[:, at] + right_ref[:, at].astype(f32)).astype(bf16)
 
 
 def finish_kernel(first, hops, low_ref, high_ref, *refs):
@@ -292,54 +302,40 @@
     mixed = lax.ppermute(key_value, "ctx", [pair for pair in pairs if pair[1] < count])
     block_cost = cost(20 * heads * rows * rows * width)
 
-    all_rows = (0, q_weight.shape[0])
-    loads = (
-        ((q_weight,), (all_rows,)),
-        ((k_weight, v_weight), (all_rows,) * 2),
-        ((), ()),
-        ((), ()),
-    )
-
-    def loaded(load):
-        return [shape((size, item.shape[1]), bf16) for item, (_, size) in zip(*load)]
-
-    deltas, total, sums, *q_low = pl.pallas_call(
-        functools.partial(own_kernel, window, heads, loads[0][1]),
-        in_specs=[in_vmem] * 6 + [in_hbm] * len(loads[0][0]),
-        out_specs=[in_vmem] * (3 + len(loads[0][0])),
+    deltas, total, sums = pl.pallas_call(
+        functools.partial(own_kernel, window, heads),
+        in_specs=[in_vmem] * 6,
+        out_specs=[in_vmem] * 3,
         out_shape=[
             shape((heads, rows), f32),
             shape((width, heads * rows), f32),
             shape((2 * rows, width), f32),
-            *loaded(loads[0]),
         ],
-        scratch_shapes=[pltpu.SemaphoreType.DMA((len(loads[0][0]),))],
         compiler_params=params,
         cost_estimate=cost(10**6),
         name="own_block",
-    )(key_value, query, grad, output, mix, norms, *map(from_hbm, loads[0][0]))
+    )(key_value, query, grad, output, mix, norms)
 
     straight, deltas = lax.optimization_barrier((straight, deltas))
     crossed = moved(straight, "ctx", lambda i: i ^ 1)
-    returned, held = [], [*q_low]
-    for load, offsets, arrived in zip(
-        loads[1:], ((2, 2), (3, 1), (1, 3)), (straight, mixed, crossed)
-    ):
+    returned, held = [], []
+    for offsets, arrived in (((2, 2), straight), ((3, 1), mixed), ((1, 3), crossed)):
+        load = () if held else (k_weight, v_weight)
         last = offsets == (1, 3)
         total, parts, *more = pl.pallas_call(
-            functools.partial(pair_kernel, offsets, window, heads, load[1], last),
-            in_specs=[in_vmem] * 7 + [in_hbm] * len(load[0]),
-            out_specs=[in_vmem] * (2 + len(load[0])),
+            functools.partial(pair_kernel, offsets, window, heads, len(load), last),
+            in_specs=[in_vmem] * 7 + [in_hbm] * len(load),
+            out_specs=[in_vmem] * (2 + len(load)),
             out_shape=[
                 shape((rows, heads * width), bf16) if last else shape((width, heads * rows), f32),
                 shape((2 * rows, width), bf16),
-                *loaded(load),
+                *[shape(item.shape, bf16) for item in load],
             ],
-            scratch_shapes=[pltpu.SemaphoreType.DMA((len(load[0]),))] * (len(load[0]) > 0),
+            scratch_shapes=[pltpu.SemaphoreType.DMA((len(load),))] * (len(load) > 0),
             compiler_params=params,
             cost_estimate=cost(10**6),
             name="block_back_%d%d" % offsets,
-        )(arrived, query, grad, mix, norms, deltas, total, *map(from_hbm, load[0]))
+        )(arrived, query, grad, mix, norms, deltas, total, *map(from_hbm, load))
         held.extend(more)
         even, odd = offsets
         shift = offsets == (1, 3)
@@ -348,28 +344,31 @@
         )
 
     cols = q_weight.shape[0] // tp_size
-    query_term = pl.pallas_call(
+    query_term, weights = pl.pallas_call(
         query_term_kernel,
-        in_specs=[in_vmem] * 2,
-        out_specs=in_vmem,
-        out_shape=shape((tp_size, rows, cols), f32),
+        in_specs=[in_vmem] * 4,
+        out_specs=[in_vmem] * 2,
+        out_shape=[
+            shape((tp_size, rows, cols), f32),
+            shape((q_weight.shape[0], 2 * width), bf16),
+        ],
         compiler_params=params,
         cost_estimate=block_cost,
         name="query_term",
-    )(total, held[0])
+    )(total, q_weight, *held)
     for item in returned:
         final = item is returned[-1]
         sums = pl.pallas_call(
             add_kernel,
             in_specs=[in_vmem] * (3 if final else 2),
             out_specs=in_vmem,
-            out_shape=shape(sums.shape, bf16 if final else f32),
+            out_shape=shape((rows, 2 * width), bf16) if final else shape(sums.shape, f32),
             compiler_params=params,
             cost_estimate=block_cost,
             name="add_returned",
         )(sums, item, *((query_term,) if final else ()))
 
-    operands = (sums, query_term, *held[1:])
+    operands = (sums, query_term, weights)
     hops = range(2, tp_size, 2)
     sizes = (cols * 5 // 8, cols * 3 // 8) if cols % 1024 == 0 else (cols // 2,) * 2
     starts = (0, sizes[0])
@@ -387,13 +386,26 @@
         after = (part,)
     part, swapped_low = swapped_term([(0, 0, cols // 2)], after)
     part, swapped_high = swapped_term([(0, cols // 2, cols // 2)], (part,))
-    sent, after = [[], []], (part,)
-    for i in range(2):
-        for j, hop in enumerate(hops):
-            piece = ((hop, False, starts[i], sizes[i]),)
-            part = term(piece, operands, (swapped[i], j * sizes[i]), after, bf16, low, params)
-            sent[i].append(moved(part, "tp", lambda k: k + hop))
-            after = (part,)
+    pieces = [(hop, False, starts[0], sizes[0]) for hop in hops]
+    ahead = term(pieces, operands, None, (part,), f32, low, params)
+    sent, after = [[], []], ()
+    for j, hop in enumerate(hops):
+        part = pl.pallas_call(
+            functools.partial(sum_kernel, j * sizes[0]),
+            in_specs=[in_vmem] * 2,
+            out_specs=in_vmem,
+            out_shape=shape((rows, sizes[0]), bf16),
+            compiler_params=params,
+            cost_estimate=cost(low),
+            name="sum",
+        )(ahead, swapped[0])
+        sent[0].append(moved(part, "tp", lambda k: k + hop))
+        after = (part,)
+    for j, hop in enumerate(hops):
+        piece = ((hop, False, starts[1], sizes[1]),)
+        part = term(piece, operands, (swapped[1], j * sizes[1]), after, bf16, low, params)
+        sent[1].append(moved(part, "tp", lambda k: k + hop))
+        after = (part,)
     mine = [
         term(((0, False, j * (cols // 2), cols // 2),), operands, (item, 0), tuple(sent[0][:1]), f32, 10 * high, params)
         for j, item in enumerate((swapped_low, swapped_high))

time: 42.5 us -> 42 us (0.988)
    pallas_call x5 -> x6, Pallas kernels: 7.87 us -> 7.51 us  [the longest x3 4.38 us: on_device(): pl.pallas_call(functools.partial(pair_kernel, offsets, window, heads, len...]
  transfers between devices with their start and end apart: 12 -> 12, of which waited for: 5 -> 6; matrix products, arithmetic and copies ran while one was open for 0% -> 0% of each run, Pallas kernels for 25% -> 24%
where the time goes in v5:
time: 42 us; the launch traced here: 41.8 us
  starting transfers between devices  16.2 us (39%)
  Pallas kernels  12.8 us (30%)
  waiting for transfers between devices  12.7 us (30%)
    ppermute x11, starting transfers between devices, moved(): lax.ppermute(array, axis, [(i, place(i) % count) for i in range(count)])  12.8 us
    ppermute x11, waiting for transfers between devices, moved(): lax.ppermute(array, axis, [(i, place(i) % count) for i in range(count)])  12.7 us
    pallas_call x3, Pallas kernels, on_device(): pl.pallas_call(functools.partial(pair_kernel, offsets, window, heads, len...  4.38 us
    ppermute x1, starting transfers between devices, on_device(): lax.ppermute(key_value, 'ctx', [pair for pair in pairs if pair[1] < count])  3.39 us
    pallas_call x8, Pallas kernels, term(): pl.pallas_call(functools.partial(term_kernel, pieces, first), in_specs=[i...  2.23 us
    pallas_call x1, Pallas kernels, on_device(): pl.pallas_call(query_term_kernel, in_specs=[in_vmem] * 4, out_specs=[in_v...  1.64 us
    pallas_call x2, Pallas kernels, on_device(): pl.pallas_call(functools.partial(finish_kernel, starts[i], len(hops)), in...  1.54 us
    pallas_call x1, Pallas kernels, on_device(): pl.pallas_call(functools.partial(own_kernel, window, heads), in_specs=[in...  1.43 us
  transfers between devices with their start and end apart: 12, of which 6 were waited for; matrix products, arithmetic and copies ran while one was open for 0% of the time, Pallas kernels for 24%

profile of v5, /device:TPU:0, one launch (start us, length us, event | category | flops | bytes accessed | tf_op | source)
XLA Modules:
  0.0 41.8 jit_solution(6531158479221738039)
XLA Ops:
  0.0 1.4 %load.1 = (bf16[512,128]{1,0:T(8,128)(2,1)S(1)}, bf16[256,512]{1,0:T(8,128)(2,1)S(1)}, bf16[256,512]{1,0:T(8,128)(2,1)S(1)}, bf16[256,512]{1,0:T(8,128)(2,1)S(1)...) custom-call(bf16[256,128]{1,0:T(8,128)(2,1)} %key_hbm.1, bf16[256,128]{1,0:T(8,128)(2,1)} %value_hbm.1, ...), custom_call_target="tpu_custom_call" | custom-call | tf_op jit(solution)/shard_map/load/pallas_call | solution.py:279
  1.4 3.1 %collective-permute-start = (bf16[512,128]{1,0:T(8,128)(2,1)S(1)}, bf16[512,128]{1,0:T(8,128)(2,1)S(1)}, u32[]{:S(2)}, u32[]{:S(2)}) collective-permute-start(bf16[512,128]{1,0:T(8,128)(2,1)S(1)} %get-tuple-element.26.key_value_ref), channel_id=1, source_target_pairs={{0,8},{4,12},{8,16},{12,20},{16,24},{20,28},{24,0},{28,4},{1,9},{5... | collective-permute-start | bytes 393224 | tf_op jit(solution)/shard_map/ppermute | solution.py:26
  4.5 3.4 %collective-permute-start.2 = (bf16[512,128]{1,0:T(8,128)(2,1)S(1)}, bf16[512,128]{1,0:T(8,128)(2,1)S(1)}, u32[]{:S(2)}, u32[]{:S(2)}) collective-permute-start(bf16[512,128]{1,0:T(8,128)(2,1)S(1)} %get-tuple-element.26.key_value_ref), channel_id=1, source_target_pairs={{0,4},{4,16},{8,12},{12,24},{16,20},{24,28},{1,5},{5,17},{9,13},{1... | collective-permute-start | bytes 393224 | tf_op jit(solution)/shard_map/ppermute | solution.py:302
  7.9 1.4 %own_block.1 = (f32[4,256]{1,0:T(4,128)S(1)}, f32[128,1024]{1,0:T(8,128)S(1)}, f32[512,128]{1,0:T(8,128)S(1)}) custom-call(bf16[512,128]{1,0:T(8,128)(2,1)S(1)} %get-tuple-element.26.key_value_ref, bf16[256,512]{1,0:T(8,128)(2,1)S(1)} %get-tuple-element.27.query_ref, bf16[256,512]{1,0:T(8,128)(2,1)S(1)} %get-tuple-element.28.grad_ref, ...), custom_call_target="tpu_custom_call" | custom-call | flops 1000000 | bytes 2500 | tf_op jit(solution)/shard_map/own_block/pallas_call | solution.py:305
  9.3 0.7 %collective-permute-done.key_value_ref = bf16[512,128]{1,0:T(8,128)(2,1)S(1)} collective-permute-done((bf16[512,128]{1,0:T(8,128)(2,1)S(1)}, bf16[512,128]{1,0:T(8,128)(2,1)S(1)}, u32[]{:S(2)}, u32[]{:S(2)}) %collective-permute-start) | collective-permute-done | bytes 131104 | tf_op jit(solution)/shard_map/ppermute | solution.py:26
  10.0 1.9 %collective-permute-start.4 = (bf16[512,128]{1,0:T(8,128)(2,1)S(1)}, bf16[512,128]{1,0:T(8,128)(2,1)S(1)}, u32[]{:S(2)}, u32[]{:S(2)}) collective-permute-start(bf16[512,128]{1,0:T(8,128)(2,1)S(1)} %collective-permute-done.key_value_ref), channel_id=1, source_target_pairs={{0,4},{4,0},{8,12},{12,8},{16,20},{20,16},{24,28},{28,24},{1,5},{5... | collective-permute-start | bytes 393224 | tf_op jit(solution)/shard_map/ppermute | solution.py:26
  12.0 1.6 %block_back_22.1 = (f32[128,1024]{1,0:T(8,128)S(1)}, bf16[512,128]{1,0:T(8,128)(2,1)S(1)}, bf16[4096,128]{1,0:T(8,128)(2,1)S(1)}, bf16[4096,128]{1,0:T(8,128)(2,1)S(1)}) custom-call(bf16[512,128]{1,0:T(8,128)(2,1)S(1)} %collective-permute-done.key_value_ref, bf16[256,512]{1,0:T(8,128)(2,1)S(1)} %get-tuple-element.27.query_ref, ...), custom_call_target="tpu_custom_call" | custom-call | flops 1000000 | bytes 2500 | tf_op jit(solution)/shard_map/block_back_22/pallas_call | solution.py:325
  13.5 1.3 %collective-permute-start.1 = (bf16[512,128]{1,0:T(8,128)(2,1)S(1)}, bf16[512,128]{1,0:T(8,128)(2,1)S(1)}, u32[]{:S(2)}, u32[]{:S(2)}) collective-permute-start(bf16[512,128]{1,0:T(8,128)(2,1)S(1)} %get-tuple-element.37), channel_id=1, source_target_pairs={{0,24},{4,28},{8,0},{12,4},{16,8},{20,12},{24,16},{28,20},{1,25},{... | collective-permute-start | bytes 393224 | tf_op jit(solution)/shard_map/ppermute | solution.py:26
  14.9 1.4 %block_back_31.1 = (f32[128,1024]{1,0:T(8,128)S(1)}, bf16[512,128]{1,0:T(8,128)(2,1)S(1)}) custom-call(bf16[512,128]{1,0:T(8,128)(2,1)S(1)} %collective-permute-done.2.key_value_ref, bf16[256,512]{1,0:T(8,128)(2,1)S(1)} %get-tuple-element.27.query_ref, bf16[256,512]{1,0:T(8,128)(2,1)S(1)} %get-tuple-element.28.grad_ref, ...), custom_call_target="tpu_custom_call" | custom-call | flops 1000000 | bytes 2500 | tf_op jit(solution)/shard_map/block_back_31/pallas_call | solution.py:325
  16.3 1.3 %collective-permute-start.3 = (bf16[512,128]{1,0:T(8,128)(2,1)S(1)}, bf16[512,128]{1,0:T(8,128)(2,1)S(1)}, u32[]{:S(2)}, u32[]{:S(2)}) collective-permute-start(bf16[512,128]{1,0:T(8,128)(2,1)S(1)} %get-tuple-element.39), channel_id=1, source_target_pairs={{0,20},{4,0},{8,28},{12,8},{16,4},{20,16},{24,12},{28,24},{1,21},{... | collective-permute-start | bytes 393224 | tf_op jit(solution)/shard_map/ppermute | solution.py:26
  17.6 1.4 %block_back_13.1 = (bf16[256,512]{1,0:T(8,128)(2,1)S(1)}, bf16[512,128]{1,0:T(8,128)(2,1)S(1)}) custom-call(bf16[512,128]{1,0:T(8,128)(2,1)S(1)} %collective-permute-done.4.key_value_ref, bf16[256,512]{1,0:T(8,128)(2,1)S(1)} %get-tuple-element.27.query_ref, bf16[256,512]{1,0:T(8,128)(2,1)S(1)} %get-tuple-element.28.grad_ref, ...), custom_call_target="tpu_custom_call" | custom-call | flops 1000000 | bytes 2500 | tf_op jit(solution)/shard_map/block_back_13/pallas_call | solution.py:325
  19.0 2.4 %collective-permute-start.5 = (bf16[512,128]{1,0:T(8,128)(2,1)S(1)}, bf16[512,128]{1,0:T(8,128)(2,1)S(1)}, u32[]{:S(2)}, u32[]{:S(2)}) collective-permute-start(bf16[512,128]{1,0:T(8,128)(2,1)S(1)} %get-tuple-element.41), channel_id=1, source_target_pairs={{0,24},{4,28},{8,4},{12,0},{16,12},{20,8},{24,20},{28,16},{1,25},{... | collective-permute-start | bytes 393224 | tf_op jit(solution)/shard_map/ppermute | solution.py:26
  21.4 1.6 %query_term.1 = (f32[4,256,1024]{2,1,0:T(8,128)S(1)}, bf16[4096,256]{1,0:T(8,128)(2,1)S(1)}) custom-call(bf16[256,512]{1,0:T(8,128)(2,1)S(1)} %get-tuple-element.42.query_ref, bf16[4096,512]{1,0:T(8,128)(2,1)S(1)} %copy-done, bf16[4096,128]{1,0:T(8,128)(2,1)S(1)} %get-tuple-element.43.wk_ref, bf16[4096,128]{1,0:T(8,128)(2,1)S(1)} %get-tuple-element.44.wv_ref), custom_call_target="tpu_custom_call" | custom-call | flops 671088640 | bytes 1677721 | tf_op jit(solution)/shard_map/query_term/pallas_call | solution.py:347
  23.1 1.8 %collective-permute-done.5.right_ref = bf16[512,128]{1,0:T(8,128)(2,1)S(1)} collective-permute-done((bf16[512,128]{1,0:T(8,128)(2,1)S(1)}, bf16[512,128]{1,0:T(8,128)(2,1)S(1)}, u32[]{:S(2)}, u32[]{:S(2)}) %collective-permute-start.5) | collective-permute-done | bytes 131104 | tf_op jit(solution)/shard_map/ppermute | solution.py:26
  25.0 0.3 term.8.refs_0_
  25.3 0.1 collective-permute-start.7
  25.4 0.3 term.9.refs_0_
  25.7 0.3 term.10.refs_0_
  25.9 0.3 term.11.refs_0_
  26.2 0.3 term.12.left_ref
  26.5 0.5 %collective-permute-done.7.right_ref = bf16[256,640]{1,0:T(8,128)(2,1)S(1)} collective-permute-done((bf16[256,640]{1,0:T(8,128)(2,1)S(1)}, bf16[256,640]{1,0:T(8,128)(2,1)S(1)}, u32[]{:S(2)}, u32[]{:S(2)}) %collective-permute-start.7) | collective-permute-done | bytes 327712 | tf_op jit(solution)/shard_map/ppermute | solution.py:26
  27.1 1.6 %collective-permute-start.8 = (bf16[256,640]{1,0:T(8,128)(2,1)S(1)}, bf16[256,640]{1,0:T(8,128)(2,1)S(1)}, u32[]{:S(2)}, u32[]{:S(2)}) collective-permute-start(bf16[256,640]{1,0:T(8,128)(2,1)S(1)} %sum.1.refs_1_), channel_id=1, source_target_pairs={{0,2},{1,3},{2,0},{3,1},{4,6},{5,7},{6,4},{7,5},{8,10},{9,11},{10,... | collective-permute-start | bytes 983048 | tf_op jit(solution)/shard_map/ppermute | solution.py:26
  28.7 0.5 %collective-permute-start.10 = (bf16[256,384]{1,0:T(8,128)(2,1)S(1)}, bf16[256,384]{1,0:T(8,128)(2,1)S(1)}, u32[]{:S(2)}, u32[]{:S(2)}) collective-permute-start(bf16[256,384]{1,0:T(8,128)(2,1)S(1)} %term.9.refs_0_), channel_id=1, source_target_pairs={{0,1},{1,0},{2,3},{3,2},{4,5},{5,4},{6,7},{7,6},{8,9},{9,8},{10,11... | collective-permute-start | bytes 589832 | tf_op jit(solution)/shard_map/ppermute | solution.py:26
  29.2 1.3 %collective-permute-done.10.refs_0_ = bf16[256,384]{1,0:T(8,128)(2,1)S(1)} collective-permute-done((bf16[256,384]{1,0:T(8,128)(2,1)S(1)}, bf16[256,384]{1,0:T(8,128)(2,1)S(1)}, u32[]{:S(2)}, u32[]{:S(2)}) %collective-permute-start.10) | collective-permute-done | bytes 196640 | tf_op jit(solution)/shard_map/ppermute | solution.py:26
  30.5 0.3 term.15
  30.7 0.6 %collective-permute-start.11 = (bf16[256,384]{1,0:T(8,128)(2,1)S(1)}, bf16[256,384]{1,0:T(8,128)(2,1)S(1)}, u32[]{:S(2)}, u32[]{:S(2)}) collective-permute-start(bf16[256,384]{1,0:T(8,128)(2,1)S(1)} %term.15), channel_id=1, source_target_pairs={{0,2},{1,3},{2,0},{3,1},{4,6},{5,7},{6,4},{7,5},{8,10},{9,11},{10,... | collective-permute-start | bytes 589832 | tf_op jit(solution)/shard_map/ppermute | solution.py:26
  31.3 6.4 %collective-permute-done.8.refs_1_.refs_0_ = bf16[256,640]{1,0:T(8,128)(2,1)S(1)} collective-permute-done((bf16[256,640]{1,0:T(8,128)(2,1)S(1)}, bf16[256,640]{1,0:T(8,128)(2,1)S(1)}, u32[]{:S(2)}, u32[]{:S(2)}) %collective-permute-start.8) | collective-permute-done | bytes 327712 | tf_op jit(solution)/shard_map/ppermute | solution.py:26
  37.7 0.3 term.14.high_ref
  38.0 0.3 term.13.low_ref
  38.2 0.8 %finish.2.refs_1_ = bf16[256,1024]{1,0:T(8,128)(2,1)} custom-call(f32[256,512]{1,0:T(8,128)S(1)} %term.13.low_ref, f32[256,512]{1,0:T(8,128)S(1)} %term.14.high_ref, bf16[256,640]{1,0:T(8,128)(2,1)S(1)} %collective-permute-done.8.refs_1_.refs_0_), custom_call_target="tpu_custom_call" | custom-call | flops 1000000 | bytes 2500 | tf_op jit(solution)/shard_map/finish/pallas_call | solution.py:415
  39.1 2.0 %collective-permute-done.11.refs_0_ = bf16[256,384]{1,0:T(8,128)(2,1)S(1)} collective-permute-done((bf16[256,384]{1,0:T(8,128)(2,1)S(1)}, bf16[256,384]{1,0:T(8,128)(2,1)S(1)}, u32[]{:S(2)}, u32[]{:S(2)}) %collective-permute-start.11) | collective-permute-done | bytes 196640 | tf_op jit(solution)/shard_map/ppermute | solution.py:26
  41.1 0.7 %finish.3 = bf16[256,1024]{1,0:T(8,128)(2,1)} custom-call(f32[256,512]{1,0:T(8,128)S(1)} %term.13.low_ref, f32[256,512]{1,0:T(8,128)S(1)} %term.14.high_ref, bf16[256,384]{1,0:T(8,128)(2,1)S(1)} %collective-permute-done.11.refs_0_, bf16[256,1024]{1,0:T(8,128)(2,1)} %finish.2.refs_1_), custom_call_target="tpu_custom_call", output_to_operand_aliasing={{}: (3, {})} | custom-call | flops 1000000 | bytes 2500 | tf_op jit(solution)/shard_map/finish/pallas_call | solution.py:415
  (14 shorter events, 0.2 us)
Async XLA Ops:
  0.0 21.4 %copy-start = (bf16[4096,512]{1,0:T(8,128)(2,1)S(1)}, bf16[4096,512]{1,0:T(8,128)(2,1)}, u32[]{:S(2)}) copy-start(bf16[4096,512]{1,0:T(8,128)(2,1)} %wq_ref.1) | copy-start | bytes 12582916
  1.4 8.6 %collective-permute-start = (bf16[512,128]{1,0:T(8,128)(2,1)S(1)}, bf16[512,128]{1,0:T(8,128)(2,1)S(1)}, u32[]{:S(2)}, u32[]{:S(2)}) collective-permute-start(bf16[512,128]{1,0:T(8,128)(2,1)S(1)} %get-tuple-element.26.key_value_ref), channel_id=1, source_target_pairs={{0,8},{4,12},{8,16},{12,20},{16,24},{20,28},{24,0},{28,4},{1,9},{5... | collective-permute-start | bytes 393224 | tf_op jit(solution)/shard_map/ppermute | solution.py:26
  4.5 10.4 %collective-permute-start.2 = (bf16[512,128]{1,0:T(8,128)(2,1)S(1)}, bf16[512,128]{1,0:T(8,128)(2,1)S(1)}, u32[]{:S(2)}, u32[]{:S(2)}) collective-permute-start(bf16[512,128]{1,0:T(8,128)(2,1)S(1)} %get-tuple-element.26.key_value_ref), channel_id=1, source_target_pairs={{0,4},{4,16},{8,12},{12,24},{16,20},{24,28},{1,5},{5,17},{9,13},{1... | collective-permute-start | bytes 393224 | tf_op jit(solution)/shard_map/ppermute | solution.py:302
  10.0 7.6 %collective-permute-start.4 = (bf16[512,128]{1,0:T(8,128)(2,1)S(1)}, bf16[512,128]{1,0:T(8,128)(2,1)S(1)}, u32[]{:S(2)}, u32[]{:S(2)}) collective-permute-start(bf16[512,128]{1,0:T(8,128)(2,1)S(1)} %collective-permute-done.key_value_ref), channel_id=1, source_target_pairs={{0,4},{4,0},{8,12},{12,8},{16,20},{20,16},{24,28},{28,24},{1,5},{5... | collective-permute-start | bytes 393224 | tf_op jit(solution)/shard_map/ppermute | solution.py:26
  13.5 9.5 %collective-permute-start.1 = (bf16[512,128]{1,0:T(8,128)(2,1)S(1)}, bf16[512,128]{1,0:T(8,128)(2,1)S(1)}, u32[]{:S(2)}, u32[]{:S(2)}) collective-permute-start(bf16[512,128]{1,0:T(8,128)(2,1)S(1)} %get-tuple-element.37), channel_id=1, source_target_pairs={{0,24},{4,28},{8,0},{12,4},{16,8},{20,12},{24,16},{28,20},{1,25},{... | collective-permute-start | bytes 393224 | tf_op jit(solution)/shard_map/ppermute | solution.py:26
  16.3 6.8 %collective-permute-start.3 = (bf16[512,128]{1,0:T(8,128)(2,1)S(1)}, bf16[512,128]{1,0:T(8,128)(2,1)S(1)}, u32[]{:S(2)}, u32[]{:S(2)}) collective-permute-start(bf16[512,128]{1,0:T(8,128)(2,1)S(1)} %get-tuple-element.39), channel_id=1, source_target_pairs={{0,20},{4,0},{8,28},{12,8},{16,4},{20,16},{24,12},{28,24},{1,21},{... | collective-permute-start | bytes 393224 | tf_op jit(solution)/shard_map/ppermute | solution.py:26
  19.0 5.9 %collective-permute-start.5 = (bf16[512,128]{1,0:T(8,128)(2,1)S(1)}, bf16[512,128]{1,0:T(8,128)(2,1)S(1)}, u32[]{:S(2)}, u32[]{:S(2)}) collective-permute-start(bf16[512,128]{1,0:T(8,128)(2,1)S(1)} %get-tuple-element.41), channel_id=1, source_target_pairs={{0,24},{4,28},{8,4},{12,0},{16,12},{20,8},{24,20},{28,16},{1,25},{... | collective-permute-start | bytes 393224 | tf_op jit(solution)/shard_map/ppermute | solution.py:26
  25.3 1.7 %collective-permute-start.7 = (bf16[256,640]{1,0:T(8,128)(2,1)S(1)}, bf16[256,640]{1,0:T(8,128)(2,1)S(1)}, u32[]{:S(2)}, u32[]{:S(2)}) collective-permute-start(bf16[256,640]{1,0:T(8,128)(2,1)S(1)} %term.8.refs_0_), channel_id=1, source_target_pairs={{0,1},{1,0},{2,3},{3,2},{4,5},{5,4},{6,7},{7,6},{8,9},{9,8},{10,11... | collective-permute-start | bytes 983048 | tf_op jit(solution)/shard_map/ppermute | solution.py:26
  27.1 10.6 %collective-permute-start.8 = (bf16[256,640]{1,0:T(8,128)(2,1)S(1)}, bf16[256,640]{1,0:T(8,128)(2,1)S(1)}, u32[]{:S(2)}, u32[]{:S(2)}) collective-permute-start(bf16[256,640]{1,0:T(8,128)(2,1)S(1)} %sum.1.refs_1_), channel_id=1, source_target_pairs={{0,2},{1,3},{2,0},{3,1},{4,6},{5,7},{6,4},{7,5},{8,10},{9,11},{10,... | collective-permute-start | bytes 983048 | tf_op jit(solution)/shard_map/ppermute | solution.py:26
  28.7 2.6 %collective-permute-start.9 = (bf16[256,512]{1,0:T(8,128)(2,1)S(1)}, bf16[256,512]{1,0:T(8,128)(2,1)S(1)}, u32[]{:S(2)}, u32[]{:S(2)}) collective-permute-start(bf16[256,512]{1,0:T(8,128)(2,1)S(1)} %term.11.refs_0_), channel_id=1, source_target_pairs={{0,1},{1,0},{2,3},{3,2},{4,5},{5,4},{6,7},{7,6},{8,9},{9,8},{10,11... | collective-permute-start | bytes 786440 | tf_op jit(solution)/shard_map/ppermute | solution.py:26
  28.7 1.8 %collective-permute-start.10 = (bf16[256,384]{1,0:T(8,128)(2,1)S(1)}, bf16[256,384]{1,0:T(8,128)(2,1)S(1)}, u32[]{:S(2)}, u32[]{:S(2)}) collective-permute-start(bf16[256,384]{1,0:T(8,128)(2,1)S(1)} %term.9.refs_0_), channel_id=1, source_target_pairs={{0,1},{1,0},{2,3},{3,2},{4,5},{5,4},{6,7},{7,6},{8,9},{9,8},{10,11... | collective-permute-start | bytes 589832 | tf_op jit(solution)/shard_map/ppermute | solution.py:26
  29.2 8.8 %collective-permute-start.6 = (bf16[256,512]{1,0:T(8,128)(2,1)S(1)}, bf16[256,512]{1,0:T(8,128)(2,1)S(1)}, u32[]{:S(2)}, u32[]{:S(2)}) collective-permute-start(bf16[256,512]{1,0:T(8,128)(2,1)S(1)} %term.10.refs_0_), channel_id=1, source_target_pairs={{0,1},{1,0},{2,3},{3,2},{4,5},{5,4},{6,7},{7,6},{8,9},{9,8},{10,11... | collective-permute-start | bytes 786440 | tf_op jit(solution)/shard_map/ppermute | solution.py:26
  30.7 10.4 %collective-permute-start.11 = (bf16[256,384]{1,0:T(8,128)(2,1)S(1)}, bf16[256,384]{1,0:T(8,128)(2,1)S(1)}, u32[]{:S(2)}, u32[]{:S(2)}) collective-permute-start(bf16[256,384]{1,0:T(8,128)(2,1)S(1)} %term.15), channel_id=1, source_target_pairs={{0,2},{1,3},{2,0},{3,1},{4,6},{5,7},{6,4},{7,5},{8,10},{9,11},{10,... | collective-permute-start | bytes 589832 | tf_op jit(solution)/shard_map/ppermute | solution.py:26

commit v6 on v5

--- a/solution.py
+++ b/solution.py
@@ -181,13 +181,19 @@
         copy.wait()
 
 
-def query_term_kernel(query_ref, wq_ref, wk_ref, wv_ref, out_ref, weight_ref):
+def query_term_kernel(query_ref, wk_ref, wv_ref, wq_hbm, out_ref, weight_ref, wq_ref, sems):
     width = wk_ref.shape[1]
+    places, _, cols = out_ref.shape
+    copies = []
+    for place in range(places):
+        at = pl.ds(place * cols, cols)
+        copies.append(pltpu.make_async_copy(wq_hbm.at[at], wq_ref.at[at], sems.at[place]))
+        copies[-1].start()
     weight_ref[:, :width] = wk_ref[...]
     weight_ref[:, width:] = wv_ref[...]
-    places, _, cols = out_ref.shape
     query = query_ref[...]
-    for place in range(places):
+    for place, copy in enumerate(copies):
+        copy.wait()
         out_ref[place] = dot(query, wq_ref[pl.ds(place * cols, cols), :], 1, 1)
 
 
@@ -346,16 +352,20 @@
     cols = q_weight.shape[0] // tp_size
     query_term, weights = pl.pallas_call(
         query_term_kernel,
-        in_specs=[in_vmem] * 4,
+        in_specs=[in_vmem] * 3 + [in_hbm],
         out_specs=[in_vmem] * 2,
         out_shape=[
             shape((tp_size, rows, cols), f32),
             shape((q_weight.shape[0], 2 * width), bf16),
         ],
+        scratch_shapes=[
+            pltpu.VMEM(q_weight.shape, bf16),
+            pltpu.SemaphoreType.DMA((tp_size,)),
+        ],
         compiler_params=params,
         cost_estimate=block_cost,
         name="query_term",
-    )(total, q_weight, *held)
+    )(total, *held, from_hbm(q_weight))
     for item in returned:
         final = item is returned[-1]
         sums = pl.pallas_call(

time: 42 us -> 41.9 us (level)
  Pallas kernels: 12.8 us -> 14.2 us
  waiting for transfers between devices: 12.7 us -> 11.3 us
    pallas_call x1, Pallas kernels: 1.64 us -> 3.14 us  [on_device(): pl.pallas_call(query_term_kernel, in_specs=[in_vmem] * 3 + [in_hbm], out_...]
    ppermute x11, waiting for transfers between devices: 12.7 us -> 11.3 us  [moved(): lax.ppermute(array, axis, [(i, place(i) % count) for i in range(count)])]
  transfers between devices with their start and end apart: 12 -> 12, of which waited for: 6 -> 6; matrix products, arithmetic and copies ran while one was open for 0% -> 0% of each run, Pallas kernels for 24% -> 28%
where the time goes in v6:
time: 41.9 us; the launch traced here: 41.7 us
  starting transfers between devices  16.1 us (38%)
  Pallas kernels  14.2 us (34%)
  waiting for transfers between devices  11.3 us (27%)
    ppermute x11, starting transfers between devices, moved(): lax.ppermute(array, axis, [(i, place(i) % count) for i in range(count)])  12.7 us
    ppermute x11, waiting for transfers between devices, moved(): lax.ppermute(array, axis, [(i, place(i) % count) for i in range(count)])  11.3 us
    pallas_call x3, Pallas kernels, on_device(): pl.pallas_call(functools.partial(pair_kernel, offsets, window, heads, len...  4.38 us
    ppermute x1, starting transfers between devices, on_device(): lax.ppermute(key_value, 'ctx', [pair for pair in pairs if pair[1] < count])  3.39 us
    pallas_call x1, Pallas kernels, on_device(): pl.pallas_call(query_term_kernel, in_specs=[in_vmem] * 3 + [in_hbm], out_...  3.14 us
    pallas_call x8, Pallas kernels, term(): pl.pallas_call(functools.partial(term_kernel, pieces, first), in_specs=[i...  2.23 us
    pallas_call x2, Pallas kernels, on_device(): pl.pallas_call(functools.partial(finish_kernel, starts[i], len(hops)), in...  1.54 us
    pallas_call x1, Pallas kernels, on_device(): pl.pallas_call(functools.partial(own_kernel, window, heads), in_specs=[in...  1.43 us
  transfers between devices with their start and end apart: 12, of which 6 were waited for; matrix products, arithmetic and copies ran while one was open for 0% of the time, Pallas kernels for 28%

profile of v6, /device:TPU:0, one launch (start us, length us, event | category | flops | bytes accessed | tf_op | source)
XLA Modules:
  0.0 41.7 jit_solution(15780029945124964762)
XLA Ops:
  0.0 1.3 %load.1 = (bf16[512,128]{1,0:T(8,128)(2,1)S(1)}, bf16[256,512]{1,0:T(8,128)(2,1)S(1)}, bf16[256,512]{1,0:T(8,128)(2,1)S(1)}, bf16[256,512]{1,0:T(8,128)(2,1)S(1)...) custom-call(bf16[256,128]{1,0:T(8,128)(2,1)} %key_hbm.1, bf16[256,128]{1,0:T(8,128)(2,1)} %value_hbm.1, ...), custom_call_target="tpu_custom_call" | custom-call | tf_op jit(solution)/shard_map/load/pallas_call | solution.py:285
  1.3 3.1 %collective-permute-start = (bf16[512,128]{1,0:T(8,128)(2,1)S(1)}, bf16[512,128]{1,0:T(8,128)(2,1)S(1)}, u32[]{:S(2)}, u32[]{:S(2)}) collective-permute-start(bf16[512,128]{1,0:T(8,128)(2,1)S(1)} %get-tuple-element.26.key_value_ref), channel_id=1, source_target_pairs={{0,8},{4,12},{8,16},{12,20},{16,24},{20,28},{24,0},{28,4},{1,9},{5... | collective-permute-start | bytes 393224 | tf_op jit(solution)/shard_map/ppermute | solution.py:26
  4.4 3.4 %collective-permute-start.2 = (bf16[512,128]{1,0:T(8,128)(2,1)S(1)}, bf16[512,128]{1,0:T(8,128)(2,1)S(1)}, u32[]{:S(2)}, u32[]{:S(2)}) collective-permute-start(bf16[512,128]{1,0:T(8,128)(2,1)S(1)} %get-tuple-element.26.key_value_ref), channel_id=1, source_target_pairs={{0,4},{4,16},{8,12},{12,24},{16,20},{24,28},{1,5},{5,17},{9,13},{1... | collective-permute-start | bytes 393224 | tf_op jit(solution)/shard_map/ppermute | solution.py:308
  7.8 1.4 %own_block.1 = (f32[4,256]{1,0:T(4,128)S(1)}, f32[128,1024]{1,0:T(8,128)S(1)}, f32[512,128]{1,0:T(8,128)S(1)}) custom-call(bf16[512,128]{1,0:T(8,128)(2,1)S(1)} %get-tuple-element.26.key_value_ref, bf16[256,512]{1,0:T(8,128)(2,1)S(1)} %get-tuple-element.27.query_ref, bf16[256,512]{1,0:T(8,128)(2,1)S(1)} %get-tuple-element.28.grad_ref, ...), custom_call_target="tpu_custom_call" | custom-call | flops 1000000 | bytes 2500 | tf_op jit(solution)/shard_map/own_block/pallas_call | solution.py:311
  9.2 0.7 %collective-permute-done.key_value_ref = bf16[512,128]{1,0:T(8,128)(2,1)S(1)} collective-permute-done((bf16[512,128]{1,0:T(8,128)(2,1)S(1)}, bf16[512,128]{1,0:T(8,128)(2,1)S(1)}, u32[]{:S(2)}, u32[]{:S(2)}) %collective-permute-start) | collective-permute-done | bytes 131104 | tf_op jit(solution)/shard_map/ppermute | solution.py:26
  9.9 1.9 %collective-permute-start.4 = (bf16[512,128]{1,0:T(8,128)(2,1)S(1)}, bf16[512,128]{1,0:T(8,128)(2,1)S(1)}, u32[]{:S(2)}, u32[]{:S(2)}) collective-permute-start(bf16[512,128]{1,0:T(8,128)(2,1)S(1)} %collective-permute-done.key_value_ref), channel_id=1, source_target_pairs={{0,4},{4,0},{8,12},{12,8},{16,20},{20,16},{24,28},{28,24},{1,5},{5... | collective-permute-start | bytes 393224 | tf_op jit(solution)/shard_map/ppermute | solution.py:26
  11.8 1.6 %block_back_22.1 = (f32[128,1024]{1,0:T(8,128)S(1)}, bf16[512,128]{1,0:T(8,128)(2,1)S(1)}, bf16[4096,128]{1,0:T(8,128)(2,1)S(1)}, bf16[4096,128]{1,0:T(8,128)(2,1)S(1)}) custom-call(bf16[512,128]{1,0:T(8,128)(2,1)S(1)} %collective-permute-done.key_value_ref, bf16[256,512]{1,0:T(8,128)(2,1)S(1)} %get-tuple-element.27.query_ref, ...), custom_call_target="tpu_custom_call" | custom-call | flops 1000000 | bytes 2500 | tf_op jit(solution)/shard_map/block_back_22/pallas_call | solution.py:331
  13.4 1.4 %collective-permute-start.1 = (bf16[512,128]{1,0:T(8,128)(2,1)S(1)}, bf16[512,128]{1,0:T(8,128)(2,1)S(1)}, u32[]{:S(2)}, u32[]{:S(2)}) collective-permute-start(bf16[512,128]{1,0:T(8,128)(2,1)S(1)} %get-tuple-element.37), channel_id=1, source_target_pairs={{0,24},{4,28},{8,0},{12,4},{16,8},{20,12},{24,16},{28,20},{1,25},{... | collective-permute-start | bytes 393224 | tf_op jit(solution)/shard_map/ppermute | solution.py:26
  14.8 1.4 %block_back_31.1 = (f32[128,1024]{1,0:T(8,128)S(1)}, bf16[512,128]{1,0:T(8,128)(2,1)S(1)}) custom-call(bf16[512,128]{1,0:T(8,128)(2,1)S(1)} %collective-permute-done.2.key_value_ref, bf16[256,512]{1,0:T(8,128)(2,1)S(1)} %get-tuple-element.27.query_ref, bf16[256,512]{1,0:T(8,128)(2,1)S(1)} %get-tuple-element.28.grad_ref, ...), custom_call_target="tpu_custom_call" | custom-call | flops 1000000 | bytes 2500 | tf_op jit(solution)/shard_map/block_back_31/pallas_call | solution.py:331
  16.1 1.3 %collective-permute-start.3 = (bf16[512,128]{1,0:T(8,128)(2,1)S(1)}, bf16[512,128]{1,0:T(8,128)(2,1)S(1)}, u32[]{:S(2)}, u32[]{:S(2)}) collective-permute-start(bf16[512,128]{1,0:T(8,128)(2,1)S(1)} %get-tuple-element.39), channel_id=1, source_target_pairs={{0,20},{4,0},{8,28},{12,8},{16,4},{20,16},{24,12},{28,24},{1,21},{... | collective-permute-start | bytes 393224 | tf_op jit(solution)/shard_map/ppermute | solution.py:26
  17.5 1.4 %block_back_13.1 = (bf16[256,512]{1,0:T(8,128)(2,1)S(1)}, bf16[512,128]{1,0:T(8,128)(2,1)S(1)}) custom-call(bf16[512,128]{1,0:T(8,128)(2,1)S(1)} %collective-permute-done.4.key_value_ref, bf16[256,512]{1,0:T(8,128)(2,1)S(1)} %get-tuple-element.27.query_ref, bf16[256,512]{1,0:T(8,128)(2,1)S(1)} %get-tuple-element.28.grad_ref, ...), custom_call_target="tpu_custom_call" | custom-call | flops 1000000 | bytes 2500 | tf_op jit(solution)/shard_map/block_back_13/pallas_call | solution.py:331
  18.9 2.2 %collective-permute-start.5 = (bf16[512,128]{1,0:T(8,128)(2,1)S(1)}, bf16[512,128]{1,0:T(8,128)(2,1)S(1)}, u32[]{:S(2)}, u32[]{:S(2)}) collective-permute-start(bf16[512,128]{1,0:T(8,128)(2,1)S(1)} %get-tuple-element.41), channel_id=1, source_target_pairs={{0,24},{4,28},{8,4},{12,0},{16,12},{20,8},{24,20},{28,16},{1,25},{... | collective-permute-start | bytes 393224 | tf_op jit(solution)/shard_map/ppermute | solution.py:26
  21.1 3.1 %query_term.1 = (f32[4,256,1024]{2,1,0:T(8,128)S(1)}, bf16[4096,256]{1,0:T(8,128)(2,1)S(1)}) custom-call(bf16[256,512]{1,0:T(8,128)(2,1)S(1)} %get-tuple-element.42.query_ref, bf16[4096,128]{1,0:T(8,128)(2,1)S(1)} %get-tuple-element.43.wk_ref, bf16[4096,128]{1,0:T(8,128)(2,1)S(1)} %get-tuple-element.44.wv_ref, bf16[4096,512]{1,0:T(8,128)(2,1)} %wq_hbm.1), custom_call_target="tpu_custom_call" | custom-call | flops 671088640 | bytes 1677721 | tf_op jit(solution)/shard_map/query_term/pallas_call | solution.py:353
  24.4 0.4 %collective-permute-done.5.right_ref = bf16[512,128]{1,0:T(8,128)(2,1)S(1)} collective-permute-done((bf16[512,128]{1,0:T(8,128)(2,1)S(1)}, bf16[512,128]{1,0:T(8,128)(2,1)S(1)}, u32[]{:S(2)}, u32[]{:S(2)}) %collective-permute-start.5) | collective-permute-done | bytes 131104 | tf_op jit(solution)/shard_map/ppermute | solution.py:26
  24.9 0.3 term.8.refs_0_
  25.2 0.1 collective-permute-start.7
  25.3 0.3 term.9.refs_0_
  25.5 0.3 term.10.refs_0_
  25.8 0.3 term.11.refs_0_
  26.1 0.3 term.12.left_ref
  26.4 0.5 %collective-permute-done.7.right_ref = bf16[256,640]{1,0:T(8,128)(2,1)S(1)} collective-permute-done((bf16[256,640]{1,0:T(8,128)(2,1)S(1)}, bf16[256,640]{1,0:T(8,128)(2,1)S(1)}, u32[]{:S(2)}, u32[]{:S(2)}) %collective-permute-start.7) | collective-permute-done | bytes 327712 | tf_op jit(solution)/shard_map/ppermute | solution.py:26
  26.9 1.6 %collective-permute-start.8 = (bf16[256,640]{1,0:T(8,128)(2,1)S(1)}, bf16[256,640]{1,0:T(8,128)(2,1)S(1)}, u32[]{:S(2)}, u32[]{:S(2)}) collective-permute-start(bf16[256,640]{1,0:T(8,128)(2,1)S(1)} %sum.1.refs_1_), channel_id=1, source_target_pairs={{0,2},{1,3},{2,0},{3,1},{4,6},{5,7},{6,4},{7,5},{8,10},{9,11},{10,... | collective-permute-start | bytes 983048 | tf_op jit(solution)/shard_map/ppermute | solution.py:26
  28.5 0.5 %collective-permute-start.10 = (bf16[256,384]{1,0:T(8,128)(2,1)S(1)}, bf16[256,384]{1,0:T(8,128)(2,1)S(1)}, u32[]{:S(2)}, u32[]{:S(2)}) collective-permute-start(bf16[256,384]{1,0:T(8,128)(2,1)S(1)} %term.9.refs_0_), channel_id=1, source_target_pairs={{0,1},{1,0},{2,3},{3,2},{4,5},{5,4},{6,7},{7,6},{8,9},{9,8},{10,11... | collective-permute-start | bytes 589832 | tf_op jit(solution)/shard_map/ppermute | solution.py:26
  29.0 1.3 %collective-permute-done.10.refs_0_ = bf16[256,384]{1,0:T(8,128)(2,1)S(1)} collective-permute-done((bf16[256,384]{1,0:T(8,128)(2,1)S(1)}, bf16[256,384]{1,0:T(8,128)(2,1)S(1)}, u32[]{:S(2)}, u32[]{:S(2)}) %collective-permute-start.10) | collective-permute-done | bytes 196640 | tf_op jit(solution)/shard_map/ppermute | solution.py:26
  30.3 0.3 term.15
  30.6 0.6 %collective-permute-start.11 = (bf16[256,384]{1,0:T(8,128)(2,1)S(1)}, bf16[256,384]{1,0:T(8,128)(2,1)S(1)}, u32[]{:S(2)}, u32[]{:S(2)}) collective-permute-start(bf16[256,384]{1,0:T(8,128)(2,1)S(1)} %term.15), channel_id=1, source_target_pairs={{0,2},{1,3},{2,0},{3,1},{4,6},{5,7},{6,4},{7,5},{8,10},{9,11},{10,... | collective-permute-start | bytes 589832 | tf_op jit(solution)/shard_map/ppermute | solution.py:26
  31.2 6.4 %collective-permute-done.8.refs_1_.refs_0_ = bf16[256,640]{1,0:T(8,128)(2,1)S(1)} collective-permute-done((bf16[256,640]{1,0:T(8,128)(2,1)S(1)}, bf16[256,640]{1,0:T(8,128)(2,1)S(1)}, u32[]{:S(2)}, u32[]{:S(2)}) %collective-permute-start.8) | collective-permute-done | bytes 327712 | tf_op jit(solution)/shard_map/ppermute | solution.py:26
  37.6 0.3 term.14.high_ref
  37.8 0.3 term.13.low_ref
  38.1 0.8 %finish.2.refs_1_ = bf16[256,1024]{1,0:T(8,128)(2,1)} custom-call(f32[256,512]{1,0:T(8,128)S(1)} %term.13.low_ref, f32[256,512]{1,0:T(8,128)S(1)} %term.14.high_ref, bf16[256,640]{1,0:T(8,128)(2,1)S(1)} %collective-permute-done.8.refs_1_.refs_0_), custom_call_target="tpu_custom_call" | custom-call | flops 1000000 | bytes 2500 | tf_op jit(solution)/shard_map/finish/pallas_call | solution.py:425
  38.9 2.0 %collective-permute-done.11.refs_0_ = bf16[256,384]{1,0:T(8,128)(2,1)S(1)} collective-permute-done((bf16[256,384]{1,0:T(8,128)(2,1)S(1)}, bf16[256,384]{1,0:T(8,128)(2,1)S(1)}, u32[]{:S(2)}, u32[]{:S(2)}) %collective-permute-start.11) | collective-permute-done | bytes 196640 | tf_op jit(solution)/shard_map/ppermute | solution.py:26
  41.0 0.7 %finish.3 = bf16[256,1024]{1,0:T(8,128)(2,1)} custom-call(f32[256,512]{1,0:T(8,128)S(1)} %term.13.low_ref, f32[256,512]{1,0:T(8,128)S(1)} %term.14.high_ref, bf16[256,384]{1,0:T(8,128)(2,1)S(1)} %collective-permute-done.11.refs_0_, bf16[256,1024]{1,0:T(8,128)(2,1)} %finish.2.refs_1_), custom_call_target="tpu_custom_call", output_to_operand_aliasing={{}: (3, {})} | custom-call | flops 1000000 | bytes 2500 | tf_op jit(solution)/shard_map/finish/pallas_call | solution.py:425
  (12 shorter events, 0.2 us)
Async XLA Ops:
  1.3 8.6 %collective-permute-start = (bf16[512,128]{1,0:T(8,128)(2,1)S(1)}, bf16[512,128]{1,0:T(8,128)(2,1)S(1)}, u32[]{:S(2)}, u32[]{:S(2)}) collective-permute-start(bf16[512,128]{1,0:T(8,128)(2,1)S(1)} %get-tuple-element.26.key_value_ref), channel_id=1, source_target_pairs={{0,8},{4,12},{8,16},{12,20},{16,24},{20,28},{24,0},{28,4},{1,9},{5... | collective-permute-start | bytes 393224 | tf_op jit(solution)/shard_map/ppermute | solution.py:26
  4.4 10.4 %collective-permute-start.2 = (bf16[512,128]{1,0:T(8,128)(2,1)S(1)}, bf16[512,128]{1,0:T(8,128)(2,1)S(1)}, u32[]{:S(2)}, u32[]{:S(2)}) collective-permute-start(bf16[512,128]{1,0:T(8,128)(2,1)S(1)} %get-tuple-element.26.key_value_ref), channel_id=1, source_target_pairs={{0,4},{4,16},{8,12},{12,24},{16,20},{24,28},{1,5},{5,17},{9,13},{1... | collective-permute-start | bytes 393224 | tf_op jit(solution)/shard_map/ppermute | solution.py:308
  9.9 7.6 %collective-permute-start.4 = (bf16[512,128]{1,0:T(8,128)(2,1)S(1)}, bf16[512,128]{1,0:T(8,128)(2,1)S(1)}, u32[]{:S(2)}, u32[]{:S(2)}) collective-permute-start(bf16[512,128]{1,0:T(8,128)(2,1)S(1)} %collective-permute-done.key_value_ref), channel_id=1, source_target_pairs={{0,4},{4,0},{8,12},{12,8},{16,20},{20,16},{24,28},{28,24},{1,5},{5... | collective-permute-start | bytes 393224 | tf_op jit(solution)/shard_map/ppermute | solution.py:26
  13.4 10.9 %collective-permute-start.1 = (bf16[512,128]{1,0:T(8,128)(2,1)S(1)}, bf16[512,128]{1,0:T(8,128)(2,1)S(1)}, u32[]{:S(2)}, u32[]{:S(2)}) collective-permute-start(bf16[512,128]{1,0:T(8,128)(2,1)S(1)} %get-tuple-element.37), channel_id=1, source_target_pairs={{0,24},{4,28},{8,0},{12,4},{16,8},{20,12},{24,16},{28,20},{1,25},{... | collective-permute-start | bytes 393224 | tf_op jit(solution)/shard_map/ppermute | solution.py:26
  16.1 8.2 %collective-permute-start.3 = (bf16[512,128]{1,0:T(8,128)(2,1)S(1)}, bf16[512,128]{1,0:T(8,128)(2,1)S(1)}, u32[]{:S(2)}, u32[]{:S(2)}) collective-permute-start(bf16[512,128]{1,0:T(8,128)(2,1)S(1)} %get-tuple-element.39), channel_id=1, source_target_pairs={{0,20},{4,0},{8,28},{12,8},{16,4},{20,16},{24,12},{28,24},{1,21},{... | collective-permute-start | bytes 393224 | tf_op jit(solution)/shard_map/ppermute | solution.py:26
  18.9 5.9 %collective-permute-start.5 = (bf16[512,128]{1,0:T(8,128)(2,1)S(1)}, bf16[512,128]{1,0:T(8,128)(2,1)S(1)}, u32[]{:S(2)}, u32[]{:S(2)}) collective-permute-start(bf16[512,128]{1,0:T(8,128)(2,1)S(1)} %get-tuple-element.41), channel_id=1, source_target_pairs={{0,24},{4,28},{8,4},{12,0},{16,12},{20,8},{24,20},{28,16},{1,25},{... | collective-permute-start | bytes 393224 | tf_op jit(solution)/shard_map/ppermute | solution.py:26
  25.2 1.7 %collective-permute-start.7 = (bf16[256,640]{1,0:T(8,128)(2,1)S(1)}, bf16[256,640]{1,0:T(8,128)(2,1)S(1)}, u32[]{:S(2)}, u32[]{:S(2)}) collective-permute-start(bf16[256,640]{1,0:T(8,128)(2,1)S(1)} %term.8.refs_0_), channel_id=1, source_target_pairs={{0,1},{1,0},{2,3},{3,2},{4,5},{5,4},{6,7},{7,6},{8,9},{9,8},{10,11... | collective-permute-start | bytes 983048 | tf_op jit(solution)/shard_map/ppermute | solution.py:26
  26.9 10.6 %collective-permute-start.8 = (bf16[256,640]{1,0:T(8,128)(2,1)S(1)}, bf16[256,640]{1,0:T(8,128)(2,1)S(1)}, u32[]{:S(2)}, u32[]{:S(2)}) collective-permute-start(bf16[256,640]{1,0:T(8,128)(2,1)S(1)} %sum.1.refs_1_), channel_id=1, source_target_pairs={{0,2},{1,3},{2,0},{3,1},{4,6},{5,7},{6,4},{7,5},{8,10},{9,11},{10,... | collective-permute-start | bytes 983048 | tf_op jit(solution)/shard_map/ppermute | solution.py:26
  28.5 2.7 %collective-permute-start.9 = (bf16[256,512]{1,0:T(8,128)(2,1)S(1)}, bf16[256,512]{1,0:T(8,128)(2,1)S(1)}, u32[]{:S(2)}, u32[]{:S(2)}) collective-permute-start(bf16[256,512]{1,0:T(8,128)(2,1)S(1)} %term.11.refs_0_), channel_id=1, source_target_pairs={{0,1},{1,0},{2,3},{3,2},{4,5},{5,4},{6,7},{7,6},{8,9},{9,8},{10,11... | collective-permute-start | bytes 786440 | tf_op jit(solution)/shard_map/ppermute | solution.py:26
  28.5 1.8 %collective-permute-start.10 = (bf16[256,384]{1,0:T(8,128)(2,1)S(1)}, bf16[256,384]{1,0:T(8,128)(2,1)S(1)}, u32[]{:S(2)}, u32[]{:S(2)}) collective-permute-start(bf16[256,384]{1,0:T(8,128)(2,1)S(1)} %term.9.refs_0_), channel_id=1, source_target_pairs={{0,1},{1,0},{2,3},{3,2},{4,5},{5,4},{6,7},{7,6},{8,9},{9,8},{10,11... | collective-permute-start | bytes 589832 | tf_op jit(solution)/shard_map/ppermute | solution.py:26
  29.0 8.8 %collective-permute-start.6 = (bf16[256,512]{1,0:T(8,128)(2,1)S(1)}, bf16[256,512]{1,0:T(8,128)(2,1)S(1)}, u32[]{:S(2)}, u32[]{:S(2)}) collective-permute-start(bf16[256,512]{1,0:T(8,128)(2,1)S(1)} %term.10.refs_0_), channel_id=1, source_target_pairs={{0,1},{1,0},{2,3},{3,2},{4,5},{5,4},{6,7},{7,6},{8,9},{9,8},{10,11... | collective-permute-start | bytes 786440 | tf_op jit(solution)/shard_map/ppermute | solution.py:26
  30.6 10.4 %collective-permute-start.11 = (bf16[256,384]{1,0:T(8,128)(2,1)S(1)}, bf16[256,384]{1,0:T(8,128)(2,1)S(1)}, u32[]{:S(2)}, u32[]{:S(2)}) collective-permute-start(bf16[256,384]{1,0:T(8,128)(2,1)S(1)} %term.15), channel_id=1, source_target_pairs={{0,2},{1,3},{2,0},{3,1},{4,6},{5,7},{6,4},{7,5},{8,10},{9,11},{10,... | collective-permute-start | bytes 589832 | tf_op jit(solution)/shard_map/ppermute | solution.py:26

commit v7 on v6

--- a/solution.py
+++ b/solution.py
@@ -106,7 +106,7 @@
     ]
     for copy in copies:
         copy.start()
-    for copy in copies:
+    for copy in copies[2:5]:
         copy.wait()
     block_id = lax.axis_index("ctx")
     first_head = lax.axis_index("tp") * heads
@@ -121,6 +121,8 @@
     for offset in range(mask_ref.shape[1]):
         active = (block_id >= offset) & (mask_ref[0, offset] == 1)
         rows_ref[pl.ds(offset * heads, heads), :] = jnp.where(active, norms, f32(jnp.inf))
+    for copy in copies[:2] + copies[5:]:
+        copy.wait()
 
 
 def with_copies(loads, results, refs):
@@ -380,7 +382,7 @@
 
     operands = (sums, query_term, weights)
     hops = range(2, tp_size, 2)
-    sizes = (cols * 5 // 8, cols * 3 // 8) if cols % 1024 == 0 else (cols // 2,) * 2
+    sizes = (cols * 3 // 4, cols // 4) if cols % 1024 == 0 else (cols // 2,) * 2
     starts = (0, sizes[0])
     low, high = 10**6, block_cost.flops
 

time: 41.9 us -> 41.9 us (level)
  no operation moved by 1% of the time
where the time goes in v7:
time: 41.9 us; the launch traced here: 41.8 us
  starting transfers between devices  16 us (38%)
  Pallas kernels  14.1 us (34%)
  waiting for transfers between devices  11.4 us (27%)
    ppermute x11, starting transfers between devices, moved(): lax.ppermute(array, axis, [(i, place(i) % count) for i in range(count)])  12.7 us
    ppermute x11, waiting for transfers between devices, moved(): lax.ppermute(array, axis, [(i, place(i) % count) for i in range(count)])  11.4 us
    pallas_call x3, Pallas kernels, on_device(): pl.pallas_call(functools.partial(pair_kernel, offsets, window, heads, len...  4.39 us
    ppermute x1, starting transfers between devices, on_device(): lax.ppermute(key_value, 'ctx', [pair for pair in pairs if pair[1] < count])  3.39 us
    pallas_call x1, Pallas kernels, on_device(): pl.pallas_call(query_term_kernel, in_specs=[in_vmem] * 3 + [in_hbm], out_...  3.14 us
    pallas_call x8, Pallas kernels, term(): pl.pallas_call(functools.partial(term_kernel, pieces, first), in_specs=[i...  2.18 us
    pallas_call x2, Pallas kernels, on_device(): pl.pallas_call(functools.partial(finish_kernel, starts[i], len(hops)), in...  1.54 us
    pallas_call x1, Pallas kernels, on_device(): pl.pallas_call(functools.partial(own_kernel, window, heads), in_specs=[in...  1.43 us
  transfers between devices with their start and end apart: 12, of which 6 were waited for; matrix products, arithmetic and copies ran while one was open for 0% of the time, Pallas kernels for 28%

profile of v7, /device:TPU:0, one launch (start us, length us, event | category | flops | bytes accessed | tf_op | source)
XLA Modules:
  0.0 41.8 jit_solution(13500475737951213574)
XLA Ops:
  0.0 1.3 %load.1 = (bf16[512,128]{1,0:T(8,128)(2,1)S(1)}, bf16[256,512]{1,0:T(8,128)(2,1)S(1)}, bf16[256,512]{1,0:T(8,128)(2,1)S(1)}, bf16[256,512]{1,0:T(8,128)(2,1)S(1)...) custom-call(bf16[256,128]{1,0:T(8,128)(2,1)} %key_hbm.1, bf16[256,128]{1,0:T(8,128)(2,1)} %value_hbm.1, ...), custom_call_target="tpu_custom_call" | custom-call | tf_op jit(solution)/shard_map/load/pallas_call | solution.py:287
  1.3 3.1 %collective-permute-start = (bf16[512,128]{1,0:T(8,128)(2,1)S(1)}, bf16[512,128]{1,0:T(8,128)(2,1)S(1)}, u32[]{:S(2)}, u32[]{:S(2)}) collective-permute-start(bf16[512,128]{1,0:T(8,128)(2,1)S(1)} %get-tuple-element.26.key_value_ref), channel_id=1, source_target_pairs={{0,8},{4,12},{8,16},{12,20},{16,24},{20,28},{24,0},{28,4},{1,9},{5... | collective-permute-start | bytes 393224 | tf_op jit(solution)/shard_map/ppermute | solution.py:26
  4.4 3.4 %collective-permute-start.2 = (bf16[512,128]{1,0:T(8,128)(2,1)S(1)}, bf16[512,128]{1,0:T(8,128)(2,1)S(1)}, u32[]{:S(2)}, u32[]{:S(2)}) collective-permute-start(bf16[512,128]{1,0:T(8,128)(2,1)S(1)} %get-tuple-element.26.key_value_ref), channel_id=1, source_target_pairs={{0,4},{4,16},{8,12},{12,24},{16,20},{24,28},{1,5},{5,17},{9,13},{1... | collective-permute-start | bytes 393224 | tf_op jit(solution)/shard_map/ppermute | solution.py:310
  7.8 1.4 %own_block.1 = (f32[4,256]{1,0:T(4,128)S(1)}, f32[128,1024]{1,0:T(8,128)S(1)}, f32[512,128]{1,0:T(8,128)S(1)}) custom-call(bf16[512,128]{1,0:T(8,128)(2,1)S(1)} %get-tuple-element.26.key_value_ref, bf16[256,512]{1,0:T(8,128)(2,1)S(1)} %get-tuple-element.27.query_ref, bf16[256,512]{1,0:T(8,128)(2,1)S(1)} %get-tuple-element.28.grad_ref, ...), custom_call_target="tpu_custom_call" | custom-call | flops 1000000 | bytes 2500 | tf_op jit(solution)/shard_map/own_block/pallas_call | solution.py:313
  9.2 0.7 %collective-permute-done.key_value_ref = bf16[512,128]{1,0:T(8,128)(2,1)S(1)} collective-permute-done((bf16[512,128]{1,0:T(8,128)(2,1)S(1)}, bf16[512,128]{1,0:T(8,128)(2,1)S(1)}, u32[]{:S(2)}, u32[]{:S(2)}) %collective-permute-start) | collective-permute-done | bytes 131104 | tf_op jit(solution)/shard_map/ppermute | solution.py:26
  9.9 1.9 %collective-permute-start.4 = (bf16[512,128]{1,0:T(8,128)(2,1)S(1)}, bf16[512,128]{1,0:T(8,128)(2,1)S(1)}, u32[]{:S(2)}, u32[]{:S(2)}) collective-permute-start(bf16[512,128]{1,0:T(8,128)(2,1)S(1)} %collective-permute-done.key_value_ref), channel_id=1, source_target_pairs={{0,4},{4,0},{8,12},{12,8},{16,20},{20,16},{24,28},{28,24},{1,5},{5... | collective-permute-start | bytes 393224 | tf_op jit(solution)/shard_map/ppermute | solution.py:26
  11.8 1.6 %block_back_22.1 = (f32[128,1024]{1,0:T(8,128)S(1)}, bf16[512,128]{1,0:T(8,128)(2,1)S(1)}, bf16[4096,128]{1,0:T(8,128)(2,1)S(1)}, bf16[4096,128]{1,0:T(8,128)(2,1)S(1)}) custom-call(bf16[512,128]{1,0:T(8,128)(2,1)S(1)} %collective-permute-done.key_value_ref, bf16[256,512]{1,0:T(8,128)(2,1)S(1)} %get-tuple-element.27.query_ref, ...), custom_call_target="tpu_custom_call" | custom-call | flops 1000000 | bytes 2500 | tf_op jit(solution)/shard_map/block_back_22/pallas_call | solution.py:333
  13.4 1.3 %collective-permute-start.1 = (bf16[512,128]{1,0:T(8,128)(2,1)S(1)}, bf16[512,128]{1,0:T(8,128)(2,1)S(1)}, u32[]{:S(2)}, u32[]{:S(2)}) collective-permute-start(bf16[512,128]{1,0:T(8,128)(2,1)S(1)} %get-tuple-element.37), channel_id=1, source_target_pairs={{0,24},{4,28},{8,0},{12,4},{16,8},{20,12},{24,16},{28,20},{1,25},{... | collective-permute-start | bytes 393224 | tf_op jit(solution)/shard_map/ppermute | solution.py:26
  14.7 1.4 %block_back_31.1 = (f32[128,1024]{1,0:T(8,128)S(1)}, bf16[512,128]{1,0:T(8,128)(2,1)S(1)}) custom-call(bf16[512,128]{1,0:T(8,128)(2,1)S(1)} %collective-permute-done.2.key_value_ref, bf16[256,512]{1,0:T(8,128)(2,1)S(1)} %get-tuple-element.27.query_ref, bf16[256,512]{1,0:T(8,128)(2,1)S(1)} %get-tuple-element.28.grad_ref, ...), custom_call_target="tpu_custom_call" | custom-call | flops 1000000 | bytes 2500 | tf_op jit(solution)/shard_map/block_back_31/pallas_call | solution.py:333
  16.1 1.3 %collective-permute-start.3 = (bf16[512,128]{1,0:T(8,128)(2,1)S(1)}, bf16[512,128]{1,0:T(8,128)(2,1)S(1)}, u32[]{:S(2)}, u32[]{:S(2)}) collective-permute-start(bf16[512,128]{1,0:T(8,128)(2,1)S(1)} %get-tuple-element.39), channel_id=1, source_target_pairs={{0,20},{4,0},{8,28},{12,8},{16,4},{20,16},{24,12},{28,24},{1,21},{... | collective-permute-start | bytes 393224 | tf_op jit(solution)/shard_map/ppermute | solution.py:26
  17.4 1.4 %block_back_13.1 = (bf16[256,512]{1,0:T(8,128)(2,1)S(1)}, bf16[512,128]{1,0:T(8,128)(2,1)S(1)}) custom-call(bf16[512,128]{1,0:T(8,128)(2,1)S(1)} %collective-permute-done.4.key_value_ref, bf16[256,512]{1,0:T(8,128)(2,1)S(1)} %get-tuple-element.27.query_ref, bf16[256,512]{1,0:T(8,128)(2,1)S(1)} %get-tuple-element.28.grad_ref, ...), custom_call_target="tpu_custom_call" | custom-call | flops 1000000 | bytes 2500 | tf_op jit(solution)/shard_map/block_back_13/pallas_call | solution.py:333
  18.9 2.2 %collective-permute-start.5 = (bf16[512,128]{1,0:T(8,128)(2,1)S(1)}, bf16[512,128]{1,0:T(8,128)(2,1)S(1)}, u32[]{:S(2)}, u32[]{:S(2)}) collective-permute-start(bf16[512,128]{1,0:T(8,128)(2,1)S(1)} %get-tuple-element.41), channel_id=1, source_target_pairs={{0,24},{4,28},{8,4},{12,0},{16,12},{20,8},{24,20},{28,16},{1,25},{... | collective-permute-start | bytes 393224 | tf_op jit(solution)/shard_map/ppermute | solution.py:26
  21.1 3.1 %query_term.1 = (f32[4,256,1024]{2,1,0:T(8,128)S(1)}, bf16[4096,256]{1,0:T(8,128)(2,1)S(1)}) custom-call(bf16[256,512]{1,0:T(8,128)(2,1)S(1)} %get-tuple-element.42.query_ref, bf16[4096,128]{1,0:T(8,128)(2,1)S(1)} %get-tuple-element.43.wk_ref, bf16[4096,128]{1,0:T(8,128)(2,1)S(1)} %get-tuple-element.44.wv_ref, bf16[4096,512]{1,0:T(8,128)(2,1)} %wq_hbm.1), custom_call_target="tpu_custom_call" | custom-call | flops 671088640 | bytes 1677721 | tf_op jit(solution)/shard_map/query_term/pallas_call | solution.py:355
  24.4 0.4 %collective-permute-done.5.right_ref = bf16[512,128]{1,0:T(8,128)(2,1)S(1)} collective-permute-done((bf16[512,128]{1,0:T(8,128)(2,1)S(1)}, bf16[512,128]{1,0:T(8,128)(2,1)S(1)}, u32[]{:S(2)}, u32[]{:S(2)}) %collective-permute-start.5) | collective-permute-done | bytes 131104 | tf_op jit(solution)/shard_map/ppermute | solution.py:26
  24.8 0.3 term.8.refs_0_
  25.2 0.1 collective-permute-start.7
  25.2 0.2 term.9.refs_0_
  25.5 0.3 term.10.refs_0_
  25.8 0.3 term.11.refs_0_
  26.1 0.3 term.12.left_ref
  26.4 0.6 %collective-permute-done.7.right_ref = bf16[256,768]{1,0:T(8,128)(2,1)S(1)} collective-permute-done((bf16[256,768]{1,0:T(8,128)(2,1)S(1)}, bf16[256,768]{1,0:T(8,128)(2,1)S(1)}, u32[]{:S(2)}, u32[]{:S(2)}) %collective-permute-start.7) | collective-permute-done | bytes 393248 | tf_op jit(solution)/shard_map/ppermute | solution.py:26
  27.0 1.6 %collective-permute-start.8 = (bf16[256,768]{1,0:T(8,128)(2,1)S(1)}, bf16[256,768]{1,0:T(8,128)(2,1)S(1)}, u32[]{:S(2)}, u32[]{:S(2)}) collective-permute-start(bf16[256,768]{1,0:T(8,128)(2,1)S(1)} %sum.1.refs_1_), channel_id=1, source_target_pairs={{0,2},{1,3},{2,0},{3,1},{4,6},{5,7},{6,4},{7,5},{8,10},{9,11},{10,... | collective-permute-start | bytes 1179656 | tf_op jit(solution)/shard_map/ppermute | solution.py:26
  28.6 0.5 %collective-permute-start.10 = (bf16[256,256]{1,0:T(8,128)(2,1)S(1)}, bf16[256,256]{1,0:T(8,128)(2,1)S(1)}, u32[]{:S(2)}, u32[]{:S(2)}) collective-permute-start(bf16[256,256]{1,0:T(8,128)(2,1)S(1)} %term.9.refs_0_), channel_id=1, source_target_pairs={{0,1},{1,0},{2,3},{3,2},{4,5},{5,4},{6,7},{7,6},{8,9},{9,8},{10,11... | collective-permute-start | bytes 393224 | tf_op jit(solution)/shard_map/ppermute | solution.py:26
  29.1 1.2 %collective-permute-done.10.refs_0_ = bf16[256,256]{1,0:T(8,128)(2,1)S(1)} collective-permute-done((bf16[256,256]{1,0:T(8,128)(2,1)S(1)}, bf16[256,256]{1,0:T(8,128)(2,1)S(1)}, u32[]{:S(2)}, u32[]{:S(2)}) %collective-permute-start.10) | collective-permute-done | bytes 131104 | tf_op jit(solution)/shard_map/ppermute | solution.py:26
  30.3 0.2 term.15
  30.6 0.6 %collective-permute-start.11 = (bf16[256,256]{1,0:T(8,128)(2,1)S(1)}, bf16[256,256]{1,0:T(8,128)(2,1)S(1)}, u32[]{:S(2)}, u32[]{:S(2)}) collective-permute-start(bf16[256,256]{1,0:T(8,128)(2,1)S(1)} %term.15), channel_id=1, source_target_pairs={{0,2},{1,3},{2,0},{3,1},{4,6},{5,7},{6,4},{7,5},{8,10},{9,11},{10,... | collective-permute-start | bytes 393224 | tf_op jit(solution)/shard_map/ppermute | solution.py:26
  31.2 7.9 %collective-permute-done.8.refs_1_.refs_0_ = bf16[256,768]{1,0:T(8,128)(2,1)S(1)} collective-permute-done((bf16[256,768]{1,0:T(8,128)(2,1)S(1)}, bf16[256,768]{1,0:T(8,128)(2,1)S(1)}, u32[]{:S(2)}, u32[]{:S(2)}) %collective-permute-start.8) | collective-permute-done | bytes 393248 | tf_op jit(solution)/shard_map/ppermute | solution.py:26
  39.1 0.3 term.14.high_ref
  39.3 0.3 term.13.low_ref
  39.6 0.8 %finish.2.refs_1_ = bf16[256,1024]{1,0:T(8,128)(2,1)} custom-call(f32[256,512]{1,0:T(8,128)S(1)} %term.13.low_ref, f32[256,512]{1,0:T(8,128)S(1)} %term.14.high_ref, bf16[256,768]{1,0:T(8,128)(2,1)S(1)} %collective-permute-done.8.refs_1_.refs_0_), custom_call_target="tpu_custom_call" | custom-call | flops 1000000 | bytes 2500 | tf_op jit(solution)/shard_map/finish/pallas_call | solution.py:427
  40.5 0.6 %collective-permute-done.11.refs_0_ = bf16[256,256]{1,0:T(8,128)(2,1)S(1)} collective-permute-done((bf16[256,256]{1,0:T(8,128)(2,1)S(1)}, bf16[256,256]{1,0:T(8,128)(2,1)S(1)}, u32[]{:S(2)}, u32[]{:S(2)}) %collective-permute-start.11) | collective-permute-done | bytes 131104 | tf_op jit(solution)/shard_map/ppermute | solution.py:26
  41.1 0.7 %finish.3 = bf16[256,1024]{1,0:T(8,128)(2,1)} custom-call(f32[256,512]{1,0:T(8,128)S(1)} %term.13.low_ref, f32[256,512]{1,0:T(8,128)S(1)} %term.14.high_ref, bf16[256,256]{1,0:T(8,128)(2,1)S(1)} %collective-permute-done.11.refs_0_, bf16[256,1024]{1,0:T(8,128)(2,1)} %finish.2.refs_1_), custom_call_target="tpu_custom_call", output_to_operand_aliasing={{}: (3, {})} | custom-call | flops 1000000 | bytes 2500 | tf_op jit(solution)/shard_map/finish/pallas_call | solution.py:427
  (12 shorter events, 0.2 us)
Async XLA Ops:
  1.3 8.6 %collective-permute-start = (bf16[512,128]{1,0:T(8,128)(2,1)S(1)}, bf16[512,128]{1,0:T(8,128)(2,1)S(1)}, u32[]{:S(2)}, u32[]{:S(2)}) collective-permute-start(bf16[512,128]{1,0:T(8,128)(2,1)S(1)} %get-tuple-element.26.key_value_ref), channel_id=1, source_target_pairs={{0,8},{4,12},{8,16},{12,20},{16,24},{20,28},{24,0},{28,4},{1,9},{5... | collective-permute-start | bytes 393224 | tf_op jit(solution)/shard_map/ppermute | solution.py:26
  4.4 10.4 %collective-permute-start.2 = (bf16[512,128]{1,0:T(8,128)(2,1)S(1)}, bf16[512,128]{1,0:T(8,128)(2,1)S(1)}, u32[]{:S(2)}, u32[]{:S(2)}) collective-permute-start(bf16[512,128]{1,0:T(8,128)(2,1)S(1)} %get-tuple-element.26.key_value_ref), channel_id=1, source_target_pairs={{0,4},{4,16},{8,12},{12,24},{16,20},{24,28},{1,5},{5,17},{9,13},{1... | collective-permute-start | bytes 393224 | tf_op jit(solution)/shard_map/ppermute | solution.py:310
  9.9 7.6 %collective-permute-start.4 = (bf16[512,128]{1,0:T(8,128)(2,1)S(1)}, bf16[512,128]{1,0:T(8,128)(2,1)S(1)}, u32[]{:S(2)}, u32[]{:S(2)}) collective-permute-start(bf16[512,128]{1,0:T(8,128)(2,1)S(1)} %collective-permute-done.key_value_ref), channel_id=1, source_target_pairs={{0,4},{4,0},{8,12},{12,8},{16,20},{20,16},{24,28},{28,24},{1,5},{5... | collective-permute-start | bytes 393224 | tf_op jit(solution)/shard_map/ppermute | solution.py:26
  13.4 10.9 %collective-permute-start.1 = (bf16[512,128]{1,0:T(8,128)(2,1)S(1)}, bf16[512,128]{1,0:T(8,128)(2,1)S(1)}, u32[]{:S(2)}, u32[]{:S(2)}) collective-permute-start(bf16[512,128]{1,0:T(8,128)(2,1)S(1)} %get-tuple-element.37), channel_id=1, source_target_pairs={{0,24},{4,28},{8,0},{12,4},{16,8},{20,12},{24,16},{28,20},{1,25},{... | collective-permute-start | bytes 393224 | tf_op jit(solution)/shard_map/ppermute | solution.py:26
  16.1 8.2 %collective-permute-start.3 = (bf16[512,128]{1,0:T(8,128)(2,1)S(1)}, bf16[512,128]{1,0:T(8,128)(2,1)S(1)}, u32[]{:S(2)}, u32[]{:S(2)}) collective-permute-start(bf16[512,128]{1,0:T(8,128)(2,1)S(1)} %get-tuple-element.39), channel_id=1, source_target_pairs={{0,20},{4,0},{8,28},{12,8},{16,4},{20,16},{24,12},{28,24},{1,21},{... | collective-permute-start | bytes 393224 | tf_op jit(solution)/shard_map/ppermute | solution.py:26
  18.9 5.9 %collective-permute-start.5 = (bf16[512,128]{1,0:T(8,128)(2,1)S(1)}, bf16[512,128]{1,0:T(8,128)(2,1)S(1)}, u32[]{:S(2)}, u32[]{:S(2)}) collective-permute-start(bf16[512,128]{1,0:T(8,128)(2,1)S(1)} %get-tuple-element.41), channel_id=1, source_target_pairs={{0,24},{4,28},{8,4},{12,0},{16,12},{20,8},{24,20},{28,16},{1,25},{... | collective-permute-start | bytes 393224 | tf_op jit(solution)/shard_map/ppermute | solution.py:26
  25.2 1.8 %collective-permute-start.7 = (bf16[256,768]{1,0:T(8,128)(2,1)S(1)}, bf16[256,768]{1,0:T(8,128)(2,1)S(1)}, u32[]{:S(2)}, u32[]{:S(2)}) collective-permute-start(bf16[256,768]{1,0:T(8,128)(2,1)S(1)} %term.8.refs_0_), channel_id=1, source_target_pairs={{0,1},{1,0},{2,3},{3,2},{4,5},{5,4},{6,7},{7,6},{8,9},{9,8},{10,11... | collective-permute-start | bytes 1179656 | tf_op jit(solution)/shard_map/ppermute | solution.py:26
  27.0 12.0 %collective-permute-start.8 = (bf16[256,768]{1,0:T(8,128)(2,1)S(1)}, bf16[256,768]{1,0:T(8,128)(2,1)S(1)}, u32[]{:S(2)}, u32[]{:S(2)}) collective-permute-start(bf16[256,768]{1,0:T(8,128)(2,1)S(1)} %sum.1.refs_1_), channel_id=1, source_target_pairs={{0,2},{1,3},{2,0},{3,1},{4,6},{5,7},{6,4},{7,5},{8,10},{9,11},{10,... | collective-permute-start | bytes 1179656 | tf_op jit(solution)/shard_map/ppermute | solution.py:26
  28.6 2.5 %collective-permute-start.9 = (bf16[256,512]{1,0:T(8,128)(2,1)S(1)}, bf16[256,512]{1,0:T(8,128)(2,1)S(1)}, u32[]{:S(2)}, u32[]{:S(2)}) collective-permute-start(bf16[256,512]{1,0:T(8,128)(2,1)S(1)} %term.11.refs_0_), channel_id=1, source_target_pairs={{0,1},{1,0},{2,3},{3,2},{4,5},{5,4},{6,7},{7,6},{8,9},{9,8},{10,11... | collective-permute-start | bytes 786440 | tf_op jit(solution)/shard_map/ppermute | solution.py:26
  28.6 1.7 %collective-permute-start.10 = (bf16[256,256]{1,0:T(8,128)(2,1)S(1)}, bf16[256,256]{1,0:T(8,128)(2,1)S(1)}, u32[]{:S(2)}, u32[]{:S(2)}) collective-permute-start(bf16[256,256]{1,0:T(8,128)(2,1)S(1)} %term.9.refs_0_), channel_id=1, source_target_pairs={{0,1},{1,0},{2,3},{3,2},{4,5},{5,4},{6,7},{7,6},{8,9},{9,8},{10,11... | collective-permute-start | bytes 393224 | tf_op jit(solution)/shard_map/ppermute | solution.py:26
  29.1 10.2 %collective-permute-start.6 = (bf16[256,512]{1,0:T(8,128)(2,1)S(1)}, bf16[256,512]{1,0:T(8,128)(2,1)S(1)}, u32[]{:S(2)}, u32[]{:S(2)}) collective-permute-start(bf16[256,512]{1,0:T(8,128)(2,1)S(1)} %term.10.refs_0_), channel_id=1, source_target_pairs={{0,1},{1,0},{2,3},{3,2},{4,5},{5,4},{6,7},{7,6},{8,9},{9,8},{10,11... | collective-permute-start | bytes 786440 | tf_op jit(solution)/shard_map/ppermute | solution.py:26
  30.6 10.5 %collective-permute-start.11 = (bf16[256,256]{1,0:T(8,128)(2,1)S(1)}, bf16[256,256]{1,0:T(8,128)(2,1)S(1)}, u32[]{:S(2)}, u32[]{:S(2)}) collective-permute-start(bf16[256,256]{1,0:T(8,128)(2,1)S(1)} %term.15), channel_id=1, source_target_pairs={{0,2},{1,3},{2,0},{3,1},{4,6},{5,7},{6,4},{7,5},{8,10},{9,11},{10,... | collective-permute-start | bytes 393224 | tf_op jit(solution)/shard_map/ppermute | solution.py:26

commit v8 on v5

--- a/solution.py
+++ b/solution.py
@@ -106,7 +106,7 @@
     ]
     for copy in copies:
         copy.start()
-    for copy in copies:
+    for copy in copies[2:5]:
         copy.wait()
     block_id = lax.axis_index("ctx")
     first_head = lax.axis_index("tp") * heads
@@ -121,6 +121,8 @@
     for offset in range(mask_ref.shape[1]):
         active = (block_id >= offset) & (mask_ref[0, offset] == 1)
         rows_ref[pl.ds(offset * heads, heads), :] = jnp.where(active, norms, f32(jnp.inf))
+    for copy in copies[:2] + copies[5:]:
+        copy.wait()
 
 
 def with_copies(loads, results, refs):
@@ -370,7 +372,7 @@
 
     operands = (sums, query_term, weights)
     hops = range(2, tp_size, 2)
-    sizes = (cols * 5 // 8, cols * 3 // 8) if cols % 1024 == 0 else (cols // 2,) * 2
+    sizes = (cols * 3 // 4, cols // 4) if cols % 1024 == 0 else (cols // 2,) * 2
     starts = (0, sizes[0])
     low, high = 10**6, block_cost.flops
 

time: 42 us -> 42.1 us (level)
  no operation moved by 1% of the time
where the time goes in v8:
time: 42.1 us; the launch traced here: 41.9 us
  starting transfers between devices  16.2 us (38%)
  waiting for transfers between devices  12.8 us (30%)
  Pallas kernels  12.7 us (30%)
    ppermute x11, waiting for transfers between devices, moved(): lax.ppermute(array, axis, [(i, place(i) % count) for i in range(count)])  12.8 us
    ppermute x11, starting transfers between devices, moved(): lax.ppermute(array, axis, [(i, place(i) % count) for i in range(count)])  12.8 us
    pallas_call x3, Pallas kernels, on_device(): pl.pallas_call(functools.partial(pair_kernel, offsets, window, heads, len...  4.39 us
    ppermute x1, starting transfers between devices, on_device(): lax.ppermute(key_value, 'ctx', [pair for pair in pairs if pair[1] < count])  3.39 us
    pallas_call x8, Pallas kernels, term(): pl.pallas_call(functools.partial(term_kernel, pieces, first), in_specs=[i...  2.18 us
    pallas_call x1, Pallas kernels, on_device(): pl.pallas_call(query_term_kernel, in_specs=[in_vmem] * 4, out_specs=[in_v...  1.64 us
    pallas_call x2, Pallas kernels, on_device(): pl.pallas_call(functools.partial(finish_kernel, starts[i], len(hops)), in...  1.54 us
    pallas_call x1, Pallas kernels, on_device(): pl.pallas_call(functools.partial(own_kernel, window, heads), in_specs=[in...  1.43 us
  transfers between devices with their start and end apart: 12, of which 6 were waited for; matrix products, arithmetic and copies ran while one was open for 0% of the time, Pallas kernels for 24%

profile of v8, /device:TPU:0, one launch (start us, length us, event | category | flops | bytes accessed | tf_op | source)
XLA Modules:
  0.0 41.9 jit_solution(16013411134244969361)
XLA Ops:
  0.0 1.4 %load.1 = (bf16[512,128]{1,0:T(8,128)(2,1)S(1)}, bf16[256,512]{1,0:T(8,128)(2,1)S(1)}, bf16[256,512]{1,0:T(8,128)(2,1)S(1)}, bf16[256,512]{1,0:T(8,128)(2,1)S(1)...) custom-call(bf16[256,128]{1,0:T(8,128)(2,1)} %key_hbm.1, bf16[256,128]{1,0:T(8,128)(2,1)} %value_hbm.1, ...), custom_call_target="tpu_custom_call" | custom-call | tf_op jit(solution)/shard_map/load/pallas_call | solution.py:281
  1.4 3.1 %collective-permute-start = (bf16[512,128]{1,0:T(8,128)(2,1)S(1)}, bf16[512,128]{1,0:T(8,128)(2,1)S(1)}, u32[]{:S(2)}, u32[]{:S(2)}) collective-permute-start(bf16[512,128]{1,0:T(8,128)(2,1)S(1)} %get-tuple-element.26.key_value_ref), channel_id=1, source_target_pairs={{0,8},{4,12},{8,16},{12,20},{16,24},{20,28},{24,0},{28,4},{1,9},{5... | collective-permute-start | bytes 393224 | tf_op jit(solution)/shard_map/ppermute | solution.py:26
  4.5 3.4 %collective-permute-start.2 = (bf16[512,128]{1,0:T(8,128)(2,1)S(1)}, bf16[512,128]{1,0:T(8,128)(2,1)S(1)}, u32[]{:S(2)}, u32[]{:S(2)}) collective-permute-start(bf16[512,128]{1,0:T(8,128)(2,1)S(1)} %get-tuple-element.26.key_value_ref), channel_id=1, source_target_pairs={{0,4},{4,16},{8,12},{12,24},{16,20},{24,28},{1,5},{5,17},{9,13},{1... | collective-permute-start | bytes 393224 | tf_op jit(solution)/shard_map/ppermute | solution.py:304
  7.9 1.4 %own_block.1 = (f32[4,256]{1,0:T(4,128)S(1)}, f32[128,1024]{1,0:T(8,128)S(1)}, f32[512,128]{1,0:T(8,128)S(1)}) custom-call(bf16[512,128]{1,0:T(8,128)(2,1)S(1)} %get-tuple-element.26.key_value_ref, bf16[256,512]{1,0:T(8,128)(2,1)S(1)} %get-tuple-element.27.query_ref, bf16[256,512]{1,0:T(8,128)(2,1)S(1)} %get-tuple-element.28.grad_ref, ...), custom_call_target="tpu_custom_call" | custom-call | flops 1000000 | bytes 2500 | tf_op jit(solution)/shard_map/own_block/pallas_call | solution.py:307
  9.3 0.7 %collective-permute-done.key_value_ref = bf16[512,128]{1,0:T(8,128)(2,1)S(1)} collective-permute-done((bf16[512,128]{1,0:T(8,128)(2,1)S(1)}, bf16[512,128]{1,0:T(8,128)(2,1)S(1)}, u32[]{:S(2)}, u32[]{:S(2)}) %collective-permute-start) | collective-permute-done | bytes 131104 | tf_op jit(solution)/shard_map/ppermute | solution.py:26
  10.0 1.9 %collective-permute-start.4 = (bf16[512,128]{1,0:T(8,128)(2,1)S(1)}, bf16[512,128]{1,0:T(8,128)(2,1)S(1)}, u32[]{:S(2)}, u32[]{:S(2)}) collective-permute-start(bf16[512,128]{1,0:T(8,128)(2,1)S(1)} %collective-permute-done.key_value_ref), channel_id=1, source_target_pairs={{0,4},{4,0},{8,12},{12,8},{16,20},{20,16},{24,28},{28,24},{1,5},{5... | collective-permute-start | bytes 393224 | tf_op jit(solution)/shard_map/ppermute | solution.py:26
  12.0 1.6 %block_back_22.1 = (f32[128,1024]{1,0:T(8,128)S(1)}, bf16[512,128]{1,0:T(8,128)(2,1)S(1)}, bf16[4096,128]{1,0:T(8,128)(2,1)S(1)}, bf16[4096,128]{1,0:T(8,128)(2,1)S(1)}) custom-call(bf16[512,128]{1,0:T(8,128)(2,1)S(1)} %collective-permute-done.key_value_ref, bf16[256,512]{1,0:T(8,128)(2,1)S(1)} %get-tuple-element.27.query_ref, ...), custom_call_target="tpu_custom_call" | custom-call | flops 1000000 | bytes 2500 | tf_op jit(solution)/shard_map/block_back_22/pallas_call | solution.py:327
  13.5 1.3 %collective-permute-start.1 = (bf16[512,128]{1,0:T(8,128)(2,1)S(1)}, bf16[512,128]{1,0:T(8,128)(2,1)S(1)}, u32[]{:S(2)}, u32[]{:S(2)}) collective-permute-start(bf16[512,128]{1,0:T(8,128)(2,1)S(1)} %get-tuple-element.37), channel_id=1, source_target_pairs={{0,24},{4,28},{8,0},{12,4},{16,8},{20,12},{24,16},{28,20},{1,25},{... | collective-permute-start | bytes 393224 | tf_op jit(solution)/shard_map/ppermute | solution.py:26
  14.9 1.4 %block_back_31.1 = (f32[128,1024]{1,0:T(8,128)S(1)}, bf16[512,128]{1,0:T(8,128)(2,1)S(1)}) custom-call(bf16[512,128]{1,0:T(8,128)(2,1)S(1)} %collective-permute-done.2.key_value_ref, bf16[256,512]{1,0:T(8,128)(2,1)S(1)} %get-tuple-element.27.query_ref, bf16[256,512]{1,0:T(8,128)(2,1)S(1)} %get-tuple-element.28.grad_ref, ...), custom_call_target="tpu_custom_call" | custom-call | flops 1000000 | bytes 2500 | tf_op jit(solution)/shard_map/block_back_31/pallas_call | solution.py:327
  16.3 1.3 %collective-permute-start.3 = (bf16[512,128]{1,0:T(8,128)(2,1)S(1)}, bf16[512,128]{1,0:T(8,128)(2,1)S(1)}, u32[]{:S(2)}, u32[]{:S(2)}) collective-permute-start(bf16[512,128]{1,0:T(8,128)(2,1)S(1)} %get-tuple-element.39), channel_id=1, source_target_pairs={{0,20},{4,0},{8,28},{12,8},{16,4},{20,16},{24,12},{28,24},{1,21},{... | collective-permute-start | bytes 393224 | tf_op jit(solution)/shard_map/ppermute | solution.py:26
  17.6 1.4 %block_back_13.1 = (bf16[256,512]{1,0:T(8,128)(2,1)S(1)}, bf16[512,128]{1,0:T(8,128)(2,1)S(1)}) custom-call(bf16[512,128]{1,0:T(8,128)(2,1)S(1)} %collective-permute-done.4.key_value_ref, bf16[256,512]{1,0:T(8,128)(2,1)S(1)} %get-tuple-element.27.query_ref, bf16[256,512]{1,0:T(8,128)(2,1)S(1)} %get-tuple-element.28.grad_ref, ...), custom_call_target="tpu_custom_call" | custom-call | flops 1000000 | bytes 2500 | tf_op jit(solution)/shard_map/block_back_13/pallas_call | solution.py:327
  19.0 2.4 %collective-permute-start.5 = (bf16[512,128]{1,0:T(8,128)(2,1)S(1)}, bf16[512,128]{1,0:T(8,128)(2,1)S(1)}, u32[]{:S(2)}, u32[]{:S(2)}) collective-permute-start(bf16[512,128]{1,0:T(8,128)(2,1)S(1)} %get-tuple-element.41), channel_id=1, source_target_pairs={{0,24},{4,28},{8,4},{12,0},{16,12},{20,8},{24,20},{28,16},{1,25},{... | collective-permute-start | bytes 393224 | tf_op jit(solution)/shard_map/ppermute | solution.py:26
  21.4 1.6 %query_term.1 = (f32[4,256,1024]{2,1,0:T(8,128)S(1)}, bf16[4096,256]{1,0:T(8,128)(2,1)S(1)}) custom-call(bf16[256,512]{1,0:T(8,128)(2,1)S(1)} %get-tuple-element.42.query_ref, bf16[4096,512]{1,0:T(8,128)(2,1)S(1)} %copy-done, bf16[4096,128]{1,0:T(8,128)(2,1)S(1)} %get-tuple-element.43.wk_ref, bf16[4096,128]{1,0:T(8,128)(2,1)S(1)} %get-tuple-element.44.wv_ref), custom_call_target="tpu_custom_call" | custom-call | flops 671088640 | bytes 1677721 | tf_op jit(solution)/shard_map/query_term/pallas_call | solution.py:349
  23.1 1.8 %collective-permute-done.5.right_ref = bf16[512,128]{1,0:T(8,128)(2,1)S(1)} collective-permute-done((bf16[512,128]{1,0:T(8,128)(2,1)S(1)}, bf16[512,128]{1,0:T(8,128)(2,1)S(1)}, u32[]{:S(2)}, u32[]{:S(2)}) %collective-permute-start.5) | collective-permute-done | bytes 131104 | tf_op jit(solution)/shard_map/ppermute | solution.py:26
  25.0 0.3 term.8.refs_0_
  25.3 0.1 collective-permute-start.7
  25.4 0.2 term.9.refs_0_
  25.6 0.3 term.10.refs_0_
  25.9 0.3 term.11.refs_0_
  26.2 0.3 term.12.left_ref
  26.5 0.6 %collective-permute-done.7.right_ref = bf16[256,768]{1,0:T(8,128)(2,1)S(1)} collective-permute-done((bf16[256,768]{1,0:T(8,128)(2,1)S(1)}, bf16[256,768]{1,0:T(8,128)(2,1)S(1)}, u32[]{:S(2)}, u32[]{:S(2)}) %collective-permute-start.7) | collective-permute-done | bytes 393248 | tf_op jit(solution)/shard_map/ppermute | solution.py:26
  27.2 1.6 %collective-permute-start.8 = (bf16[256,768]{1,0:T(8,128)(2,1)S(1)}, bf16[256,768]{1,0:T(8,128)(2,1)S(1)}, u32[]{:S(2)}, u32[]{:S(2)}) collective-permute-start(bf16[256,768]{1,0:T(8,128)(2,1)S(1)} %sum.1.refs_1_), channel_id=1, source_target_pairs={{0,2},{1,3},{2,0},{3,1},{4,6},{5,7},{6,4},{7,5},{8,10},{9,11},{10,... | collective-permute-start | bytes 1179656 | tf_op jit(solution)/shard_map/ppermute | solution.py:26
  28.8 0.5 %collective-permute-start.10 = (bf16[256,256]{1,0:T(8,128)(2,1)S(1)}, bf16[256,256]{1,0:T(8,128)(2,1)S(1)}, u32[]{:S(2)}, u32[]{:S(2)}) collective-permute-start(bf16[256,256]{1,0:T(8,128)(2,1)S(1)} %term.9.refs_0_), channel_id=1, source_target_pairs={{0,1},{1,0},{2,3},{3,2},{4,5},{5,4},{6,7},{7,6},{8,9},{9,8},{10,11... | collective-permute-start | bytes 393224 | tf_op jit(solution)/shard_map/ppermute | solution.py:26
  29.3 1.2 %collective-permute-done.10.refs_0_ = bf16[256,256]{1,0:T(8,128)(2,1)S(1)} collective-permute-done((bf16[256,256]{1,0:T(8,128)(2,1)S(1)}, bf16[256,256]{1,0:T(8,128)(2,1)S(1)}, u32[]{:S(2)}, u32[]{:S(2)}) %collective-permute-start.10) | collective-permute-done | bytes 131104 | tf_op jit(solution)/shard_map/ppermute | solution.py:26
  30.5 0.2 term.15
  30.7 0.6 %collective-permute-start.11 = (bf16[256,256]{1,0:T(8,128)(2,1)S(1)}, bf16[256,256]{1,0:T(8,128)(2,1)S(1)}, u32[]{:S(2)}, u32[]{:S(2)}) collective-permute-start(bf16[256,256]{1,0:T(8,128)(2,1)S(1)} %term.15), channel_id=1, source_target_pairs={{0,2},{1,3},{2,0},{3,1},{4,6},{5,7},{6,4},{7,5},{8,10},{9,11},{10,... | collective-permute-start | bytes 393224 | tf_op jit(solution)/shard_map/ppermute | solution.py:26
  31.3 7.9 %collective-permute-done.8.refs_1_.refs_0_ = bf16[256,768]{1,0:T(8,128)(2,1)S(1)} collective-permute-done((bf16[256,768]{1,0:T(8,128)(2,1)S(1)}, bf16[256,768]{1,0:T(8,128)(2,1)S(1)}, u32[]{:S(2)}, u32[]{:S(2)}) %collective-permute-start.8) | collective-permute-done | bytes 393248 | tf_op jit(solution)/shard_map/ppermute | solution.py:26
  39.2 0.3 term.14.high_ref
  39.5 0.3 term.13.low_ref
  39.7 0.8 %finish.2.refs_1_ = bf16[256,1024]{1,0:T(8,128)(2,1)} custom-call(f32[256,512]{1,0:T(8,128)S(1)} %term.13.low_ref, f32[256,512]{1,0:T(8,128)S(1)} %term.14.high_ref, bf16[256,768]{1,0:T(8,128)(2,1)S(1)} %collective-permute-done.8.refs_1_.refs_0_), custom_call_target="tpu_custom_call" | custom-call | flops 1000000 | bytes 2500 | tf_op jit(solution)/shard_map/finish/pallas_call | solution.py:417
  40.6 0.6 %collective-permute-done.11.refs_0_ = bf16[256,256]{1,0:T(8,128)(2,1)S(1)} collective-permute-done((bf16[256,256]{1,0:T(8,128)(2,1)S(1)}, bf16[256,256]{1,0:T(8,128)(2,1)S(1)}, u32[]{:S(2)}, u32[]{:S(2)}) %collective-permute-start.11) | collective-permute-done | bytes 131104 | tf_op jit(solution)/shard_map/ppermute | solution.py:26
  41.2 0.7 %finish.3 = bf16[256,1024]{1,0:T(8,128)(2,1)} custom-call(f32[256,512]{1,0:T(8,128)S(1)} %term.13.low_ref, f32[256,512]{1,0:T(8,128)S(1)} %term.14.high_ref, bf16[256,256]{1,0:T(8,128)(2,1)S(1)} %collective-permute-done.11.refs_0_, bf16[256,1024]{1,0:T(8,128)(2,1)} %finish.2.refs_1_), custom_call_target="tpu_custom_call", output_to_operand_aliasing={{}: (3, {})} | custom-call | flops 1000000 | bytes 2500 | tf_op jit(solution)/shard_map/finish/pallas_call | solution.py:417
  (14 shorter events, 0.2 us)
Async XLA Ops:
  0.0 21.4 %copy-start = (bf16[4096,512]{1,0:T(8,128)(2,1)S(1)}, bf16[4096,512]{1,0:T(8,128)(2,1)}, u32[]{:S(2)}) copy-start(bf16[4096,512]{1,0:T(8,128)(2,1)} %wq_ref.1) | copy-start | bytes 12582916
  1.4 8.6 %collective-permute-start = (bf16[512,128]{1,0:T(8,128)(2,1)S(1)}, bf16[512,128]{1,0:T(8,128)(2,1)S(1)}, u32[]{:S(2)}, u32[]{:S(2)}) collective-permute-start(bf16[512,128]{1,0:T(8,128)(2,1)S(1)} %get-tuple-element.26.key_value_ref), channel_id=1, source_target_pairs={{0,8},{4,12},{8,16},{12,20},{16,24},{20,28},{24,0},{28,4},{1,9},{5... | collective-permute-start | bytes 393224 | tf_op jit(solution)/shard_map/ppermute | solution.py:26
  4.5 10.4 %collective-permute-start.2 = (bf16[512,128]{1,0:T(8,128)(2,1)S(1)}, bf16[512,128]{1,0:T(8,128)(2,1)S(1)}, u32[]{:S(2)}, u32[]{:S(2)}) collective-permute-start(bf16[512,128]{1,0:T(8,128)(2,1)S(1)} %get-tuple-element.26.key_value_ref), channel_id=1, source_target_pairs={{0,4},{4,16},{8,12},{12,24},{16,20},{24,28},{1,5},{5,17},{9,13},{1... | collective-permute-start | bytes 393224 | tf_op jit(solution)/shard_map/ppermute | solution.py:304
  10.0 7.6 %collective-permute-start.4 = (bf16[512,128]{1,0:T(8,128)(2,1)S(1)}, bf16[512,128]{1,0:T(8,128)(2,1)S(1)}, u32[]{:S(2)}, u32[]{:S(2)}) collective-permute-start(bf16[512,128]{1,0:T(8,128)(2,1)S(1)} %collective-permute-done.key_value_ref), channel_id=1, source_target_pairs={{0,4},{4,0},{8,12},{12,8},{16,20},{20,16},{24,28},{28,24},{1,5},{5... | collective-permute-start | bytes 393224 | tf_op jit(solution)/shard_map/ppermute | solution.py:26
  13.5 9.5 %collective-permute-start.1 = (bf16[512,128]{1,0:T(8,128)(2,1)S(1)}, bf16[512,128]{1,0:T(8,128)(2,1)S(1)}, u32[]{:S(2)}, u32[]{:S(2)}) collective-permute-start(bf16[512,128]{1,0:T(8,128)(2,1)S(1)} %get-tuple-element.37), channel_id=1, source_target_pairs={{0,24},{4,28},{8,0},{12,4},{16,8},{20,12},{24,16},{28,20},{1,25},{... | collective-permute-start | bytes 393224 | tf_op jit(solution)/shard_map/ppermute | solution.py:26
  16.3 6.8 %collective-permute-start.3 = (bf16[512,128]{1,0:T(8,128)(2,1)S(1)}, bf16[512,128]{1,0:T(8,128)(2,1)S(1)}, u32[]{:S(2)}, u32[]{:S(2)}) collective-permute-start(bf16[512,128]{1,0:T(8,128)(2,1)S(1)} %get-tuple-element.39), channel_id=1, source_target_pairs={{0,20},{4,0},{8,28},{12,8},{16,4},{20,16},{24,12},{28,24},{1,21},{... | collective-permute-start | bytes 393224 | tf_op jit(solution)/shard_map/ppermute | solution.py:26
  19.0 5.9 %collective-permute-start.5 = (bf16[512,128]{1,0:T(8,128)(2,1)S(1)}, bf16[512,128]{1,0:T(8,128)(2,1)S(1)}, u32[]{:S(2)}, u32[]{:S(2)}) collective-permute-start(bf16[512,128]{1,0:T(8,128)(2,1)S(1)} %get-tuple-element.41), channel_id=1, source_target_pairs={{0,24},{4,28},{8,4},{12,0},{16,12},{20,8},{24,20},{28,16},{1,25},{... | collective-permute-start | bytes 393224 | tf_op jit(solution)/shard_map/ppermute | solution.py:26
  25.3 1.8 %collective-permute-start.7 = (bf16[256,768]{1,0:T(8,128)(2,1)S(1)}, bf16[256,768]{1,0:T(8,128)(2,1)S(1)}, u32[]{:S(2)}, u32[]{:S(2)}) collective-permute-start(bf16[256,768]{1,0:T(8,128)(2,1)S(1)} %term.8.refs_0_), channel_id=1, source_target_pairs={{0,1},{1,0},{2,3},{3,2},{4,5},{5,4},{6,7},{7,6},{8,9},{9,8},{10,11... | collective-permute-start | bytes 1179656 | tf_op jit(solution)/shard_map/ppermute | solution.py:26
  27.2 12.0 %collective-permute-start.8 = (bf16[256,768]{1,0:T(8,128)(2,1)S(1)}, bf16[256,768]{1,0:T(8,128)(2,1)S(1)}, u32[]{:S(2)}, u32[]{:S(2)}) collective-permute-start(bf16[256,768]{1,0:T(8,128)(2,1)S(1)} %sum.1.refs_1_), channel_id=1, source_target_pairs={{0,2},{1,3},{2,0},{3,1},{4,6},{5,7},{6,4},{7,5},{8,10},{9,11},{10,... | collective-permute-start | bytes 1179656 | tf_op jit(solution)/shard_map/ppermute | solution.py:26
  28.7 2.5 %collective-permute-start.9 = (bf16[256,512]{1,0:T(8,128)(2,1)S(1)}, bf16[256,512]{1,0:T(8,128)(2,1)S(1)}, u32[]{:S(2)}, u32[]{:S(2)}) collective-permute-start(bf16[256,512]{1,0:T(8,128)(2,1)S(1)} %term.11.refs_0_), channel_id=1, source_target_pairs={{0,1},{1,0},{2,3},{3,2},{4,5},{5,4},{6,7},{7,6},{8,9},{9,8},{10,11... | collective-permute-start | bytes 786440 | tf_op jit(solution)/shard_map/ppermute | solution.py:26
  28.8 1.7 %collective-permute-start.10 = (bf16[256,256]{1,0:T(8,128)(2,1)S(1)}, bf16[256,256]{1,0:T(8,128)(2,1)S(1)}, u32[]{:S(2)}, u32[]{:S(2)}) collective-permute-start(bf16[256,256]{1,0:T(8,128)(2,1)S(1)} %term.9.refs_0_), channel_id=1, source_target_pairs={{0,1},{1,0},{2,3},{3,2},{4,5},{5,4},{6,7},{7,6},{8,9},{9,8},{10,11... | collective-permute-start | bytes 393224 | tf_op jit(solution)/shard_map/ppermute | solution.py:26
  29.3 10.2 %collective-permute-start.6 = (bf16[256,512]{1,0:T(8,128)(2,1)S(1)}, bf16[256,512]{1,0:T(8,128)(2,1)S(1)}, u32[]{:S(2)}, u32[]{:S(2)}) collective-permute-start(bf16[256,512]{1,0:T(8,128)(2,1)S(1)} %term.10.refs_0_), channel_id=1, source_target_pairs={{0,1},{1,0},{2,3},{3,2},{4,5},{5,4},{6,7},{7,6},{8,9},{9,8},{10,11... | collective-permute-start | bytes 786440 | tf_op jit(solution)/shard_map/ppermute | solution.py:26
  30.7 10.5 %collective-permute-start.11 = (bf16[256,256]{1,0:T(8,128)(2,1)S(1)}, bf16[256,256]{1,0:T(8,128)(2,1)S(1)}, u32[]{:S(2)}, u32[]{:S(2)}) collective-permute-start(bf16[256,256]{1,0:T(8,128)(2,1)S(1)} %term.15), channel_id=1, source_target_pairs={{0,2},{1,3},{2,0},{3,1},{4,6},{5,7},{6,4},{7,5},{8,10},{9,11},{10,... | collective-permute-start | bytes 393224 | tf_op jit(solution)/shard_map/ppermute | solution.py:26

commit v9 on v5

--- a/solution.py
+++ b/solution.py
@@ -240,15 +240,23 @@
 def finish_kernel(first, hops, low_ref, high_ref, *refs):
     out_hbm, held, sem = refs[-3:]
     half, size = low_ref.shape[1], held.shape[1]
+    copies = []
     for start in range(first, first + size, 128):
         ref, at = (low_ref, start) if start < half else (high_ref, start - half)
         total = ref[:, pl.ds(at, 128)]
         for ref in refs[:hops]:
             total = total + ref[:, pl.ds(start - first, 128)].astype(f32)
         held[:, pl.ds(start - first, 128)] = total.astype(bf16)
-    copy = pltpu.make_async_copy(held, out_hbm.at[:, pl.ds(first, size)], sem)
-    copy.start()
-    copy.wait()
+        copies.append(
+            pltpu.make_async_copy(
+                held.at[:, pl.ds(start - first, 128)],
+                out_hbm.at[:, pl.ds(start, 128)],
+                sem.at[len(copies)],
+            )
+        )
+        copies[-1].start()
+    for copy in copies:
+        copy.wait()
 
 
 def cost(flops):
@@ -418,7 +426,10 @@
             out_specs=in_hbm,
             out_shape=shape((rows, cols), bf16),
             input_output_aliases={2 + len(hops): 0} if out else {},
-            scratch_shapes=[pltpu.VMEM((rows, sizes[i]), bf16), pltpu.SemaphoreType.DMA],
+            scratch_shapes=[
+                pltpu.VMEM((rows, sizes[i]), bf16),
+                pltpu.SemaphoreType.DMA((sizes[i] // 128,)),
+            ],
             compiler_params=params,
             cost_estimate=cost(low),
             name="finish",

time: 42 us -> 42 us (level)
  no operation moved by 1% of the time
where the time goes in v9:
time: 42 us; the launch traced here: 41.8 us
  starting transfers between devices  16.2 us (39%)
  Pallas kernels  12.7 us (30%)
  waiting for transfers between devices  12.7 us (30%)
    ppermute x11, starting transfers between devices, moved(): lax.ppermute(array, axis, [(i, place(i) % count) for i in range(count)])  12.8 us
    ppermute x11, waiting for transfers between devices, moved(): lax.ppermute(array, axis, [(i, place(i) % count) for i in range(count)])  12.7 us
    pallas_call x3, Pallas kernels, on_device(): pl.pallas_call(functools.partial(pair_kernel, offsets, window, heads, len...  4.38 us
    ppermute x1, starting transfers between devices, on_device(): lax.ppermute(key_value, 'ctx', [pair for pair in pairs if pair[1] < count])  3.39 us
    pallas_call x8, Pallas kernels, term(): pl.pallas_call(functools.partial(term_kernel, pieces, first), in_specs=[i...  2.23 us
    pallas_call x1, Pallas kernels, on_device(): pl.pallas_call(query_term_kernel, in_specs=[in_vmem] * 4, out_specs=[in_v...  1.64 us
    pallas_call x2, Pallas kernels, on_device(): pl.pallas_call(functools.partial(finish_kernel, starts[i], len(hops)), in...  1.5 us
    pallas_call x1, Pallas kernels, on_device(): pl.pallas_call(functools.partial(own_kernel, window, heads), in_specs=[in...  1.43 us
  transfers between devices with their start and end apart: 12, of which 6 were waited for; matrix products, arithmetic and copies ran while one was open for 0% of the time, Pallas kernels for 24%

profile of v9, /device:TPU:0, one launch (start us, length us, event | category | flops | bytes accessed | tf_op | source)
XLA Modules:
  0.0 41.8 jit_solution(13449238009900146470)
XLA Ops:
  0.0 1.4 %load.1 = (bf16[512,128]{1,0:T(8,128)(2,1)S(1)}, bf16[256,512]{1,0:T(8,128)(2,1)S(1)}, bf16[256,512]{1,0:T(8,128)(2,1)S(1)}, bf16[256,512]{1,0:T(8,128)(2,1)S(1)...) custom-call(bf16[256,128]{1,0:T(8,128)(2,1)} %key_hbm.1, bf16[256,128]{1,0:T(8,128)(2,1)} %value_hbm.1, ...), custom_call_target="tpu_custom_call" | custom-call | tf_op jit(solution)/shard_map/load/pallas_call | solution.py:287
  1.4 3.1 %collective-permute-start = (bf16[512,128]{1,0:T(8,128)(2,1)S(1)}, bf16[512,128]{1,0:T(8,128)(2,1)S(1)}, u32[]{:S(2)}, u32[]{:S(2)}) collective-permute-start(bf16[512,128]{1,0:T(8,128)(2,1)S(1)} %get-tuple-element.26.key_value_ref), channel_id=1, source_target_pairs={{0,8},{4,12},{8,16},{12,20},{16,24},{20,28},{24,0},{28,4},{1,9},{5... | collective-permute-start | bytes 393224 | tf_op jit(solution)/shard_map/ppermute | solution.py:26
  4.5 3.4 %collective-permute-start.2 = (bf16[512,128]{1,0:T(8,128)(2,1)S(1)}, bf16[512,128]{1,0:T(8,128)(2,1)S(1)}, u32[]{:S(2)}, u32[]{:S(2)}) collective-permute-start(bf16[512,128]{1,0:T(8,128)(2,1)S(1)} %get-tuple-element.26.key_value_ref), channel_id=1, source_target_pairs={{0,4},{4,16},{8,12},{12,24},{16,20},{24,28},{1,5},{5,17},{9,13},{1... | collective-permute-start | bytes 393224 | tf_op jit(solution)/shard_map/ppermute | solution.py:310
  7.9 1.4 %own_block.1 = (f32[4,256]{1,0:T(4,128)S(1)}, f32[128,1024]{1,0:T(8,128)S(1)}, f32[512,128]{1,0:T(8,128)S(1)}) custom-call(bf16[512,128]{1,0:T(8,128)(2,1)S(1)} %get-tuple-element.26.key_value_ref, bf16[256,512]{1,0:T(8,128)(2,1)S(1)} %get-tuple-element.27.query_ref, bf16[256,512]{1,0:T(8,128)(2,1)S(1)} %get-tuple-element.28.grad_ref, ...), custom_call_target="tpu_custom_call" | custom-call | flops 1000000 | bytes 2500 | tf_op jit(solution)/shard_map/own_block/pallas_call | solution.py:313
  9.3 0.7 %collective-permute-done.key_value_ref = bf16[512,128]{1,0:T(8,128)(2,1)S(1)} collective-permute-done((bf16[512,128]{1,0:T(8,128)(2,1)S(1)}, bf16[512,128]{1,0:T(8,128)(2,1)S(1)}, u32[]{:S(2)}, u32[]{:S(2)}) %collective-permute-start) | collective-permute-done | bytes 131104 | tf_op jit(solution)/shard_map/ppermute | solution.py:26
  10.0 1.9 %collective-permute-start.4 = (bf16[512,128]{1,0:T(8,128)(2,1)S(1)}, bf16[512,128]{1,0:T(8,128)(2,1)S(1)}, u32[]{:S(2)}, u32[]{:S(2)}) collective-permute-start(bf16[512,128]{1,0:T(8,128)(2,1)S(1)} %collective-permute-done.key_value_ref), channel_id=1, source_target_pairs={{0,4},{4,0},{8,12},{12,8},{16,20},{20,16},{24,28},{28,24},{1,5},{5... | collective-permute-start | bytes 393224 | tf_op jit(solution)/shard_map/ppermute | solution.py:26
  12.0 1.6 %block_back_22.1 = (f32[128,1024]{1,0:T(8,128)S(1)}, bf16[512,128]{1,0:T(8,128)(2,1)S(1)}, bf16[4096,128]{1,0:T(8,128)(2,1)S(1)}, bf16[4096,128]{1,0:T(8,128)(2,1)S(1)}) custom-call(bf16[512,128]{1,0:T(8,128)(2,1)S(1)} %collective-permute-done.key_value_ref, bf16[256,512]{1,0:T(8,128)(2,1)S(1)} %get-tuple-element.27.query_ref, ...), custom_call_target="tpu_custom_call" | custom-call | flops 1000000 | bytes 2500 | tf_op jit(solution)/shard_map/block_back_22/pallas_call | solution.py:333
  13.5 1.3 %collective-permute-start.1 = (bf16[512,128]{1,0:T(8,128)(2,1)S(1)}, bf16[512,128]{1,0:T(8,128)(2,1)S(1)}, u32[]{:S(2)}, u32[]{:S(2)}) collective-permute-start(bf16[512,128]{1,0:T(8,128)(2,1)S(1)} %get-tuple-element.37), channel_id=1, source_target_pairs={{0,24},{4,28},{8,0},{12,4},{16,8},{20,12},{24,16},{28,20},{1,25},{... | collective-permute-start | bytes 393224 | tf_op jit(solution)/shard_map/ppermute | solution.py:26
  14.9 1.4 %block_back_31.1 = (f32[128,1024]{1,0:T(8,128)S(1)}, bf16[512,128]{1,0:T(8,128)(2,1)S(1)}) custom-call(bf16[512,128]{1,0:T(8,128)(2,1)S(1)} %collective-permute-done.2.key_value_ref, bf16[256,512]{1,0:T(8,128)(2,1)S(1)} %get-tuple-element.27.query_ref, bf16[256,512]{1,0:T(8,128)(2,1)S(1)} %get-tuple-element.28.grad_ref, ...), custom_call_target="tpu_custom_call" | custom-call | flops 1000000 | bytes 2500 | tf_op jit(solution)/shard_map/block_back_31/pallas_call | solution.py:333
  16.3 1.3 %collective-permute-start.3 = (bf16[512,128]{1,0:T(8,128)(2,1)S(1)}, bf16[512,128]{1,0:T(8,128)(2,1)S(1)}, u32[]{:S(2)}, u32[]{:S(2)}) collective-permute-start(bf16[512,128]{1,0:T(8,128)(2,1)S(1)} %get-tuple-element.39), channel_id=1, source_target_pairs={{0,20},{4,0},{8,28},{12,8},{16,4},{20,16},{24,12},{28,24},{1,21},{... | collective-permute-start | bytes 393224 | tf_op jit(solution)/shard_map/ppermute | solution.py:26
  17.6 1.4 %block_back_13.1 = (bf16[256,512]{1,0:T(8,128)(2,1)S(1)}, bf16[512,128]{1,0:T(8,128)(2,1)S(1)}) custom-call(bf16[512,128]{1,0:T(8,128)(2,1)S(1)} %collective-permute-done.4.key_value_ref, bf16[256,512]{1,0:T(8,128)(2,1)S(1)} %get-tuple-element.27.query_ref, bf16[256,512]{1,0:T(8,128)(2,1)S(1)} %get-tuple-element.28.grad_ref, ...), custom_call_target="tpu_custom_call" | custom-call | flops 1000000 | bytes 2500 | tf_op jit(solution)/shard_map/block_back_13/pallas_call | solution.py:333
  19.0 2.4 %collective-permute-start.5 = (bf16[512,128]{1,0:T(8,128)(2,1)S(1)}, bf16[512,128]{1,0:T(8,128)(2,1)S(1)}, u32[]{:S(2)}, u32[]{:S(2)}) collective-permute-start(bf16[512,128]{1,0:T(8,128)(2,1)S(1)} %get-tuple-element.41), channel_id=1, source_target_pairs={{0,24},{4,28},{8,4},{12,0},{16,12},{20,8},{24,20},{28,16},{1,25},{... | collective-permute-start | bytes 393224 | tf_op jit(solution)/shard_map/ppermute | solution.py:26
  21.4 1.6 %query_term.1 = (f32[4,256,1024]{2,1,0:T(8,128)S(1)}, bf16[4096,256]{1,0:T(8,128)(2,1)S(1)}) custom-call(bf16[256,512]{1,0:T(8,128)(2,1)S(1)} %get-tuple-element.42.query_ref, bf16[4096,512]{1,0:T(8,128)(2,1)S(1)} %copy-done, bf16[4096,128]{1,0:T(8,128)(2,1)S(1)} %get-tuple-element.43.wk_ref, bf16[4096,128]{1,0:T(8,128)(2,1)S(1)} %get-tuple-element.44.wv_ref), custom_call_target="tpu_custom_call" | custom-call | flops 671088640 | bytes 1677721 | tf_op jit(solution)/shard_map/query_term/pallas_call | solution.py:355
  23.1 1.8 %collective-permute-done.5.right_ref = bf16[512,128]{1,0:T(8,128)(2,1)S(1)} collective-permute-done((bf16[512,128]{1,0:T(8,128)(2,1)S(1)}, bf16[512,128]{1,0:T(8,128)(2,1)S(1)}, u32[]{:S(2)}, u32[]{:S(2)}) %collective-permute-start.5) | collective-permute-done | bytes 131104 | tf_op jit(solution)/shard_map/ppermute | solution.py:26
  25.0 0.3 term.8.refs_0_
  25.3 0.1 collective-permute-start.7
  25.4 0.3 term.9.refs_0_
  25.7 0.3 term.10.refs_0_
  25.9 0.3 term.11.refs_0_
  26.2 0.3 term.12.left_ref
  26.5 0.5 %collective-permute-done.7.right_ref = bf16[256,640]{1,0:T(8,128)(2,1)S(1)} collective-permute-done((bf16[256,640]{1,0:T(8,128)(2,1)S(1)}, bf16[256,640]{1,0:T(8,128)(2,1)S(1)}, u32[]{:S(2)}, u32[]{:S(2)}) %collective-permute-start.7) | collective-permute-done | bytes 327712 | tf_op jit(solution)/shard_map/ppermute | solution.py:26
  27.1 1.6 %collective-permute-start.8 = (bf16[256,640]{1,0:T(8,128)(2,1)S(1)}, bf16[256,640]{1,0:T(8,128)(2,1)S(1)}, u32[]{:S(2)}, u32[]{:S(2)}) collective-permute-start(bf16[256,640]{1,0:T(8,128)(2,1)S(1)} %sum.1.refs_1_), channel_id=1, source_target_pairs={{0,2},{1,3},{2,0},{3,1},{4,6},{5,7},{6,4},{7,5},{8,10},{9,11},{10,... | collective-permute-start | bytes 983048 | tf_op jit(solution)/shard_map/ppermute | solution.py:26
  28.7 0.5 %collective-permute-start.10 = (bf16[256,384]{1,0:T(8,128)(2,1)S(1)}, bf16[256,384]{1,0:T(8,128)(2,1)S(1)}, u32[]{:S(2)}, u32[]{:S(2)}) collective-permute-start(bf16[256,384]{1,0:T(8,128)(2,1)S(1)} %term.9.refs_0_), channel_id=1, source_target_pairs={{0,1},{1,0},{2,3},{3,2},{4,5},{5,4},{6,7},{7,6},{8,9},{9,8},{10,11... | collective-permute-start | bytes 589832 | tf_op jit(solution)/shard_map/ppermute | solution.py:26
  29.2 1.3 %collective-permute-done.10.refs_0_ = bf16[256,384]{1,0:T(8,128)(2,1)S(1)} collective-permute-done((bf16[256,384]{1,0:T(8,128)(2,1)S(1)}, bf16[256,384]{1,0:T(8,128)(2,1)S(1)}, u32[]{:S(2)}, u32[]{:S(2)}) %collective-permute-start.10) | collective-permute-done | bytes 196640 | tf_op jit(solution)/shard_map/ppermute | solution.py:26
  30.5 0.3 term.15
  30.7 0.6 %collective-permute-start.11 = (bf16[256,384]{1,0:T(8,128)(2,1)S(1)}, bf16[256,384]{1,0:T(8,128)(2,1)S(1)}, u32[]{:S(2)}, u32[]{:S(2)}) collective-permute-start(bf16[256,384]{1,0:T(8,128)(2,1)S(1)} %term.15), channel_id=1, source_target_pairs={{0,2},{1,3},{2,0},{3,1},{4,6},{5,7},{6,4},{7,5},{8,10},{9,11},{10,... | collective-permute-start | bytes 589832 | tf_op jit(solution)/shard_map/ppermute | solution.py:26
  31.3 6.4 %collective-permute-done.8.refs_1_.refs_0_ = bf16[256,640]{1,0:T(8,128)(2,1)S(1)} collective-permute-done((bf16[256,640]{1,0:T(8,128)(2,1)S(1)}, bf16[256,640]{1,0:T(8,128)(2,1)S(1)}, u32[]{:S(2)}, u32[]{:S(2)}) %collective-permute-start.8) | collective-permute-done | bytes 327712 | tf_op jit(solution)/shard_map/ppermute | solution.py:26
  37.7 0.3 term.14.high_ref
  38.0 0.3 term.13.low_ref
  38.2 0.8 %finish.2.refs_1_ = bf16[256,1024]{1,0:T(8,128)(2,1)} custom-call(f32[256,512]{1,0:T(8,128)S(1)} %term.13.low_ref, f32[256,512]{1,0:T(8,128)S(1)} %term.14.high_ref, bf16[256,640]{1,0:T(8,128)(2,1)S(1)} %collective-permute-done.8.refs_1_.refs_0_), custom_call_target="tpu_custom_call" | custom-call | flops 1000000 | bytes 2500 | tf_op jit(solution)/shard_map/finish/pallas_call | solution.py:423
  39.0 2.1 %collective-permute-done.11.refs_0_ = bf16[256,384]{1,0:T(8,128)(2,1)S(1)} collective-permute-done((bf16[256,384]{1,0:T(8,128)(2,1)S(1)}, bf16[256,384]{1,0:T(8,128)(2,1)S(1)}, u32[]{:S(2)}, u32[]{:S(2)}) %collective-permute-start.11) | collective-permute-done | bytes 196640 | tf_op jit(solution)/shard_map/ppermute | solution.py:26
  41.1 0.7 %finish.3 = bf16[256,1024]{1,0:T(8,128)(2,1)} custom-call(f32[256,512]{1,0:T(8,128)S(1)} %term.13.low_ref, f32[256,512]{1,0:T(8,128)S(1)} %term.14.high_ref, bf16[256,384]{1,0:T(8,128)(2,1)S(1)} %collective-permute-done.11.refs_0_, bf16[256,1024]{1,0:T(8,128)(2,1)} %finish.2.refs_1_), custom_call_target="tpu_custom_call", output_to_operand_aliasing={{}: (3, {})} | custom-call | flops 1000000 | bytes 2500 | tf_op jit(solution)/shard_map/finish/pallas_call | solution.py:423
  (14 shorter events, 0.2 us)
Async XLA Ops:
  0.0 21.4 %copy-start = (bf16[4096,512]{1,0:T(8,128)(2,1)S(1)}, bf16[4096,512]{1,0:T(8,128)(2,1)}, u32[]{:S(2)}) copy-start(bf16[4096,512]{1,0:T(8,128)(2,1)} %wq_ref.1) | copy-start | bytes 12582916
  1.4 8.6 %collective-permute-start = (bf16[512,128]{1,0:T(8,128)(2,1)S(1)}, bf16[512,128]{1,0:T(8,128)(2,1)S(1)}, u32[]{:S(2)}, u32[]{:S(2)}) collective-permute-start(bf16[512,128]{1,0:T(8,128)(2,1)S(1)} %get-tuple-element.26.key_value_ref), channel_id=1, source_target_pairs={{0,8},{4,12},{8,16},{12,20},{16,24},{20,28},{24,0},{28,4},{1,9},{5... | collective-permute-start | bytes 393224 | tf_op jit(solution)/shard_map/ppermute | solution.py:26
  4.5 10.4 %collective-permute-start.2 = (bf16[512,128]{1,0:T(8,128)(2,1)S(1)}, bf16[512,128]{1,0:T(8,128)(2,1)S(1)}, u32[]{:S(2)}, u32[]{:S(2)}) collective-permute-start(bf16[512,128]{1,0:T(8,128)(2,1)S(1)} %get-tuple-element.26.key_value_ref), channel_id=1, source_target_pairs={{0,4},{4,16},{8,12},{12,24},{16,20},{24,28},{1,5},{5,17},{9,13},{1... | collective-permute-start | bytes 393224 | tf_op jit(solution)/shard_map/ppermute | solution.py:310
  10.0 7.6 %collective-permute-start.4 = (bf16[512,128]{1,0:T(8,128)(2,1)S(1)}, bf16[512,128]{1,0:T(8,128)(2,1)S(1)}, u32[]{:S(2)}, u32[]{:S(2)}) collective-permute-start(bf16[512,128]{1,0:T(8,128)(2,1)S(1)} %collective-permute-done.key_value_ref), channel_id=1, source_target_pairs={{0,4},{4,0},{8,12},{12,8},{16,20},{20,16},{24,28},{28,24},{1,5},{5... | collective-permute-start | bytes 393224 | tf_op jit(solution)/shard_map/ppermute | solution.py:26
  13.5 9.5 %collective-permute-start.1 = (bf16[512,128]{1,0:T(8,128)(2,1)S(1)}, bf16[512,128]{1,0:T(8,128)(2,1)S(1)}, u32[]{:S(2)}, u32[]{:S(2)}) collective-permute-start(bf16[512,128]{1,0:T(8,128)(2,1)S(1)} %get-tuple-element.37), channel_id=1, source_target_pairs={{0,24},{4,28},{8,0},{12,4},{16,8},{20,12},{24,16},{28,20},{1,25},{... | collective-permute-start | bytes 393224 | tf_op jit(solution)/shard_map/ppermute | solution.py:26
  16.3 6.8 %collective-permute-start.3 = (bf16[512,128]{1,0:T(8,128)(2,1)S(1)}, bf16[512,128]{1,0:T(8,128)(2,1)S(1)}, u32[]{:S(2)}, u32[]{:S(2)}) collective-permute-start(bf16[512,128]{1,0:T(8,128)(2,1)S(1)} %get-tuple-element.39), channel_id=1, source_target_pairs={{0,20},{4,0},{8,28},{12,8},{16,4},{20,16},{24,12},{28,24},{1,21},{... | collective-permute-start | bytes 393224 | tf_op jit(solution)/shard_map/ppermute | solution.py:26
  19.0 5.9 %collective-permute-start.5 = (bf16[512,128]{1,0:T(8,128)(2,1)S(1)}, bf16[512,128]{1,0:T(8,128)(2,1)S(1)}, u32[]{:S(2)}, u32[]{:S(2)}) collective-permute-start(bf16[512,128]{1,0:T(8,128)(2,1)S(1)} %get-tuple-element.41), channel_id=1, source_target_pairs={{0,24},{4,28},{8,4},{12,0},{16,12},{20,8},{24,20},{28,16},{1,25},{... | collective-permute-start | bytes 393224 | tf_op jit(solution)/shard_map/ppermute | solution.py:26
  25.3 1.7 %collective-permute-start.7 = (bf16[256,640]{1,0:T(8,128)(2,1)S(1)}, bf16[256,640]{1,0:T(8,128)(2,1)S(1)}, u32[]{:S(2)}, u32[]{:S(2)}) collective-permute-start(bf16[256,640]{1,0:T(8,128)(2,1)S(1)} %term.8.refs_0_), channel_id=1, source_target_pairs={{0,1},{1,0},{2,3},{3,2},{4,5},{5,4},{6,7},{7,6},{8,9},{9,8},{10,11... | collective-permute-start | bytes 983048 | tf_op jit(solution)/shard_map/ppermute | solution.py:26
  27.1 10.6 %collective-permute-start.8 = (bf16[256,640]{1,0:T(8,128)(2,1)S(1)}, bf16[256,640]{1,0:T(8,128)(2,1)S(1)}, u32[]{:S(2)}, u32[]{:S(2)}) collective-permute-start(bf16[256,640]{1,0:T(8,128)(2,1)S(1)} %sum.1.refs_1_), channel_id=1, source_target_pairs={{0,2},{1,3},{2,0},{3,1},{4,6},{5,7},{6,4},{7,5},{8,10},{9,11},{10,... | collective-permute-start | bytes 983048 | tf_op jit(solution)/shard_map/ppermute | solution.py:26
  28.7 2.6 %collective-permute-start.9 = (bf16[256,512]{1,0:T(8,128)(2,1)S(1)}, bf16[256,512]{1,0:T(8,128)(2,1)S(1)}, u32[]{:S(2)}, u32[]{:S(2)}) collective-permute-start(bf16[256,512]{1,0:T(8,128)(2,1)S(1)} %term.11.refs_0_), channel_id=1, source_target_pairs={{0,1},{1,0},{2,3},{3,2},{4,5},{5,4},{6,7},{7,6},{8,9},{9,8},{10,11... | collective-permute-start | bytes 786440 | tf_op jit(solution)/shard_map/ppermute | solution.py:26
  28.7 1.8 %collective-permute-start.10 = (bf16[256,384]{1,0:T(8,128)(2,1)S(1)}, bf16[256,384]{1,0:T(8,128)(2,1)S(1)}, u32[]{:S(2)}, u32[]{:S(2)}) collective-permute-start(bf16[256,384]{1,0:T(8,128)(2,1)S(1)} %term.9.refs_0_), channel_id=1, source_target_pairs={{0,1},{1,0},{2,3},{3,2},{4,5},{5,4},{6,7},{7,6},{8,9},{9,8},{10,11... | collective-permute-start | bytes 589832 | tf_op jit(solution)/shard_map/ppermute | solution.py:26
  29.2 8.8 %collective-permute-start.6 = (bf16[256,512]{1,0:T(8,128)(2,1)S(1)}, bf16[256,512]{1,0:T(8,128)(2,1)S(1)}, u32[]{:S(2)}, u32[]{:S(2)}) collective-permute-start(bf16[256,512]{1,0:T(8,128)(2,1)S(1)} %term.10.refs_0_), channel_id=1, source_target_pairs={{0,1},{1,0},{2,3},{3,2},{4,5},{5,4},{6,7},{7,6},{8,9},{9,8},{10,11... | collective-permute-start | bytes 786440 | tf_op jit(solution)/shard_map/ppermute | solution.py:26
  30.7 10.4 %collective-permute-start.11 = (bf16[256,384]{1,0:T(8,128)(2,1)S(1)}, bf16[256,384]{1,0:T(8,128)(2,1)S(1)}, u32[]{:S(2)}, u32[]{:S(2)}) collective-permute-start(bf16[256,384]{1,0:T(8,128)(2,1)S(1)} %term.15), channel_id=1, source_target_pairs={{0,2},{1,3},{2,0},{3,1},{4,6},{5,7},{6,4},{7,5},{8,10},{9,11},{10,... | collective-permute-start | bytes 589832 | tf_op jit(solution)/shard_map/ppermute | solution.py:26
